TPU v7x, 32 devices: a whole 2x2x4 slice. The times are simulated.
32 devices in a mesh: range: 2 (over x), ping: 16 (over z, y, core).
Axes of the slice: x: 2, y: 2, z: 4, core: 2. Of those that a mesh axis runs over, the one named last changes fastest.
Arguments:
- echoes: bfloat16 [128, 32, 256], P('ping', None, 'range'), may hold values from -6 to 6
- band_offset: int32 [128], P('ping'), may hold values from -128 to 64
- sway_delay: float32 [128, 32], P('ping'), may hold values from 0 to 1
- channel_gain: float32 [128, 32], P('ping'), may hold values from 0.5 to 2
- track_bin: int32 [128], P('ping'), may hold values from 0 to 2047
Outputs:
- image_real: float32 [2048, 256], P('ping', 'range')
- image_imag: float32 [2048, 256], P('ping', 'range')
All inputs are finite; a program needn't handle non-finite values.
Results may differ from a plain program's by a relative error of at most 0.017.
Values may be sent and summed in bfloat16 or wider, within the bound.
No kernel may reach another device: no remote copies, remote signals or barrier semaphores. Data moves between devices by JAX's collectives and lax.ppermute only.
A program may use at most 64 MiB of HBM per device.

v0:
```python
import math

import jax
import jax.numpy as jnp
from jax import lax
from jax.sharding import PartitionSpec as P

X = 2048
BAND = 64
HALO = 128


def extended(block, sides, width):
    for axis, dim in sides:
        count = lax.axis_size(axis)
        forward = [(i, i + 1) for i in range(count - 1)]
        backward = [(target, source) for source, target in forward]
        low = lax.ppermute(
            lax.slice_in_dim(block, block.shape[dim] - width, None, axis=dim), axis, forward
        )
        high = lax.ppermute(lax.slice_in_dim(block, 0, width, axis=dim), axis, backward)
        block = jnp.concatenate([low, block, high], axis=dim)
    return block


def make_taps(sway_delay, channel_gain):
    kpos = jnp.arange(BAND, dtype=jnp.float32)
    shift = kpos - (BAND / 2 - 1) - sway_delay[..., None]
    window = 0.5 - 0.5 * jnp.cos(2.0 * math.pi * (kpos + 0.5) / BAND)
    return jnp.sinc(shift) * window * channel_gain[..., None]


def compensate(padded, offsets, taps, samples):
    padded = padded.astype(jnp.float32)
    ping_count, channels, _ = padded.shape

    def pick(row, shift):
        return lax.dynamic_slice_in_dim(row, shift + HALO, samples + BAND - 1, 1)

    windows = jax.vmap(pick)(padded, offsets)
    lhs = windows.reshape(1, ping_count * channels, samples + BAND - 1)
    rhs = taps.reshape(ping_count * channels, 1, BAND).astype(jnp.float32)
    result = lax.conv_general_dilated(
        lhs,
        rhs,
        (1,),
        "VALID",
        dimension_numbers=("NCH", "OIH", "NCH"),
        feature_group_count=ping_count * channels,
        precision=lax.Precision.HIGHEST,
    )
    return result.reshape(ping_count, channels, samples).astype(jnp.bfloat16)


def make_steer(first_row, row_count, track, channels, scaling, spread):
    xpos = jnp.asarray(first_row).astype(jnp.float32) + jnp.arange(row_count, dtype=jnp.float32)
    centre = (
        track.astype(jnp.float32)[:, None] + 0.5 * jnp.arange(channels, dtype=jnp.float32)[None, :]
    )
    centre = centre.reshape(-1)
    diff = xpos[:, None] - centre[None, :]
    dist = diff * (8.0 / X)
    weight = jnp.exp(-0.5 * dist * dist) * scaling
    phase = diff * diff * (math.pi / spread)
    return (
        (weight * jnp.cos(phase)).astype(jnp.bfloat16),
        (weight * jnp.sin(phase)).astype(jnp.bfloat16),
    )


def image_rows(first_row, row_count, track, columns, channels, scaling, spread):
    block_rows = math.gcd(row_count, 256)
    block_count = row_count // block_rows

    def one_block(block_index):
        steer_real, steer_imag = make_steer(
            first_row + block_index * block_rows, block_rows, track, channels, scaling, spread
        )
        part_real = jnp.dot(steer_real, columns, preferred_element_type=jnp.float32)
        part_imag = jnp.dot(steer_imag, columns, preferred_element_type=jnp.float32)
        return jnp.concatenate([part_real, part_imag], axis=1)

    blocks = lax.map(one_block, jnp.arange(block_count, dtype=jnp.int32))
    return blocks.reshape(row_count, 2 * columns.shape[1])


def shards(echoes, band_offset, sway_delay, channel_gain, track_bin):
    ping_count, channels, samples = echoes.shape
    taps = make_taps(sway_delay, channel_gain)
    padded = extended(echoes, (("range", 2),), HALO)
    compensated = compensate(padded, band_offset, taps, samples)
    columns = compensated.reshape(ping_count * channels, samples)
    scaling = 1.0 / math.sqrt(lax.axis_size("ping") * ping_count * channels)
    band_share = samples / (samples * lax.axis_size("range"))
    spread = 0.5 * X * (1.0 + (lax.axis_index("range").astype(jnp.float32) + 0.5) * band_share)
    whole = image_rows(0, X, track_bin, columns, channels, scaling, spread)
    image = lax.psum_scatter(
        whole.astype(jnp.bfloat16), "ping", scatter_dimension=0, tiled=True
    ).astype(jnp.float32)
    return (image[:, :samples], image[:, samples:])


def solution(mesh):
    return jax.shard_map(
        shards,
        mesh=mesh,
        in_specs=(P("ping", None, "range"), P("ping"), P("ping", None), P("ping", None), P("ping")),
        out_specs=(P("ping", "range"), P("ping", "range")),
        check_vma=False,
    )
```

profile of v0, /device:TPU:0, one launch (start us, length us, event | category | flops | bytes accessed | tf_op | source)
XLA Modules:
  0.0 119.1 jit_solution(3027712717810031516)
XLA Ops:
  7.2 0.0 copy-start
  7.2 0.0 reduce-scatter.2.cloned.1.call-start
  7.2 4.8 %collective-permute-start = (bf16[8,32,128]{2,1,0:T(8,128)(2,1)}, bf16[8,32,128]{2,1,0:T(8,128)(2,1)S(1)}, u32[]{:S(2)}, u32[]{:S(2)}) collective-permute-start(bf16[8,32,128]{2,1,0:T(8,128)(2,1)} %param.7), channel_id=1, source_target_pairs={{0,16},{1,17},{2,18},{3,19},{4,20},{5,21},{6,22},{7,23},{8,24},{9,... | collective-permute-start | bytes 196616 | tf_op jit(solution)/shard_map/ppermute | solution.py:18
  12.1 1.3 %collective-permute-start.1 = (bf16[8,32,128]{2,1,0:T(8,128)(2,1)}, bf16[8,32,128]{2,1,0:T(8,128)(2,1)S(1)}, u32[]{:S(2)}, u32[]{:S(2)}) collective-permute-start(bf16[8,32,128]{2,1,0:T(8,128)(2,1)} %param.7), channel_id=1, source_target_pairs={{16,0},{17,1},{18,2},{19,3},{20,4},{21,5},{22,6},{23,7},{24,8},{25... | collective-permute-start | bytes 196616 | tf_op jit(solution)/shard_map/ppermute | solution.py:21
  13.4 0.8 mul.258
  14.2 0.8 sub.81
  15.0 0.7 fusion.60
  15.6 0.0 copy-start.1
  15.6 0.2 fusion.39
  15.8 0.5 copy-done.1
  16.3 0.0 collective-permute-done
  16.3 2.1 %collective-permute-done.1 = bf16[8,32,128]{2,1,0:T(8,128)(2,1)S(1)} collective-permute-done((bf16[8,32,128]{2,1,0:T(8,128)(2,1)}, bf16[8,32,128]{2,1,0:T(8,128)(2,1)S(1)}, u32[]{:S(2)}, u32[]{:S(2)}) %collective-permute-start.1) | collective-permute-done | bytes 65568 | tf_op jit(solution)/shard_map/ppermute | solution.py:21
  18.4 0.0 copy-done
  18.5 0.5 copy.25
  19.0 1.7 %gather_fusion = bf16[8,32,191]{1,0,2:T(8,128)(2,1)S(1)} fusion(bf16[8,32,384]{1,0,2:T(8,128)(2,1)S(1)} %copy.25, s32[8]{0:T(128)S(1)} %fusion.60), kind=kCustom, calls=%fused_computation | custom fusion | bytes 195680 | tf_op jit(solution)/shard_map/vmap()/gather | solution.py:38
  20.7 0.3 copy.26
  21.0 0.2 copy.27
  21.2 1.0 convolution_convert_fusion
  22.1 0.1 copy.29
  22.3 29.3 %while.12 = (s32[]{:T(128)}, bf16[8,256,256]{1,2,0:T(8,128)(2,1)S(1)}, s32[8]{0:T(128)S(1)}, f32[8,1]{0,1:T(1,128)S(1)}, f32[]{:T(128)}, /*index=5*/bf16[256,128]{1,0:T(8,128)(2,1)S(1)}, s32[]{:T(128)}, s32[1]{0:T(128)}) while((s32[]{:T(128)}, bf16[8,256,256]{1,2,0:T(8,128)(2,1)S(1)}, s32[8]{0:T(128)S(1)}, f32[8,1]{0,1:T(1,128)S(1)}, ...), condition=%wide.region_1.2_spmd, body=%wide.region_0.1_spmd.sunk | while | flops 34996772 | bytes 532901 | solution.py:83
  22.3 0.6 dynamic_slice.8
  23.5 0.1 broadcast_add_fusion.2
  23.5 0.1 add.305
  23.6 1.2 fusion.76
  24.8 1.1 fusion.77
  26.0 0.6 dynamic_slice.8
  27.1 0.1 broadcast_add_fusion.2
  27.2 0.1 add.305
  27.3 1.2 fusion.76
  28.4 1.1 fusion.77
  29.6 0.6 dynamic_slice.8
  30.8 0.1 broadcast_add_fusion.2
  30.9 0.1 add.305
  31.0 1.2 fusion.76
  32.1 1.1 fusion.77
  33.3 0.6 dynamic_slice.8
  34.5 0.1 broadcast_add_fusion.2
  34.5 0.1 add.305
  34.6 1.2 fusion.76
  35.8 1.1 fusion.77
  37.0 0.6 dynamic_slice.8
  38.1 0.1 broadcast_add_fusion.2
  38.2 0.1 add.305
  38.3 1.2 fusion.76
  39.4 1.1 fusion.77
  40.6 0.6 dynamic_slice.8
  41.8 0.1 broadcast_add_fusion.2
  41.9 0.1 add.305
  42.0 1.2 fusion.76
  43.1 1.1 fusion.77
  44.3 0.6 dynamic_slice.8
  45.5 0.1 broadcast_add_fusion.2
  45.5 0.1 add.305
  45.6 1.2 fusion.76
  46.8 1.1 fusion.77
  48.0 0.6 dynamic_slice.8
  49.1 0.1 broadcast_add_fusion.2
  49.2 0.1 add.305
  49.3 1.2 fusion.76
  50.4 1.1 fusion.77
  51.6 1.3 %copy.30 = bf16[8,256,256]{2,1,0:T(8,128)(2,1)} copy(bf16[8,256,256]{1,2,0:T(8,128)(2,1)S(1)} %get-tuple-element.83) | data formatting | bytes 2097152 | tf_op jit(solution)/shard_map/convert_element_type | solution.py:98
  52.9 0.0 reduce-scatter.2.cloned.1.call-update
  53.0 57.9 %reduce-scatter.2.cloned.1.call-done = bf16[128,256]{1,0:T(8,128)(2,1)} async-done(((bf16[2048,256]{1,0:T(8,128)(2,1)}), bf16[128,256]{1,0:T(8,128)(2,1)}) %reduce-scatter.2.cloned.1.call-update) | async-done | bytes 65552 | tf_op jit(solution)/shard_map/reduce_scatter | solution.py:97
  110.9 1.4 %fusion.61 = (f32[128,128]{1,0:T(8,128)}, f32[128,128]{1,0:T(8,128)}) fusion(bf16[128,256]{1,0:T(8,128)(2,1)} %reduce-scatter.2.cloned.1.call-done), kind=kLoop, calls=%fused_computation.81 | loop fusion | bytes 262144 | tf_op jit(solution)/shard_map/slice | solution.py:100
  (29 shorter events, 0.4 us)
Async XLA Ops:
  7.2 11.3 %copy-start = (bf16[8,32,128]{2,1,0:T(8,128)(2,1)S(1)}, bf16[8,32,128]{2,1,0:T(8,128)(2,1)}, u32[]{:S(2)}) copy-start(bf16[8,32,128]{2,1,0:T(8,128)(2,1)} %param.7) | copy-start | bytes 196612
  7.2 103.7 %reduce-scatter.2.cloned.1.call-start = ((), (), s32[]{:S(2)}) async-start(), calls=%async_computation.1 | async-start | bytes 1114112 | tf_op jit(solution)/shard_map/reduce_scatter | solution.py:97
  7.2 9.1 %collective-permute-start = (bf16[8,32,128]{2,1,0:T(8,128)(2,1)}, bf16[8,32,128]{2,1,0:T(8,128)(2,1)S(1)}, u32[]{:S(2)}, u32[]{:S(2)}) collective-permute-start(bf16[8,32,128]{2,1,0:T(8,128)(2,1)} %param.7), channel_id=1, source_target_pairs={{0,16},{1,17},{2,18},{3,19},{4,20},{5,21},{6,22},{7,23},{8,24},{9,... | collective-permute-start | bytes 196616 | tf_op jit(solution)/shard_map/ppermute | solution.py:18
  12.1 6.4 %collective-permute-start.1 = (bf16[8,32,128]{2,1,0:T(8,128)(2,1)}, bf16[8,32,128]{2,1,0:T(8,128)(2,1)S(1)}, u32[]{:S(2)}, u32[]{:S(2)}) collective-permute-start(bf16[8,32,128]{2,1,0:T(8,128)(2,1)} %param.7), channel_id=1, source_target_pairs={{16,0},{17,1},{18,2},{19,3},{20,4},{21,5},{22,6},{23,7},{24,8},{25... | collective-permute-start | bytes 196616 | tf_op jit(solution)/shard_map/ppermute | solution.py:21
  15.6 0.7 copy-start.1
Sparse Core Ops, SparseCore 0:
  53.1 57.7 reduce-scatter.1
where the time goes:
time: 120 us; the launch traced here: 119 us
  waiting for transfers between devices  60 us (50%)
  matrix products  19.4 us (16%)
  between operations  14.2 us (12%)
  local copies, waits for them, and re-layouts  12.8 us (11%)
  starting transfers between devices  6.17 us (5%)
  loops' own time  4.8 us (4%)
  other arithmetic  1.74 us (1%)
    reduce_scatter x1, waiting for transfers between devices, shards(): lax.psum_scatter(whole.astype(jnp.bfloat16), 'ping', scatter_dimension=0,...  57.9 us
    dot_general x8, matrix products, one_block(): part_imag = jnp.dot(steer_imag, columns, preferred_element_type=jnp.float32)  9.21 us
    dot_general x8, matrix products, one_block(): part_real = jnp.dot(steer_real, columns, preferred_element_type=jnp.float32)  9.19 us
    ppermute x1, starting transfers between devices, extended(): lax.ppermute(lax.slice_in_dim(block, block.shape[dim] - width, None, axis...  4.85 us
    another operation x1, loops' own time, image_rows(): blocks = lax.map(one_block, jnp.arange(block_count, dtype=jnp.int32))  4.8 us
    dynamic_slice x8, local copies, waits for them, and re-layouts, image_rows(): blocks = lax.map(one_block, jnp.arange(block_count, dtype=jnp.int32))  4.64 us
  transfers between devices with their start and end apart: 3, of which 2 were waited for; matrix products, arithmetic and copies ran while one was open for 2% of the time, Pallas kernels for 0%

commit v1 on v0

v1 whole, which is shorter than its diff:
```python
import functools
import math

import jax
import jax.numpy as jnp
from jax import lax
from jax.experimental import pallas as pl
from jax.experimental.pallas import tpu as pltpu
from jax.sharding import PartitionSpec as P

X = 2048
BAND = 64
HALO = 128
LANES = 128
SUB = 8
VMEM_LIMIT = 48 * 1024 * 1024


def round_up(value, unit):
    return -(-value // unit) * unit


def lane_row(values, lanes):
    pings, channels = values.shape
    spread = jnp.concatenate([values] * pings, axis=1)
    owner = lax.broadcasted_iota(jnp.int32, (pings, lanes), 1) // channels
    row = lax.broadcasted_iota(jnp.int32, (pings, lanes), 0)
    return jnp.sum(jnp.where(owner == row, spread, 0.0), axis=0, keepdims=True)


def fir_kernel(
    bands,
    front,
    offset_ref,
    echo_ref,
    sway_ref,
    gain_ref,
    out_ref,
    tap_ref,
    copies_ref,
    placed_ref,
):
    pings, channels = sway_ref.shape
    lanes, samples = echo_ref.shape
    rows = out_ref.shape[0] * out_ref.shape[1]
    if bands == 1:
        base = 0
    elif bands == 2:
        base = -samples * lax.axis_index("range")
    else:
        base = -samples

    sway = lane_row(sway_ref[...], lanes)
    gain = lane_row(gain_ref[...], lanes)
    amplitude = jnp.sin(math.pi * jnp.minimum(sway, 1.0 - sway)) * gain * (1.0 / math.pi)
    tap_index = lax.broadcasted_iota(jnp.int32, (BAND, lanes), 0)
    kpos = tap_index.astype(jnp.float32)
    shift = kpos - (BAND / 2 - 1) - sway
    window = 0.5 - 0.5 * jnp.cos(2.0 * math.pi * (kpos + 0.5) / BAND)
    sign = jnp.where(tap_index % 2 == 0, 1.0, -1.0)
    whole = shift == 0.0
    sinc_gain = jnp.where(whole, gain, sign * amplitude / jnp.where(whole, 1.0, shift))
    tap_ref[...] = sinc_gain * window

    echo = jnp.transpose(echo_ref[...].astype(jnp.float32))
    edge = jnp.zeros((SUB, lanes), jnp.float32)
    for s in range(SUB):
        copies_ref[s, 0:SUB, :] = edge
        copies_ref[s, samples : samples + SUB, :] = edge
        copies_ref[s, SUB - s : SUB - s + samples, :] = echo

    ext = round_up(samples + BAND - 1, SUB)
    tail = placed_ref.shape[1] - front - ext
    for tile in range(lanes // LANES):
        placed_ref[tile, :front, :] = jnp.zeros((front, LANES), jnp.float32)
        placed_ref[tile, front + ext :, :] = jnp.zeros((tail, LANES), jnp.float32)
    group = 8
    blocks = ext // SUB
    for tile in range(lanes // LANES):
        cols = slice(tile * LANES, (tile + 1) * LANES)
        for first in range(0, blocks, group):
            members = range(first, min(first + group, blocks))
            total = {j: None for j in members}
            for k in range(BAND):
                used = [j for j in members if -SUB < j * SUB - (BAND - 1) + k < samples]
                if not used:
                    continue
                tap = jnp.broadcast_to(tap_ref[k : k + 1, cols], (SUB, LANES))
                for j in used:
                    row = j * SUB - (BAND - 1) + k + SUB
                    s = row % SUB
                    term = copies_ref[s, row - s : row - s + SUB, cols] * tap
                    total[j] = term if total[j] is None else total[j] + term
            for j in members:
                value = jnp.zeros((SUB, LANES), jnp.float32) if total[j] is None else total[j]
                placed_ref[tile, front + j * SUB : front + (j + 1) * SUB, :] = value

    lane = lax.broadcasted_iota(jnp.int32, (rows, LANES), 1)
    for tile in range(lanes // LANES):
        cols = slice(tile * LANES, (tile + 1) * LANES)
        value = None
        for ping in range(pings):
            low, high = ping * channels - tile * LANES, (ping + 1) * channels - tile * LANES
            if high <= 0 or low >= LANES:
                continue
            start = base + offset_ref[ping] + (front + BAND - 1)
            moved = placed_ref[tile, pl.ds(start, rows), :]
            value = moved if value is None else jnp.where(lane >= low, moved, value)
        out_ref[:, :, cols] = value.reshape(rows // SUB, SUB, LANES).astype(jnp.bfloat16)


def own_share(echoes, band_offset, sway_delay, channel_gain, bands):
    pings, channels, samples = echoes.shape
    lanes = pings * channels
    rows = samples * min(bands, 3)
    front = round_up(samples + HALO - BAND + 1, SUB)
    height = round_up(front + 2 * samples + HALO - 1, SUB)
    vmem = pl.BlockSpec(memory_space=pltpu.VMEM)
    return pl.pallas_call(
        functools.partial(fir_kernel, bands, front),
        out_shape=jax.ShapeDtypeStruct((rows // SUB, SUB, lanes), jnp.bfloat16),
        in_specs=[pl.BlockSpec(memory_space=pltpu.SMEM), vmem, vmem, vmem],
        out_specs=vmem,
        scratch_shapes=[
            pltpu.VMEM((BAND, lanes), jnp.float32),
            pltpu.VMEM((SUB, samples + SUB, lanes), jnp.float32),
            pltpu.VMEM((lanes // LANES, height, LANES), jnp.float32),
        ],
        compiler_params=pltpu.CompilerParams(vmem_limit_bytes=VMEM_LIMIT),
        name="fir",
    )(band_offset, echoes.reshape(lanes, samples), sway_delay, channel_gain)


def half_turn_sincos(turns):
    angle = (turns - jnp.round(turns)) * math.pi
    square = angle * angle
    sin_sum, cos_sum = jnp.zeros_like(angle), jnp.zeros_like(angle)
    for order in range(7, -1, -1):
        sin_sum = sin_sum * square + (-1.0) ** order / math.factorial(2 * order + 1)
        cos_sum = cos_sum * square + (-1.0) ** order / math.factorial(2 * order)
    sine = sin_sum * angle
    return 2.0 * sine * cos_sum, 1.0 - 2.0 * sine * sine


def steer_kernel(bands, scaling, out_ref):
    depth, width = out_ref.shape
    spans = width // (2 * LANES)
    band = lax.axis_index("range").astype(jnp.float32)
    spread = 0.5 * X * (1.0 + (band + 0.5) * (1.0 / bands))
    length = (spans + 1) * LANES
    lane = lax.broadcasted_iota(jnp.int32, (SUB, length), 1) - (spans // 2 + 1) * LANES
    row = lax.broadcasted_iota(jnp.int32, (SUB, length), 0)
    twice = (2 * lane - row).astype(jnp.float32)
    square = twice * twice
    weight = jnp.exp(square * (-0.125 * (8.0 / X) ** 2)) * scaling
    sine, cosine = half_turn_sincos(square * (0.125 / spread))
    parts = (weight * cosine, weight * sine)
    for first in range(0, depth, 2 * SUB):
        for part in range(2):
            moved = [
                pltpu.roll(parts[part], (first + more) // 2, 1) if first + more else parts[part]
                for more in (0, SUB)
            ]
            both = jnp.concatenate(moved, axis=0).astype(jnp.bfloat16)
            for span in range(spans):
                at = (2 * span + part) * LANES
                out_ref[first : first + 2 * SUB, at : at + LANES] = both[
                    :, (span + 1) * LANES : (span + 2) * LANES
                ]


def steer_table(bands, scaling):
    blocks = X // LANES
    return pl.pallas_call(
        functools.partial(steer_kernel, bands, scaling),
        out_shape=jax.ShapeDtypeStruct((2 * LANES, 2 * blocks * 2 * LANES), jnp.bfloat16),
        out_specs=pl.BlockSpec(memory_space=pltpu.VMEM),
        compiler_params=pltpu.CompilerParams(vmem_limit_bytes=VMEM_LIMIT),
        name="steer",
    )()


def image_kernel(copies, track_ref, share_ref, table_ref, out_ref, *scratch):
    groups = out_ref.shape[0]
    channels_all = share_ref.shape[2]
    sums, held_ref = scratch[:-1], scratch[-1]
    half = sums[0].shape[0] // 2
    pings = track_ref.shape[0] // groups
    channels = channels_all // pings
    for ref in sums:
        ref[...] = jnp.zeros(ref.shape, jnp.float32)
    lane = lax.broadcasted_iota(jnp.int32, (SUB, LANES), 1)
    for group in range(groups):
        share = share_ref[group].astype(jnp.float32)
        for copy in range(1, copies):
            share = share + share_ref[copy * groups + group].astype(jnp.float32)
        for ping in range(pings):
            tile, low = ping * channels // LANES, ping * channels % LANES
            at = 2 * track_ref[group * pings + ping]
            own = share[:, tile * LANES : (tile + 1) * LANES]
            own = jnp.where((lane >= low) & (lane < low + channels), own, 0.0)
            inside = at & (LANES - 1)
            moved = pltpu.roll(own, (at - low) & (LANES - 1), 1)
            ref = sums[ping % len(sums)]
            block = at // LANES
            slot = (block & 1) * half + (block >> 1)
            after = block + 1
            slot_after = (after & 1) * half + (after >> 1)
            ref[slot] = ref[slot] + jnp.where(lane >= inside, moved, 0.0)
            ref[slot_after] = ref[slot_after] + jnp.where(lane < inside, moved, 0.0)
    total = sums[0][...]
    for ref in sums[1:]:
        total = total + ref[...]
    total = total.reshape(2 * half * SUB, LANES).astype(jnp.bfloat16)
    held_ref[:, :LANES] = total[: half * SUB]
    held_ref[:, LANES:] = total[half * SUB :]

    blocks = X // LANES
    image = [None] * blocks
    for step in range(-blocks, blocks):
        first, last = max(0, -step), min(blocks, blocks - 1 - step)
        low = first - first % 2
        high = min(half, low + round_up(last + 1 - low, 2))
        at = (step + blocks) * 2 * LANES
        part = jnp.dot(
            held_ref[low * SUB : high * SUB, :],
            table_ref[:, at : at + 2 * LANES],
            preferred_element_type=jnp.float32,
        )
        for k in range(first, last + 1):
            term = part[(k - low) * SUB : (k - low + 1) * SUB]
            image[k + step] = term if image[k + step] is None else image[k + step] + term
    share_rows = blocks // groups
    for block in range(blocks):
        group, within = block // share_rows, block % share_rows
        out_ref[group, :, within * 2 * LANES : (within + 1) * 2 * LANES] = image[block].astype(
            jnp.bfloat16
        )


def image_share(track, share, table, groups):
    copies = share.shape[0] // groups
    lanes = share.shape[2]
    blocks = X // LANES
    half = round_up(blocks + 1, 2)
    vmem = pl.BlockSpec(memory_space=pltpu.VMEM)
    return pl.pallas_call(
        functools.partial(image_kernel, copies),
        out_shape=jax.ShapeDtypeStruct((groups, SUB, blocks // groups * 2 * LANES), jnp.bfloat16),
        in_specs=[pl.BlockSpec(memory_space=pltpu.SMEM), vmem, vmem],
        out_specs=vmem,
        scratch_shapes=[pltpu.VMEM((2 * half, SUB, LANES), jnp.float32)] * 4
        + [pltpu.VMEM((half * SUB, 2 * LANES), jnp.bfloat16)],
        compiler_params=pltpu.CompilerParams(vmem_limit_bytes=VMEM_LIMIT),
        name="image",
    )(track, share, table)


def turn_kernel(in_ref, real_ref, imag_ref):
    groups, sub, width = in_ref.shape
    whole = in_ref[...].astype(jnp.float32).reshape(groups * sub, width)
    for block in range(width // (2 * LANES)):
        rows = slice(block * LANES, (block + 1) * LANES)
        at = block * 2 * LANES
        real_ref[rows, :] = jnp.transpose(whole[:, at : at + LANES])
        imag_ref[rows, :] = jnp.transpose(whole[:, at + LANES : at + 2 * LANES])


def turned(image, rows, samples):
    vmem = pl.BlockSpec(memory_space=pltpu.VMEM)
    out = jax.ShapeDtypeStruct((rows, samples), jnp.float32)
    return pl.pallas_call(
        turn_kernel,
        out_shape=(out, out),
        in_specs=[vmem],
        out_specs=(vmem, vmem),
        compiler_params=pltpu.CompilerParams(vmem_limit_bytes=VMEM_LIMIT),
        name="turn",
    )(image)


def shards(echoes, band_offset, sway_delay, channel_gain, track_bin):
    pings, channels, samples = echoes.shape
    bands, groups = lax.axis_size("range"), lax.axis_size("ping")
    scaling = 1.0 / math.sqrt(groups * pings * channels)
    track = lax.all_gather(track_bin, "ping", tiled=True)
    share = own_share(echoes, band_offset, sway_delay, channel_gain, bands)
    if bands <= 2:
        share = lax.all_to_all(share, ("range", "ping"), 0, 0, tiled=True)
    else:
        low, own, high = jnp.split(share, 3)
        up = [(i, i + 1) for i in range(bands - 1)]
        down = [(target, source) for source, target in up]
        from_low = lax.ppermute(high, "range", up)
        from_high = lax.ppermute(low, "range", down)
        share = jnp.concatenate(
            [lax.all_to_all(a, "ping", 0, 0, tiled=True) for a in (own, from_low, from_high)]
        )
    table = steer_table(bands, scaling)
    image = image_share(track, share, table, groups)
    image = lax.all_to_all(image, "ping", 0, 0, tiled=True)
    return turned(image, X // groups, samples)


def solution(mesh):
    return jax.shard_map(
        shards,
        mesh=mesh,
        in_specs=(P("ping", None, "range"), P("ping"), P("ping", None), P("ping", None), P("ping")),
        out_specs=(P("ping", "range"), P("ping", "range")),
        check_vma=False,
    )
```

time: 120 us -> 45.7 us (0.38)
  waiting for transfers between devices: 60 us -> 0.01 us
  blocking collectives: 0 us -> 21.7 us
  matrix products: 19.4 us -> 0 us
  between operations: 14.2 us -> 1.36 us
  Pallas kernels: 0 us -> 7.1 us
  local copies, waits for them, and re-layouts: 12.8 us -> 7.83 us
  loops' own time: 4.8 us -> 0 us
  other arithmetic: 1.74 us -> 0 us
    reduce_scatter x1 -> x0, waiting for transfers between devices: 57.9 us -> none  [shards(): lax.psum_scatter(whole.astype(jnp.bfloat16), 'ping', scatter_dimension=0,...]
    dot_general x16 -> x0, matrix products: 18.4 us -> none  [the longest x8 9.21 us: one_block(): part_imag = jnp.dot(steer_imag, columns, preferred_element_type=jnp.float32)]
    unnamed x0 -> x1, blocking collectives: none -> 12.3 us
    all_to_all x0 -> x1, blocking collectives: none -> 9.47 us  [shards(): image = lax.all_to_all(image, 'ping', 0, 0, tiled=True)]
    unnamed x4 -> x19, local copies, waits for them, and re-layouts: 0.5 us -> 7.83 us
    all_to_all x0 -> x1, starting transfers between devices: none -> 7.3 us  [shards(): share = lax.all_to_all(share, ('range', 'ping'), 0, 0, tiled=True)]
    pallas_call x0 -> x4, Pallas kernels: none -> 7.1 us  [the longest x1 2.59 us: image_share(): pl.pallas_call(functools.partial(image_kernel, copies), out_shape=jax.Sha...]
    ppermute x2 -> x0, starting transfers between devices: 6.14 us -> none  [the longest x1 4.85 us: extended(): lax.ppermute(lax.slice_in_dim(block, block.shape[dim] - width, None, axis...]
  transfers between devices with their start and end apart: 3 -> 1, of which waited for: 2 -> 0; matrix products, arithmetic and copies ran while one was open for 2% -> 2% of each run, Pallas kernels for 0% -> 3%
where the time goes in v1:
time: 45.7 us; the launch traced here: 45.3 us
  blocking collectives  21.7 us (47%)
  local copies, waits for them, and re-layouts  7.83 us (17%)
  starting transfers between devices  7.3 us (16%)
  Pallas kernels  7.1 us (16%)
  between operations  1.36 us (3%)
    unnamed x1, blocking collectives  12.3 us
    all_to_all x1, blocking collectives, shards(): image = lax.all_to_all(image, 'ping', 0, 0, tiled=True)  9.47 us
    unnamed x19, local copies, waits for them, and re-layouts  7.83 us
    all_to_all x1, starting transfers between devices, shards(): share = lax.all_to_all(share, ('range', 'ping'), 0, 0, tiled=True)  7.3 us
    pallas_call x1, Pallas kernels, image_share(): pl.pallas_call(functools.partial(image_kernel, copies), out_shape=jax.Sha...  2.59 us
    pallas_call x1, Pallas kernels, own_share(): pl.pallas_call(functools.partial(fir_kernel, bands, front), out_shape=jax...  2.35 us
    pallas_call x1, Pallas kernels, steer_table(): pl.pallas_call(functools.partial(steer_kernel, bands, scaling), out_shape...  1.41 us
  transfers between devices with their start and end apart: 1, of which 0 were waited for; matrix products, arithmetic and copies ran while one was open for 2% of the time, Pallas kernels for 3%

profile of v1, /device:TPU:0, one launch (start us, length us, event | category | flops | bytes accessed | tf_op | source)
XLA Modules:
  0.0 45.3 jit_solution(4577264490547737805)
XLA Ops:
  0.6 0.0 copy-start.7
  0.6 0.0 copy-start.6
  0.7 0.0 copy-start.2
  0.7 0.8 %copy-done.2 = bf16[8,32,128]{2,1,0:T(8,128)(2,1)S(1)} copy-done((bf16[8,32,128]{2,1,0:T(8,128)(2,1)S(1)}, bf16[8,32,128]{2,1,0:T(8,128)(2,1)}, u32[]{:S(2)}) %copy-start.2) | copy-done | bytes 65560
  1.5 0.0 copy-start.3
  1.5 0.7 %copy-done.3 = f32[8,32]{1,0:T(8,128)S(1)} copy-done((f32[8,32]{1,0:T(8,128)S(1)}, f32[8,32]{1,0:T(8,128)}, u32[]{:S(2)}) %copy-start.3) | copy-done | bytes 1048
  2.2 0.0 copy-start.4
  2.2 0.7 %copy-done.4 = f32[8,32]{1,0:T(8,128)S(1)} copy-done((f32[8,32]{1,0:T(8,128)S(1)}, f32[8,32]{1,0:T(8,128)}, u32[]{:S(2)}) %copy-start.4) | copy-done | bytes 1048
  2.9 0.0 copy-start.5
  2.9 0.7 %copy-done.5 = s32[8]{0:T(128)S(1)} copy-done((s32[8]{0:T(128)S(1)}, s32[8]{0:T(128)}, u32[]{:S(2)}) %copy-start.5) | copy-done | bytes 56
  3.5 2.3 %fir.1 = bf16[32,8,256]{2,1,0:T(8,128)(2,1)} custom-call(s32[8]{0:T(128)S(1)} %copy-done.5, bf16[256,128]{1,0:T(8,128)(2,1)S(1)} %bitcast.2, f32[8,32]{1,0:T(8,128)S(1)} %copy-done.3, f32[8,32]{1,0:T(8,128)S(1)} %copy-done.4), custom_call_target="tpu_custom_call" | custom-call | tf_op jit(solution)/shard_map/fir/pallas_call | solution.py:119
  5.9 7.3 %all-to-all-start = ((bf16[32,8,256]{2,1,0:T(8,128)(2,1)}), bf16[32,8,256]{2,1,0:T(8,128)(2,1)S(1)}, u32[]{:S(2)}, u32[]{:S(2)}) async-start(bf16[32,8,256]{2,1,0:T(8,128)(2,1)} %fir.1), calls=%async_computation | async-start | bytes 262144 | tf_op jit(solution)/shard_map/all_to_all | solution.py:289
  13.2 1.4 %steer.1.table_ref = bf16[256,8192]{1,0:T(8,128)(2,1)S(1)} custom-call(), custom_call_target="tpu_custom_call" | custom-call | tf_op jit(solution)/shard_map/steer/pallas_call | solution.py:174
  14.6 0.0 copy-start
  14.6 1.9 %copy-done = bf16[256,8192]{1,0:T(8,128)(2,1)} copy-done((bf16[256,8192]{1,0:T(8,128)(2,1)}, bf16[256,8192]{1,0:T(8,128)(2,1)S(1)}, u32[]{:S(2)}) %copy-start) | copy-done | bytes 4194328
  16.6 0.0 copy-done.7
  16.6 0.6 %dynamic-slice = u32[1]{0:T(128)} dynamic-slice(u32[32]{0:T(128)S(1)} %copy-done.7, u32[]{:T(128)S(6)} %add), dynamic_slice_sizes={1} | dynamic-slice | bytes 12
  17.8 0.0 copy-done.6
  17.8 0.2 dynamic-update-slice
  18.0 12.3 %all-reduce.track_ref = s32[128]{0:T(128)S(1)} all-reduce(s32[128]{0:T(128)S(1)} %dynamic-update-slice), channel_id=1, replica_groups=mesh['range'=2,'ping'=16] {'ping'}, use_global_device_ids=true, to_apply=%add | all-reduce | flops 128 | bytes 1024
  30.3 0.0 all-to-all-done.share_ref
  30.3 0.0 copy-start.1
  30.3 2.2 %copy-done.1 = bf16[256,8192]{1,0:T(8,128)(2,1)S(1)} copy-done((bf16[256,8192]{1,0:T(8,128)(2,1)S(1)}, bf16[256,8192]{1,0:T(8,128)(2,1)}, u32[]{:S(2)}) %copy-start.1) | copy-done | bytes 4194328
  32.5 2.6 %image.1 = bf16[16,8,256]{2,1,0:T(8,128)(2,1)S(1)} custom-call(s32[128]{0:T(128)S(1)} %all-reduce.track_ref, bf16[32,8,256]{2,1,0:T(8,128)(2,1)S(1)} %all-to-all-done.share_ref, bf16[256,8192]{1,0:T(8,128)(2,1)S(1)} %copy-done.1), custom_call_target="tpu_custom_call" | custom-call | tf_op jit(solution)/shard_map/image/pallas_call | solution.py:247
  35.1 9.5 %all_to_all.10.in_ref = bf16[16,8,256]{2,1,0:T(8,128)(2,1)S(1)} all-to-all(bf16[16,8,256]{2,1,0:T(8,128)(2,1)S(1)} %image.1), channel_id=1, replica_groups=mesh['range'=2,'ping'=16] {'ping'}, dimensions={0} | all-to-all | bytes 131072 | tf_op jit(solution)/shard_map/all_to_all | solution.py:301
  44.6 0.8 %turn.1 = (f32[128,128]{1,0:T(8,128)}, f32[128,128]{1,0:T(8,128)}) custom-call(bf16[16,8,256]{2,1,0:T(8,128)(2,1)S(1)} %all_to_all.10.in_ref), custom_call_target="tpu_custom_call" | custom-call | tf_op jit(solution)/shard_map/turn/pallas_call | solution.py:272
  (1 shorter events, 0.0 us)
Async XLA Ops:
  0.6 15.9 %copy-start.7 = (u32[32]{0:T(128)S(1)}, u32[32]{0:T(128)}, u32[]{:S(2)}) copy-start(u32[32]{0:T(128)} %constant.7) | copy-start | bytes 388
  0.6 17.2 %copy-start.6 = (s32[8]{0:T(128)S(1)}, s32[8]{0:T(128)}, u32[]{:S(2)}) copy-start(s32[8]{0:T(128)} %param.9) | copy-start | bytes 100
  0.7 0.9 %copy-start.2 = (bf16[8,32,128]{2,1,0:T(8,128)(2,1)S(1)}, bf16[8,32,128]{2,1,0:T(8,128)(2,1)}, u32[]{:S(2)}) copy-start(bf16[8,32,128]{2,1,0:T(8,128)(2,1)} %param.5) | copy-start | bytes 196612
  1.5 0.7 %copy-start.3 = (f32[8,32]{1,0:T(8,128)S(1)}, f32[8,32]{1,0:T(8,128)}, u32[]{:S(2)}) copy-start(f32[8,32]{1,0:T(8,128)} %sway_ref.1) | copy-start | bytes 3076
  2.2 0.7 %copy-start.4 = (f32[8,32]{1,0:T(8,128)S(1)}, f32[8,32]{1,0:T(8,128)}, u32[]{:S(2)}) copy-start(f32[8,32]{1,0:T(8,128)} %gain_ref.1) | copy-start | bytes 3076
  2.9 0.7 %copy-start.5 = (s32[8]{0:T(128)S(1)}, s32[8]{0:T(128)}, u32[]{:S(2)}) copy-start(s32[8]{0:T(128)} %offset_ref.1) | copy-start | bytes 100
  5.9 24.4 %all-to-all-start = ((bf16[32,8,256]{2,1,0:T(8,128)(2,1)}), bf16[32,8,256]{2,1,0:T(8,128)(2,1)S(1)}, u32[]{:S(2)}, u32[]{:S(2)}) async-start(bf16[32,8,256]{2,1,0:T(8,128)(2,1)} %fir.1), calls=%async_computation | async-start | bytes 262144 | tf_op jit(solution)/shard_map/all_to_all | solution.py:289
  14.6 1.9 %copy-start = (bf16[256,8192]{1,0:T(8,128)(2,1)}, bf16[256,8192]{1,0:T(8,128)(2,1)S(1)}, u32[]{:S(2)}) copy-start(bf16[256,8192]{1,0:T(8,128)(2,1)S(1)} %steer.1.table_ref) | copy-start | bytes 12582916
  30.3 2.2 %copy-start.1 = (bf16[256,8192]{1,0:T(8,128)(2,1)S(1)}, bf16[256,8192]{1,0:T(8,128)(2,1)}, u32[]{:S(2)}) copy-start(bf16[256,8192]{1,0:T(8,128)(2,1)} %copy-done) | copy-start | bytes 12582916

commit v2 on v1

--- a/solution.py
+++ b/solution.py
@@ -13,7 +13,7 @@
 HALO = 128
 LANES = 128
 SUB = 8
-VMEM_LIMIT = 48 * 1024 * 1024
+MIB = 1024 * 1024
 
 
 def round_up(value, unit):
@@ -31,15 +31,32 @@
 def fir_kernel(
     bands,
     front,
+    offset_hbm,
+    track_hbm,
+    echo_hbm,
+    sway_hbm,
+    gain_hbm,
+    out_ref,
     offset_ref,
+    track_ref,
     echo_ref,
     sway_ref,
     gain_ref,
-    out_ref,
     tap_ref,
     copies_ref,
     placed_ref,
+    sems,
 ):
+    pairs = (
+        (echo_hbm, echo_ref),
+        (sway_hbm, sway_ref),
+        (gain_hbm, gain_ref),
+        (offset_hbm, offset_ref),
+        (track_hbm, track_ref),
+    )
+    fetches = [pltpu.make_async_copy(a, b, sems.at[i]) for i, (a, b) in enumerate(pairs)]
+    for fetch in fetches:
+        fetch.start()
     pings, channels = sway_ref.shape
     lanes, samples = echo_ref.shape
     rows = out_ref.shape[0] * out_ref.shape[1]
@@ -50,30 +67,37 @@
     else:
         base = -samples
 
-    sway = lane_row(sway_ref[...], lanes)
-    gain = lane_row(gain_ref[...], lanes)
-    amplitude = jnp.sin(math.pi * jnp.minimum(sway, 1.0 - sway)) * gain * (1.0 / math.pi)
-    tap_index = lax.broadcasted_iota(jnp.int32, (BAND, lanes), 0)
-    kpos = tap_index.astype(jnp.float32)
-    shift = kpos - (BAND / 2 - 1) - sway
-    window = 0.5 - 0.5 * jnp.cos(2.0 * math.pi * (kpos + 0.5) / BAND)
-    sign = jnp.where(tap_index % 2 == 0, 1.0, -1.0)
-    whole = shift == 0.0
-    sinc_gain = jnp.where(whole, gain, sign * amplitude / jnp.where(whole, 1.0, shift))
-    tap_ref[...] = sinc_gain * window
-
-    echo = jnp.transpose(echo_ref[...].astype(jnp.float32))
-    edge = jnp.zeros((SUB, lanes), jnp.float32)
-    for s in range(SUB):
-        copies_ref[s, 0:SUB, :] = edge
-        copies_ref[s, samples : samples + SUB, :] = edge
-        copies_ref[s, SUB - s : SUB - s + samples, :] = echo
-
     ext = round_up(samples + BAND - 1, SUB)
     tail = placed_ref.shape[1] - front - ext
     for tile in range(lanes // LANES):
         placed_ref[tile, :front, :] = jnp.zeros((front, LANES), jnp.float32)
         placed_ref[tile, front + ext :, :] = jnp.zeros((tail, LANES), jnp.float32)
+    edge = jnp.zeros((SUB, lanes), jnp.float32)
+    for s in range(SUB):
+        copies_ref[s, 0:SUB, :] = edge
+        copies_ref[s, samples : samples + SUB, :] = edge
+    tap_index = lax.broadcasted_iota(jnp.int32, (BAND, LANES), 0)
+    window = 0.5 - 0.5 * jnp.cos(2.0 * math.pi * (tap_index.astype(jnp.float32) + 0.5) / BAND)
+    window = jnp.where(tap_index % 2 == 0, window, -window)
+
+    for fetch in fetches:
+        fetch.wait()
+
+    sway = lane_row(sway_ref[...], lanes)
+    gain = lane_row(gain_ref[...], lanes)
+    amplitude = jnp.sin(math.pi * jnp.minimum(sway, 1.0 - sway)) * gain * (1.0 / math.pi)
+    for tile in range(lanes // LANES):
+        cols = slice(tile * LANES, (tile + 1) * LANES)
+        shift = tap_index.astype(jnp.float32) - (BAND / 2 - 1) - sway[:, cols]
+        whole = shift == 0.0
+        signed = jnp.where(tap_index % 2 == 0, gain[:, cols], -gain[:, cols])
+        scaled = jnp.where(whole, signed, amplitude[:, cols] / jnp.where(whole, 1.0, shift))
+        tap_ref[:, cols] = scaled * window
+
+    echo = jnp.transpose(echo_ref[...].astype(jnp.float32))
+    for s in range(SUB):
+        copies_ref[s, SUB - s : SUB - s + samples, :] = echo
+
     group = 8
     blocks = ext // SUB
     for tile in range(lanes // LANES):
@@ -95,8 +119,11 @@
                 value = jnp.zeros((SUB, LANES), jnp.float32) if total[j] is None else total[j]
                 placed_ref[tile, front + j * SUB : front + (j + 1) * SUB, :] = value
 
+    tiles = lanes // LANES
     lane = lax.broadcasted_iota(jnp.int32, (rows, LANES), 1)
-    for tile in range(lanes // LANES):
+    where_row = lax.broadcasted_iota(jnp.int32, (SUB, LANES), 0)
+    place = jnp.zeros((SUB, LANES), jnp.float32)
+    for tile in range(tiles):
         cols = slice(tile * LANES, (tile + 1) * LANES)
         value = None
         for ping in range(pings):
@@ -105,30 +132,46 @@
                 continue
             start = base + offset_ref[ping] + (front + BAND - 1)
             moved = placed_ref[tile, pl.ds(start, rows), :]
-            value = moved if value is None else jnp.where(lane >= low, moved, value)
+            at = lane[:SUB] + (2 * track_ref[ping] - low)
+            if value is None:
+                value, meets = moved, at
+            else:
+                value = jnp.where(lane >= low, moved, value)
+                meets = jnp.where(lane[:SUB] >= low, at, meets)
         out_ref[:, :, cols] = value.reshape(rows // SUB, SUB, LANES).astype(jnp.bfloat16)
-
-
-def own_share(echoes, band_offset, sway_delay, channel_gain, bands):
+        block = (meets // (2 * LANES)).astype(jnp.float32)
+        inside = (meets % (2 * LANES)).astype(jnp.float32)
+        place = jnp.where(where_row == tile, block, place)
+        place = jnp.where(where_row == tiles + tile, inside, place)
+    place = jnp.broadcast_to(place[None], (rows // SUB, SUB, LANES))
+    out_ref[:, :, lanes:] = place.astype(jnp.bfloat16)
+
+
+def own_share(echoes, band_offset, track_bin, sway_delay, channel_gain, bands):
     pings, channels, samples = echoes.shape
     lanes = pings * channels
     rows = samples * min(bands, 3)
     front = round_up(samples + HALO - BAND + 1, SUB)
     height = round_up(front + 2 * samples + HALO - 1, SUB)
-    vmem = pl.BlockSpec(memory_space=pltpu.VMEM)
     return pl.pallas_call(
         functools.partial(fir_kernel, bands, front),
-        out_shape=jax.ShapeDtypeStruct((rows // SUB, SUB, lanes), jnp.bfloat16),
-        in_specs=[pl.BlockSpec(memory_space=pltpu.SMEM), vmem, vmem, vmem],
-        out_specs=vmem,
+        out_shape=jax.ShapeDtypeStruct((rows // SUB, SUB, lanes + LANES), jnp.bfloat16),
+        in_specs=[pl.BlockSpec(memory_space=pltpu.HBM)] * 5,
+        out_specs=pl.BlockSpec(memory_space=pltpu.VMEM),
         scratch_shapes=[
+            pltpu.SMEM((pings,), jnp.int32),
+            pltpu.SMEM((pings,), jnp.int32),
+            pltpu.VMEM((lanes, samples), jnp.bfloat16),
+            pltpu.VMEM((pings, channels), jnp.float32),
+            pltpu.VMEM((pings, channels), jnp.float32),
             pltpu.VMEM((BAND, lanes), jnp.float32),
             pltpu.VMEM((SUB, samples + SUB, lanes), jnp.float32),
             pltpu.VMEM((lanes // LANES, height, LANES), jnp.float32),
+            pltpu.SemaphoreType.DMA((5,)),
         ],
-        compiler_params=pltpu.CompilerParams(vmem_limit_bytes=VMEM_LIMIT),
+        compiler_params=pltpu.CompilerParams(vmem_limit_bytes=56 * MIB),
         name="fir",
-    )(band_offset, echoes.reshape(lanes, samples), sway_delay, channel_gain)
+    )(band_offset, track_bin, echoes.reshape(lanes, samples), sway_delay, channel_gain)
 
 
 def half_turn_sincos(turns):
@@ -175,45 +218,44 @@
         functools.partial(steer_kernel, bands, scaling),
         out_shape=jax.ShapeDtypeStruct((2 * LANES, 2 * blocks * 2 * LANES), jnp.bfloat16),
         out_specs=pl.BlockSpec(memory_space=pltpu.VMEM),
-        compiler_params=pltpu.CompilerParams(vmem_limit_bytes=VMEM_LIMIT),
+        compiler_params=pltpu.CompilerParams(vmem_limit_bytes=16 * MIB),
         name="steer",
     )()
 
 
-def image_kernel(copies, track_ref, share_ref, table_ref, out_ref, *scratch):
+def image_kernel(copies, share_ref, table_ref, out_ref, held_ref):
     groups = out_ref.shape[0]
-    channels_all = share_ref.shape[2]
-    sums, held_ref = scratch[:-1], scratch[-1]
-    half = sums[0].shape[0] // 2
-    pings = track_ref.shape[0] // groups
-    channels = channels_all // pings
-    for ref in sums:
-        ref[...] = jnp.zeros(ref.shape, jnp.float32)
-    lane = lax.broadcasted_iota(jnp.int32, (SUB, LANES), 1)
+    lanes = share_ref.shape[2] - LANES
+    tiles = lanes // LANES
+    half = held_ref.shape[0] // SUB
+    depth = 2 * LANES
+    pair_row = lax.broadcasted_iota(jnp.int32, (2 * SUB, lanes), 0) // SUB
+    pair_row = pair_row.astype(jnp.float32)
+    depth_row = lax.broadcasted_iota(jnp.int32, (depth, lanes), 0).astype(jnp.bfloat16)
+    one, none = jnp.ones((), jnp.bfloat16), jnp.zeros((), jnp.bfloat16)
+    held = None
     for group in range(groups):
-        share = share_ref[group].astype(jnp.float32)
+        share = share_ref[group, :, :lanes].astype(jnp.float32)
         for copy in range(1, copies):
-            share = share + share_ref[copy * groups + group].astype(jnp.float32)
-        for ping in range(pings):
-            tile, low = ping * channels // LANES, ping * channels % LANES
-            at = 2 * track_ref[group * pings + ping]
-            own = share[:, tile * LANES : (tile + 1) * LANES]
-            own = jnp.where((lane >= low) & (lane < low + channels), own, 0.0)
-            inside = at & (LANES - 1)
-            moved = pltpu.roll(own, (at - low) & (LANES - 1), 1)
-            ref = sums[ping % len(sums)]
-            block = at // LANES
-            slot = (block & 1) * half + (block >> 1)
-            after = block + 1
-            slot_after = (after & 1) * half + (after >> 1)
-            ref[slot] = ref[slot] + jnp.where(lane >= inside, moved, 0.0)
-            ref[slot_after] = ref[slot_after] + jnp.where(lane < inside, moved, 0.0)
-    total = sums[0][...]
-    for ref in sums[1:]:
-        total = total + ref[...]
-    total = total.reshape(2 * half * SUB, LANES).astype(jnp.bfloat16)
-    held_ref[:, :LANES] = total[: half * SUB]
-    held_ref[:, LANES:] = total[half * SUB :]
+            share = share + share_ref[copy * groups + group, :, :lanes].astype(jnp.float32)
+        place = share_ref[group, :, lanes:]
+        block = jnp.concatenate([place[i : i + 1] for i in range(tiles)], axis=1)
+        inside = jnp.concatenate([place[tiles + i : tiles + i + 1] for i in range(tiles)], axis=1)
+        block = block.astype(jnp.float32)
+        pair = jnp.concatenate([share, share], axis=0)
+        spread = jnp.concatenate(
+            [
+                jnp.where(pair_row == block - k, pair, 0.0).astype(jnp.bfloat16)
+                for k in range(0, half, 2)
+            ],
+            axis=0,
+        )
+        hot = jnp.where(depth_row == inside, one, none)
+        part = lax.dot_general(
+            spread, hot, (((1,), (1,)), ((), ())), preferred_element_type=jnp.float32
+        )
+        held = part if held is None else held + part
+    held_ref[...] = held.astype(jnp.bfloat16)
 
     blocks = X // LANES
     image = [None] * blocks
@@ -238,22 +280,20 @@
         )
 
 
-def image_share(track, share, table, groups):
+def image_share(share, table, groups):
     copies = share.shape[0] // groups
-    lanes = share.shape[2]
     blocks = X // LANES
     half = round_up(blocks + 1, 2)
     vmem = pl.BlockSpec(memory_space=pltpu.VMEM)
     return pl.pallas_call(
         functools.partial(image_kernel, copies),
         out_shape=jax.ShapeDtypeStruct((groups, SUB, blocks // groups * 2 * LANES), jnp.bfloat16),
-        in_specs=[pl.BlockSpec(memory_space=pltpu.SMEM), vmem, vmem],
+        in_specs=[vmem, vmem],
         out_specs=vmem,
-        scratch_shapes=[pltpu.VMEM((2 * half, SUB, LANES), jnp.float32)] * 4
-        + [pltpu.VMEM((half * SUB, 2 * LANES), jnp.bfloat16)],
-        compiler_params=pltpu.CompilerParams(vmem_limit_bytes=VMEM_LIMIT),
+        scratch_shapes=[pltpu.VMEM((half * SUB, 2 * LANES), jnp.bfloat16)],
+        compiler_params=pltpu.CompilerParams(vmem_limit_bytes=16 * MIB),
         name="image",
-    )(track, share, table)
+    )(share, table)
 
 
 def turn_kernel(in_ref, real_ref, imag_ref):
@@ -274,7 +314,7 @@
         out_shape=(out, out),
         in_specs=[vmem],
         out_specs=(vmem, vmem),
-        compiler_params=pltpu.CompilerParams(vmem_limit_bytes=VMEM_LIMIT),
+        compiler_params=pltpu.CompilerParams(vmem_limit_bytes=4 * MIB),
         name="turn",
     )(image)
 
@@ -283,8 +323,7 @@
     pings, channels, samples = echoes.shape
     bands, groups = lax.axis_size("range"), lax.axis_size("ping")
     scaling = 1.0 / math.sqrt(groups * pings * channels)
-    track = lax.all_gather(track_bin, "ping", tiled=True)
-    share = own_share(echoes, band_offset, sway_delay, channel_gain, bands)
+    share = own_share(echoes, band_offset, track_bin, sway_delay, channel_gain, bands)
     if bands <= 2:
         share = lax.all_to_all(share, ("range", "ping"), 0, 0, tiled=True)
     else:
@@ -297,7 +336,7 @@
             [lax.all_to_all(a, "ping", 0, 0, tiled=True) for a in (own, from_low, from_high)]
         )
     table = steer_table(bands, scaling)
-    image = image_share(track, share, table, groups)
+    image = image_share(share, table, groups)
     image = lax.all_to_all(image, "ping", 0, 0, tiled=True)
     return turned(image, X // groups, samples)
 

time: 45.7 us -> 35.5 us (0.78)
  blocking collectives: 21.7 us -> 10.3 us
  waiting for transfers between devices: 0.01 us -> 5.52 us
  local copies, waits for them, and re-layouts: 7.83 us -> 4.12 us
  between operations: 1.36 us -> 0.67 us
    unnamed x1 -> x0, blocking collectives: 12.3 us -> none
    all_to_all x1, waiting for transfers between devices: 0.01 us -> 5.52 us  [shards(): share = lax.all_to_all(share, ('range', 'ping'), 0, 0, tiled=True)]
    unnamed x19 -> x4, local copies, waits for them, and re-layouts: 7.83 us -> 4.12 us
    all_to_all x1, blocking collectives: 9.47 us -> 10.3 us  [shards(): image = lax.all_to_all(image, 'ping', 0, 0, tiled=True)]
  transfers between devices with their start and end apart: 1 -> 1, of which waited for: 0 -> 1; matrix products, arithmetic and copies ran while one was open for 2% -> 0% of each run, Pallas kernels for 3% -> 4%
where the time goes in v2:
time: 35.5 us; the launch traced here: 35.3 us
  blocking collectives  10.3 us (29%)
  Pallas kernels  7.35 us (21%)
  starting transfers between devices  7.3 us (21%)
  waiting for transfers between devices  5.52 us (16%)
  local copies, waits for them, and re-layouts  4.12 us (12%)
  between operations  0.67 us (2%)
    all_to_all x1, blocking collectives, shards(): image = lax.all_to_all(image, 'ping', 0, 0, tiled=True)  10.3 us
    all_to_all x1, starting transfers between devices, shards(): share = lax.all_to_all(share, ('range', 'ping'), 0, 0, tiled=True)  7.3 us
    all_to_all x1, waiting for transfers between devices, shards(): share = lax.all_to_all(share, ('range', 'ping'), 0, 0, tiled=True)  5.52 us
    unnamed x4, local copies, waits for them, and re-layouts  4.12 us
    pallas_call x1, Pallas kernels, own_share(): pl.pallas_call(functools.partial(fir_kernel, bands, front), out_shape=jax...  2.71 us
    pallas_call x1, Pallas kernels, image_share(): pl.pallas_call(functools.partial(image_kernel, copies), out_shape=jax.Sha...  2.48 us
    pallas_call x1, Pallas kernels, steer_table(): pl.pallas_call(functools.partial(steer_kernel, bands, scaling), out_shape...  1.41 us
    pallas_call x1, Pallas kernels, turned(): pl.pallas_call(turn_kernel, out_shape=(out, out), in_specs=[vmem], out_sp...  0.75 us
  transfers between devices with their start and end apart: 1, of which 1 were waited for; matrix products, arithmetic and copies ran while one was open for 0% of the time, Pallas kernels for 4%

profile of v2, /device:TPU:0, one launch (start us, length us, event | category | flops | bytes accessed | tf_op | source)
XLA Modules:
  0.0 35.3 jit_solution(96108805950023657)
XLA Ops:
  0.6 2.7 %fir.1 = bf16[32,8,384]{2,1,0:T(8,128)(2,1)} custom-call(s32[8]{0:T(128)} %offset_hbm.1, s32[8]{0:T(128)} %track_hbm.1, bf16[256,128]{1,0:T(8,128)(2,1)} %bitcast.1, f32[8,32]{1,0:T(8,128)} %sway_hbm.1, f32[8,32]{1,0:T(8,128)} %gain_hbm.1), custom_call_target="tpu_custom_call" | custom-call | tf_op jit(solution)/shard_map/fir/pallas_call | solution.py:156
  3.3 7.3 %all-to-all-start = ((bf16[32,8,384]{2,1,0:T(8,128)(2,1)}), bf16[32,8,384]{2,1,0:T(8,128)(2,1)S(1)}, u32[]{:S(2)}, u32[]{:S(2)}) async-start(bf16[32,8,384]{2,1,0:T(8,128)(2,1)} %fir.1), calls=%async_computation | async-start | bytes 393216 | tf_op jit(solution)/shard_map/all_to_all | solution.py:328
  10.7 1.4 %steer.1.table_ref = bf16[256,8192]{1,0:T(8,128)(2,1)S(1)} custom-call(), custom_call_target="tpu_custom_call" | custom-call | tf_op jit(solution)/shard_map/steer/pallas_call | solution.py:217
  12.1 0.0 copy-start
  12.1 1.9 %copy-done = bf16[256,8192]{1,0:T(8,128)(2,1)} copy-done((bf16[256,8192]{1,0:T(8,128)(2,1)}, bf16[256,8192]{1,0:T(8,128)(2,1)S(1)}, u32[]{:S(2)}) %copy-start) | copy-done | bytes 4194328
  14.0 5.5 %all-to-all-done.share_ref = bf16[32,8,384]{2,1,0:T(8,128)(2,1)S(1)} async-done(((bf16[32,8,384]{2,1,0:T(8,128)(2,1)}), bf16[32,8,384]{2,1,0:T(8,128)(2,1)S(1)}, u32[]{:S(2)}, u32[]{:S(2)}) %all-to-all-start) | async-done | bytes 196640 | tf_op jit(solution)/shard_map/all_to_all | solution.py:328
  19.5 0.0 copy-start.1
  19.5 2.2 %copy-done.1 = bf16[256,8192]{1,0:T(8,128)(2,1)S(1)} copy-done((bf16[256,8192]{1,0:T(8,128)(2,1)S(1)}, bf16[256,8192]{1,0:T(8,128)(2,1)}, u32[]{:S(2)}) %copy-start.1) | copy-done | bytes 4194328
  21.7 2.5 %image.1 = bf16[16,8,256]{2,1,0:T(8,128)(2,1)S(1)} custom-call(bf16[32,8,384]{2,1,0:T(8,128)(2,1)S(1)} %all-to-all-done.share_ref, bf16[256,8192]{1,0:T(8,128)(2,1)S(1)} %copy-done.1), custom_call_target="tpu_custom_call" | custom-call | tf_op jit(solution)/shard_map/image/pallas_call | solution.py:288
  24.2 10.3 %all_to_all.10.in_ref = bf16[16,8,256]{2,1,0:T(8,128)(2,1)S(1)} all-to-all(bf16[16,8,256]{2,1,0:T(8,128)(2,1)S(1)} %image.1), channel_id=1, replica_groups=mesh['range'=2,'ping'=16] {'ping'}, dimensions={0} | all-to-all | bytes 131072 | tf_op jit(solution)/shard_map/all_to_all | solution.py:340
  34.5 0.8 %turn.1 = (f32[128,128]{1,0:T(8,128)}, f32[128,128]{1,0:T(8,128)}) custom-call(bf16[16,8,256]{2,1,0:T(8,128)(2,1)S(1)} %all_to_all.10.in_ref), custom_call_target="tpu_custom_call" | custom-call | tf_op jit(solution)/shard_map/turn/pallas_call | solution.py:312
Async XLA Ops:
  3.3 16.2 %all-to-all-start = ((bf16[32,8,384]{2,1,0:T(8,128)(2,1)}), bf16[32,8,384]{2,1,0:T(8,128)(2,1)S(1)}, u32[]{:S(2)}, u32[]{:S(2)}) async-start(bf16[32,8,384]{2,1,0:T(8,128)(2,1)} %fir.1), calls=%async_computation | async-start | bytes 393216 | tf_op jit(solution)/shard_map/all_to_all | solution.py:328
  12.1 1.9 %copy-start = (bf16[256,8192]{1,0:T(8,128)(2,1)}, bf16[256,8192]{1,0:T(8,128)(2,1)S(1)}, u32[]{:S(2)}) copy-start(bf16[256,8192]{1,0:T(8,128)(2,1)S(1)} %steer.1.table_ref) | copy-start | bytes 12582916
  19.5 2.2 %copy-start.1 = (bf16[256,8192]{1,0:T(8,128)(2,1)S(1)}, bf16[256,8192]{1,0:T(8,128)(2,1)}, u32[]{:S(2)}) copy-start(bf16[256,8192]{1,0:T(8,128)(2,1)} %copy-done) | copy-start | bytes 12582916

commit v3 on v2

--- a/solution.py
+++ b/solution.py
@@ -18,6 +18,10 @@
 
 def round_up(value, unit):
     return -(-value // unit) * unit
+
+
+def in_hbm(array):
+    return pltpu.with_memory_space_constraint(array, pltpu.HBM)
 
 
 def lane_row(values, lanes):
@@ -155,7 +159,7 @@
     height = round_up(front + 2 * samples + HALO - 1, SUB)
     return pl.pallas_call(
         functools.partial(fir_kernel, bands, front),
-        out_shape=jax.ShapeDtypeStruct((rows // SUB, SUB, lanes + LANES), jnp.bfloat16),
+        out_shape=pltpu.VMEM((rows // SUB, SUB, lanes + LANES), jnp.bfloat16),
         in_specs=[pl.BlockSpec(memory_space=pltpu.HBM)] * 5,
         out_specs=pl.BlockSpec(memory_space=pltpu.VMEM),
         scratch_shapes=[
@@ -169,9 +173,15 @@
             pltpu.VMEM((lanes // LANES, height, LANES), jnp.float32),
             pltpu.SemaphoreType.DMA((5,)),
         ],
-        compiler_params=pltpu.CompilerParams(vmem_limit_bytes=56 * MIB),
+        compiler_params=pltpu.CompilerParams(vmem_limit_bytes=8 * MIB),
         name="fir",
-    )(band_offset, track_bin, echoes.reshape(lanes, samples), sway_delay, channel_gain)
+    )(
+        in_hbm(band_offset),
+        in_hbm(track_bin),
+        in_hbm(echoes.reshape(lanes, samples)),
+        in_hbm(sway_delay),
+        in_hbm(channel_gain),
+    )
 
 
 def half_turn_sincos(turns):
@@ -186,8 +196,7 @@
 
 
 def steer_kernel(bands, scaling, out_ref):
-    depth, width = out_ref.shape
-    spans = width // (2 * LANES)
+    spans, depth, _ = out_ref.shape
     band = lax.axis_index("range").astype(jnp.float32)
     spread = 0.5 * X * (1.0 + (band + 0.5) * (1.0 / bands))
     length = (spans + 1) * LANES
@@ -206,8 +215,7 @@
             ]
             both = jnp.concatenate(moved, axis=0).astype(jnp.bfloat16)
             for span in range(spans):
-                at = (2 * span + part) * LANES
-                out_ref[first : first + 2 * SUB, at : at + LANES] = both[
+                out_ref[span, first : first + 2 * SUB, part * LANES : (part + 1) * LANES] = both[
                     :, (span + 1) * LANES : (span + 2) * LANES
                 ]
 
@@ -216,14 +224,22 @@
     blocks = X // LANES
     return pl.pallas_call(
         functools.partial(steer_kernel, bands, scaling),
-        out_shape=jax.ShapeDtypeStruct((2 * LANES, 2 * blocks * 2 * LANES), jnp.bfloat16),
+        out_shape=pltpu.HBM((2 * blocks, 2 * LANES, 2 * LANES), jnp.bfloat16),
         out_specs=pl.BlockSpec(memory_space=pltpu.VMEM),
         compiler_params=pltpu.CompilerParams(vmem_limit_bytes=16 * MIB),
         name="steer",
     )()
 
 
-def image_kernel(copies, share_ref, table_ref, out_ref, held_ref):
+def image_kernel(copies, share_ref, table_hbm, out_ref, held_ref, table_ref, sems):
+    parts = sems.shape[0]
+    steps = table_ref.shape[0] // parts
+    fetches = []
+    for i in range(parts):
+        at = pl.ds(i * steps, steps)
+        fetches.append(pltpu.make_async_copy(table_hbm.at[at], table_ref.at[at], sems.at[i]))
+        fetches[-1].start()
+
     groups = out_ref.shape[0]
     lanes = share_ref.shape[2] - LANES
     tiles = lanes // LANES
@@ -263,10 +279,11 @@
         first, last = max(0, -step), min(blocks, blocks - 1 - step)
         low = first - first % 2
         high = min(half, low + round_up(last + 1 - low, 2))
-        at = (step + blocks) * 2 * LANES
+        if (step + blocks) % steps == 0:
+            fetches[(step + blocks) // steps].wait()
         part = jnp.dot(
             held_ref[low * SUB : high * SUB, :],
-            table_ref[:, at : at + 2 * LANES],
+            table_ref[step + blocks],
             preferred_element_type=jnp.float32,
         )
         for k in range(first, last + 1):
@@ -288,12 +305,16 @@
     return pl.pallas_call(
         functools.partial(image_kernel, copies),
         out_shape=jax.ShapeDtypeStruct((groups, SUB, blocks // groups * 2 * LANES), jnp.bfloat16),
-        in_specs=[vmem, vmem],
+        in_specs=[vmem, pl.BlockSpec(memory_space=pltpu.HBM)],
         out_specs=vmem,
-        scratch_shapes=[pltpu.VMEM((half * SUB, 2 * LANES), jnp.bfloat16)],
+        scratch_shapes=[
+            pltpu.VMEM((half * SUB, 2 * LANES), jnp.bfloat16),
+            pltpu.VMEM(table.shape, table.dtype),
+            pltpu.SemaphoreType.DMA((8,)),
+        ],
         compiler_params=pltpu.CompilerParams(vmem_limit_bytes=16 * MIB),
         name="image",
-    )(share, table)
+    )(share, in_hbm(table))
 
 
 def turn_kernel(in_ref, real_ref, imag_ref):

time: 35.5 us -> 35.2 us (level)
  local copies, waits for them, and re-layouts: 4.12 us -> 0 us
  Pallas kernels: 7.35 us -> 11.3 us
    unnamed x4 -> x0, local copies, waits for them, and re-layouts: 4.12 us -> none
    pallas_call x1, Pallas kernels: 1.41 us -> 3.45 us  [steer_table(): pl.pallas_call(functools.partial(steer_kernel, bands, scaling), out_shape...]
    pallas_call x1, Pallas kernels: 2.48 us -> 4.36 us  [image_share(): pl.pallas_call(functools.partial(image_kernel, copies), out_shape=jax.Sha...]
  transfers between devices with their start and end apart: 1 -> 1, of which waited for: 1 -> 1; matrix products, arithmetic and copies ran while one was open for 0% -> 0% of each run, Pallas kernels for 4% -> 10%
where the time goes in v3:
time: 35.2 us; the launch traced here: 34.9 us
  Pallas kernels  11.3 us (32%)
  blocking collectives  10.3 us (29%)
  starting transfers between devices  7.3 us (21%)
  waiting for transfers between devices  5.43 us (15%)
  between operations  0.66 us (2%)
    all_to_all x1, blocking collectives, shards(): image = lax.all_to_all(image, 'ping', 0, 0, tiled=True)  10.3 us
    all_to_all x1, starting transfers between devices, shards(): share = lax.all_to_all(share, ('range', 'ping'), 0, 0, tiled=True)  7.3 us
    all_to_all x1, waiting for transfers between devices, shards(): share = lax.all_to_all(share, ('range', 'ping'), 0, 0, tiled=True)  5.43 us
    pallas_call x1, Pallas kernels, image_share(): pl.pallas_call(functools.partial(image_kernel, copies), out_shape=jax.Sha...  4.36 us
    pallas_call x1, Pallas kernels, steer_table(): pl.pallas_call(functools.partial(steer_kernel, bands, scaling), out_shape...  3.45 us
    pallas_call x1, Pallas kernels, own_share(): pl.pallas_call(functools.partial(fir_kernel, bands, front), out_shape=plt...  2.7 us
    pallas_call x1, Pallas kernels, turned(): pl.pallas_call(turn_kernel, out_shape=(out, out), in_specs=[vmem], out_sp...  0.75 us
  transfers between devices with their start and end apart: 1, of which 1 were waited for; matrix products, arithmetic and copies ran while one was open for 0% of the time, Pallas kernels for 10%

profile of v3, /device:TPU:0, one launch (start us, length us, event | category | flops | bytes accessed | tf_op | source)
XLA Modules:
  0.0 34.9 jit_solution(16130051536194967169)
XLA Ops:
  0.6 2.7 %fir.1 = bf16[32,8,384]{2,1,0:T(8,128)(2,1)} custom-call(s32[8]{0:T(128)} %offset_hbm.1, s32[8]{0:T(128)} %track_hbm.1, bf16[256,128]{1,0:T(8,128)(2,1)} %bitcast.1, f32[8,32]{1,0:T(8,128)} %sway_hbm.1, f32[8,32]{1,0:T(8,128)} %gain_hbm.1), custom_call_target="tpu_custom_call" | custom-call | tf_op jit(solution)/shard_map/fir/pallas_call | solution.py:160
  3.3 7.3 %all-to-all-start = ((bf16[32,8,384]{2,1,0:T(8,128)(2,1)}), bf16[32,8,384]{2,1,0:T(8,128)(2,1)S(1)}, u32[]{:S(2)}, u32[]{:S(2)}) async-start(bf16[32,8,384]{2,1,0:T(8,128)(2,1)} %fir.1), calls=%async_computation | async-start | bytes 393216 | tf_op jit(solution)/shard_map/all_to_all | solution.py:349
  10.6 3.5 %steer.1.table_hbm = bf16[32,256,256]{2,1,0:T(8,128)(2,1)} custom-call(), custom_call_target="tpu_custom_call" | custom-call | tf_op jit(solution)/shard_map/steer/pallas_call | solution.py:225
  14.1 5.4 %all-to-all-done.share_ref = bf16[32,8,384]{2,1,0:T(8,128)(2,1)S(1)} async-done(((bf16[32,8,384]{2,1,0:T(8,128)(2,1)}), bf16[32,8,384]{2,1,0:T(8,128)(2,1)S(1)}, u32[]{:S(2)}, u32[]{:S(2)}) %all-to-all-start) | async-done | bytes 196640 | tf_op jit(solution)/shard_map/all_to_all | solution.py:349
  19.5 4.4 %image.1 = bf16[16,8,256]{2,1,0:T(8,128)(2,1)S(1)} custom-call(bf16[32,8,384]{2,1,0:T(8,128)(2,1)S(1)} %all-to-all-done.share_ref, bf16[32,256,256]{2,1,0:T(8,128)(2,1)} %steer.1.table_hbm), custom_call_target="tpu_custom_call" | custom-call | tf_op jit(solution)/shard_map/image/pallas_call | solution.py:305
  23.9 10.3 %all_to_all.10.in_ref = bf16[16,8,256]{2,1,0:T(8,128)(2,1)S(1)} all-to-all(bf16[16,8,256]{2,1,0:T(8,128)(2,1)S(1)} %image.1), channel_id=1, replica_groups=mesh['range'=2,'ping'=16] {'ping'}, dimensions={0} | all-to-all | bytes 131072 | tf_op jit(solution)/shard_map/all_to_all | solution.py:361
  34.2 0.8 %turn.1 = (f32[128,128]{1,0:T(8,128)}, f32[128,128]{1,0:T(8,128)}) custom-call(bf16[16,8,256]{2,1,0:T(8,128)(2,1)S(1)} %all_to_all.10.in_ref), custom_call_target="tpu_custom_call" | custom-call | tf_op jit(solution)/shard_map/turn/pallas_call | solution.py:333
Async XLA Ops:
  3.3 16.2 %all-to-all-start = ((bf16[32,8,384]{2,1,0:T(8,128)(2,1)}), bf16[32,8,384]{2,1,0:T(8,128)(2,1)S(1)}, u32[]{:S(2)}, u32[]{:S(2)}) async-start(bf16[32,8,384]{2,1,0:T(8,128)(2,1)} %fir.1), calls=%async_computation | async-start | bytes 393216 | tf_op jit(solution)/shard_map/all_to_all | solution.py:349

commit v4 on v3

--- a/solution.py
+++ b/solution.py
@@ -14,6 +14,7 @@
 LANES = 128
 SUB = 8
 MIB = 1024 * 1024
+FAR = 2
 
 
 def round_up(value, unit):
@@ -35,6 +36,7 @@
 def fir_kernel(
     bands,
     front,
+    stack,
     offset_hbm,
     track_hbm,
     echo_hbm,
@@ -63,7 +65,8 @@
         fetch.start()
     pings, channels = sway_ref.shape
     lanes, samples = echo_ref.shape
-    rows = out_ref.shape[0] * out_ref.shape[1]
+    chunks = out_ref.shape[0]
+    rows = chunks * stack * SUB
     if bands == 1:
         base = 0
     elif bands == 2:
@@ -142,24 +145,28 @@
             else:
                 value = jnp.where(lane >= low, moved, value)
                 meets = jnp.where(lane[:SUB] >= low, at, meets)
-        out_ref[:, :, cols] = value.reshape(rows // SUB, SUB, LANES).astype(jnp.bfloat16)
+        value = value.astype(jnp.bfloat16).reshape(chunks, stack, SUB, LANES)
+        for more in range(stack):
+            at = more * lanes + tile * LANES
+            out_ref[:, :, at : at + LANES] = value[:, more]
         block = (meets // (2 * LANES)).astype(jnp.float32)
         inside = (meets % (2 * LANES)).astype(jnp.float32)
         place = jnp.where(where_row == tile, block, place)
         place = jnp.where(where_row == tiles + tile, inside, place)
-    place = jnp.broadcast_to(place[None], (rows // SUB, SUB, LANES))
-    out_ref[:, :, lanes:] = place.astype(jnp.bfloat16)
-
-
-def own_share(echoes, band_offset, track_bin, sway_delay, channel_gain, bands):
+    place = jnp.broadcast_to(place[None], (chunks, SUB, LANES))
+    out_ref[:, :, stack * lanes :] = place.astype(jnp.bfloat16)
+
+
+def own_share(echoes, band_offset, track_bin, sway_delay, channel_gain, bands, near):
     pings, channels, samples = echoes.shape
     lanes = pings * channels
-    rows = samples * min(bands, 3)
+    chunks = near * min(bands, 3)
+    stack = samples // near // SUB
     front = round_up(samples + HALO - BAND + 1, SUB)
     height = round_up(front + 2 * samples + HALO - 1, SUB)
     return pl.pallas_call(
-        functools.partial(fir_kernel, bands, front),
-        out_shape=pltpu.VMEM((rows // SUB, SUB, lanes + LANES), jnp.bfloat16),
+        functools.partial(fir_kernel, bands, front, stack),
+        out_shape=pltpu.VMEM((chunks, SUB, stack * lanes + LANES), jnp.bfloat16),
         in_specs=[pl.BlockSpec(memory_space=pltpu.HBM)] * 5,
         out_specs=pl.BlockSpec(memory_space=pltpu.VMEM),
         scratch_shapes=[
@@ -195,76 +202,56 @@
     return 2.0 * sine * cos_sum, 1.0 - 2.0 * sine * sine
 
 
-def steer_kernel(bands, scaling, out_ref):
-    spans, depth, _ = out_ref.shape
+def fill_table(bands, scaling, table_ref):
+    steps, depth, _ = table_ref.shape
     band = lax.axis_index("range").astype(jnp.float32)
     spread = 0.5 * X * (1.0 + (band + 0.5) * (1.0 / bands))
-    length = (spans + 1) * LANES
-    lane = lax.broadcasted_iota(jnp.int32, (SUB, length), 1) - (spans // 2 + 1) * LANES
-    row = lax.broadcasted_iota(jnp.int32, (SUB, length), 0)
+    length = (steps + 1) * LANES
+    pack = 2 * SUB
+    lane = lax.broadcasted_iota(jnp.int32, (pack, length), 1) - (steps // 2 + 1) * LANES
+    row = lax.broadcasted_iota(jnp.int32, (pack, length), 0)
     twice = (2 * lane - row).astype(jnp.float32)
     square = twice * twice
     weight = jnp.exp(square * (-0.125 * (8.0 / X) ** 2)) * scaling
     sine, cosine = half_turn_sincos(square * (0.125 / spread))
-    parts = (weight * cosine, weight * sine)
-    for first in range(0, depth, 2 * SUB):
-        for part in range(2):
-            moved = [
-                pltpu.roll(parts[part], (first + more) // 2, 1) if first + more else parts[part]
-                for more in (0, SUB)
-            ]
-            both = jnp.concatenate(moved, axis=0).astype(jnp.bfloat16)
-            for span in range(spans):
-                out_ref[span, first : first + 2 * SUB, part * LANES : (part + 1) * LANES] = both[
-                    :, (span + 1) * LANES : (span + 2) * LANES
+    parts = ((weight * cosine).astype(jnp.bfloat16), (weight * sine).astype(jnp.bfloat16))
+    for first in range(0, depth, pack):
+        for i, part in enumerate(parts):
+            moved = pltpu.roll(part, first // 2, 1) if first else part
+            for step in range(steps):
+                table_ref[step, first : first + pack, i * LANES : (i + 1) * LANES] = moved[
+                    :, (step + 1) * LANES : (step + 2) * LANES
                 ]
 
 
-def steer_table(bands, scaling):
-    blocks = X // LANES
-    return pl.pallas_call(
-        functools.partial(steer_kernel, bands, scaling),
-        out_shape=pltpu.HBM((2 * blocks, 2 * LANES, 2 * LANES), jnp.bfloat16),
-        out_specs=pl.BlockSpec(memory_space=pltpu.VMEM),
-        compiler_params=pltpu.CompilerParams(vmem_limit_bytes=16 * MIB),
-        name="steer",
-    )()
-
-
-def image_kernel(copies, share_ref, table_hbm, out_ref, held_ref, table_ref, sems):
-    parts = sems.shape[0]
-    steps = table_ref.shape[0] // parts
-    fetches = []
-    for i in range(parts):
-        at = pl.ds(i * steps, steps)
-        fetches.append(pltpu.make_async_copy(table_hbm.at[at], table_ref.at[at], sems.at[i]))
-        fetches[-1].start()
-
+def image_kernel(bands, scaling, near, share_ref, out_ref, held_ref, table_ref):
     groups = out_ref.shape[0]
-    lanes = share_ref.shape[2] - LANES
+    copies = share_ref.shape[0] // near
+    depth = 2 * LANES
+    stack = out_ref.shape[2] // (X // groups // LANES * depth)
+    rows = stack * SUB
+    lanes = (share_ref.shape[2] - LANES) // stack
     tiles = lanes // LANES
-    half = held_ref.shape[0] // SUB
-    depth = 2 * LANES
-    pair_row = lax.broadcasted_iota(jnp.int32, (2 * SUB, lanes), 0) // SUB
-    pair_row = pair_row.astype(jnp.float32)
+    half = held_ref.shape[0] // rows
+    fill_table(bands, scaling, table_ref)
+
     depth_row = lax.broadcasted_iota(jnp.int32, (depth, lanes), 0).astype(jnp.bfloat16)
     one, none = jnp.ones((), jnp.bfloat16), jnp.zeros((), jnp.bfloat16)
     held = None
-    for group in range(groups):
-        share = share_ref[group, :, :lanes].astype(jnp.float32)
+    for group in range(near):
+        share = share_ref[group, :, : stack * lanes].astype(jnp.float32)
         for copy in range(1, copies):
-            share = share + share_ref[copy * groups + group, :, :lanes].astype(jnp.float32)
-        place = share_ref[group, :, lanes:]
+            more = share_ref[copy * near + group, :, : stack * lanes]
+            share = share + more.astype(jnp.float32)
+        share = jnp.concatenate(
+            [share[:, i * lanes : (i + 1) * lanes] for i in range(stack)], axis=0
+        ).astype(jnp.bfloat16)
+        place = share_ref[group, :, stack * lanes :]
         block = jnp.concatenate([place[i : i + 1] for i in range(tiles)], axis=1)
         inside = jnp.concatenate([place[tiles + i : tiles + i + 1] for i in range(tiles)], axis=1)
-        block = block.astype(jnp.float32)
-        pair = jnp.concatenate([share, share], axis=0)
+        block = jnp.broadcast_to(block, share.shape)
         spread = jnp.concatenate(
-            [
-                jnp.where(pair_row == block - k, pair, 0.0).astype(jnp.bfloat16)
-                for k in range(0, half, 2)
-            ],
-            axis=0,
+            [jnp.where(block == float(k), share, none) for k in range(half)], axis=0
         )
         hot = jnp.where(depth_row == inside, one, none)
         part = lax.dot_general(
@@ -277,61 +264,65 @@
     image = [None] * blocks
     for step in range(-blocks, blocks):
         first, last = max(0, -step), min(blocks, blocks - 1 - step)
-        low = first - first % 2
-        high = min(half, low + round_up(last + 1 - low, 2))
-        if (step + blocks) % steps == 0:
-            fetches[(step + blocks) // steps].wait()
         part = jnp.dot(
-            held_ref[low * SUB : high * SUB, :],
+            held_ref[first * rows : (last + 1) * rows, :],
             table_ref[step + blocks],
             preferred_element_type=jnp.float32,
         )
         for k in range(first, last + 1):
-            term = part[(k - low) * SUB : (k - low + 1) * SUB]
+            term = part[(k - first) * rows : (k - first + 1) * rows]
             image[k + step] = term if image[k + step] is None else image[k + step] + term
     share_rows = blocks // groups
     for block in range(blocks):
         group, within = block // share_rows, block % share_rows
-        out_ref[group, :, within * 2 * LANES : (within + 1) * 2 * LANES] = image[block].astype(
-            jnp.bfloat16
-        )
-
-
-def image_share(share, table, groups):
-    copies = share.shape[0] // groups
+        value = image[block].astype(jnp.bfloat16)
+        for i in range(stack):
+            at = (i * share_rows + within) * depth
+            out_ref[group, :, at : at + depth] = value[i * SUB : (i + 1) * SUB]
+
+
+def image_share(share, bands, scaling, far, near, stack):
+    groups = far * near
     blocks = X // LANES
-    half = round_up(blocks + 1, 2)
+    depth = 2 * LANES
     vmem = pl.BlockSpec(memory_space=pltpu.VMEM)
     return pl.pallas_call(
-        functools.partial(image_kernel, copies),
-        out_shape=jax.ShapeDtypeStruct((groups, SUB, blocks // groups * 2 * LANES), jnp.bfloat16),
-        in_specs=[vmem, pl.BlockSpec(memory_space=pltpu.HBM)],
+        functools.partial(image_kernel, bands, scaling, near),
+        out_shape=jax.ShapeDtypeStruct(
+            (groups, SUB, stack * (blocks // groups) * depth), jnp.bfloat16
+        ),
+        in_specs=[vmem],
         out_specs=vmem,
         scratch_shapes=[
-            pltpu.VMEM((half * SUB, 2 * LANES), jnp.bfloat16),
-            pltpu.VMEM(table.shape, table.dtype),
-            pltpu.SemaphoreType.DMA((8,)),
+            pltpu.VMEM(((blocks + 1) * stack * SUB, depth), jnp.bfloat16),
+            pltpu.VMEM((2 * blocks, depth, depth), jnp.bfloat16),
         ],
         compiler_params=pltpu.CompilerParams(vmem_limit_bytes=16 * MIB),
         name="image",
-    )(share, in_hbm(table))
-
-
-def turn_kernel(in_ref, real_ref, imag_ref):
+    )(share)
+
+
+def turn_kernel(far, stack, in_ref, real_ref, imag_ref):
     groups, sub, width = in_ref.shape
-    whole = in_ref[...].astype(jnp.float32).reshape(groups * sub, width)
-    for block in range(width // (2 * LANES)):
+    near = groups // far
+    whole = in_ref[:near].astype(jnp.float32)
+    for i in range(1, far):
+        whole = whole + in_ref[i * near : (i + 1) * near].astype(jnp.float32)
+    part = width // stack
+    whole = jnp.stack([whole[:, :, i * part : (i + 1) * part] for i in range(stack)], axis=1)
+    whole = whole.reshape(near * stack * sub, part)
+    for block in range(part // (2 * LANES)):
         rows = slice(block * LANES, (block + 1) * LANES)
         at = block * 2 * LANES
         real_ref[rows, :] = jnp.transpose(whole[:, at : at + LANES])
         imag_ref[rows, :] = jnp.transpose(whole[:, at + LANES : at + 2 * LANES])
 
 
-def turned(image, rows, samples):
+def turned(image, rows, samples, far, stack):
     vmem = pl.BlockSpec(memory_space=pltpu.VMEM)
     out = jax.ShapeDtypeStruct((rows, samples), jnp.float32)
     return pl.pallas_call(
-        turn_kernel,
+        functools.partial(turn_kernel, far, stack),
         out_shape=(out, out),
         in_specs=[vmem],
         out_specs=(vmem, vmem),
@@ -342,11 +333,12 @@
 
 def shards(echoes, band_offset, sway_delay, channel_gain, track_bin):
     pings, channels, samples = echoes.shape
-    bands, groups = lax.axis_size("range"), lax.axis_size("ping")
-    scaling = 1.0 / math.sqrt(groups * pings * channels)
-    share = own_share(echoes, band_offset, track_bin, sway_delay, channel_gain, bands)
+    bands, far, near = (lax.axis_size(axis) for axis in ("range", "far", "near"))
+    stack = samples // near // SUB
+    scaling = 1.0 / math.sqrt(far * near * pings * channels)
+    share = own_share(echoes, band_offset, track_bin, sway_delay, channel_gain, bands, near)
     if bands <= 2:
-        share = lax.all_to_all(share, ("range", "ping"), 0, 0, tiled=True)
+        share = lax.all_to_all(share, ("range", "near"), 0, 0, tiled=True)
     else:
         low, own, high = jnp.split(share, 3)
         up = [(i, i + 1) for i in range(bands - 1)]
@@ -354,19 +346,24 @@
         from_low = lax.ppermute(high, "range", up)
         from_high = lax.ppermute(low, "range", down)
         share = jnp.concatenate(
-            [lax.all_to_all(a, "ping", 0, 0, tiled=True) for a in (own, from_low, from_high)]
+            [lax.all_to_all(a, "near", 0, 0, tiled=True) for a in (own, from_low, from_high)]
         )
-    table = steer_table(bands, scaling)
-    image = image_share(share, table, groups)
-    image = lax.all_to_all(image, "ping", 0, 0, tiled=True)
-    return turned(image, X // groups, samples)
+    image = image_share(share, bands, scaling, far, near, stack)
+    image = lax.all_to_all(image, ("far", "near"), 0, 0, tiled=True)
+    return turned(image, X // (far * near), samples, far, stack)
 
 
 def solution(mesh):
+    bands, groups = mesh.shape["range"], mesh.shape["ping"]
+    far = FAR if groups % FAR == 0 else 1
+    split = jax.sharding.Mesh(
+        mesh.devices.reshape(bands, far, groups // far), ("range", "far", "near")
+    )
+    ping = ("far", "near")
     return jax.shard_map(
         shards,
-        mesh=mesh,
-        in_specs=(P("ping", None, "range"), P("ping"), P("ping", None), P("ping", None), P("ping")),
-        out_specs=(P("ping", "range"), P("ping", "range")),
+        mesh=split,
+        in_specs=(P(ping, None, "range"), P(ping), P(ping, None), P(ping, None), P(ping)),
+        out_specs=(P(ping, "range"), P(ping, "range")),
         check_vma=False,
     )

time: 35.2 us -> 30.2 us (0.86)
  blocking collectives: 10.3 us -> 24.5 us
  starting transfers between devices: 7.3 us -> 0 us
  Pallas kernels: 11.3 us -> 4.86 us
  waiting for transfers between devices: 5.43 us -> 0 us
    all_to_all x1 -> x2, blocking collectives: 10.3 us -> 24.5 us  [the longest x1 12.8 us: shards(): share = lax.all_to_all(share, ('range', 'near'), 0, 0, tiled=True)]
    all_to_all x1 -> x0, starting transfers between devices: 7.3 us -> none  [shards(): share = lax.all_to_all(share, ('range', 'ping'), 0, 0, tiled=True)]
    pallas_call x4 -> x3, Pallas kernels: 11.3 us -> 4.86 us  [the longest x1 2.07 us: image_share(): pl.pallas_call(functools.partial(image_kernel, bands, scaling, near), out...]
    all_to_all x1 -> x0, waiting for transfers between devices: 5.43 us -> none  [shards(): share = lax.all_to_all(share, ('range', 'ping'), 0, 0, tiled=True)]
  transfers between devices with their start and end apart: 1 -> 0, of which waited for: 1 -> 0; matrix products, arithmetic and copies ran while one was open for 0% -> 0% of each run, Pallas kernels for 10% -> 0%
where the time goes in v4:
time: 30.2 us; the launch traced here: 30 us
  blocking collectives  24.5 us (81%)
  Pallas kernels  4.86 us (16%)
  between operations  0.64 us (2%)
    all_to_all x1, blocking collectives, shards(): share = lax.all_to_all(share, ('range', 'near'), 0, 0, tiled=True)  12.8 us
    all_to_all x1, blocking collectives, shards(): image = lax.all_to_all(image, ('far', 'near'), 0, 0, tiled=True)  11.7 us
    pallas_call x1, Pallas kernels, image_share(): pl.pallas_call(functools.partial(image_kernel, bands, scaling, near), out...  2.07 us
    pallas_call x1, Pallas kernels, own_share(): pl.pallas_call(functools.partial(fir_kernel, bands, front, stack), out_sh...  2.04 us
    pallas_call x1, Pallas kernels, turned(): pl.pallas_call(functools.partial(turn_kernel, far, stack), out_shape=(out...  0.75 us

profile of v4, /device:TPU:0, one launch (start us, length us, event | category | flops | bytes accessed | tf_op | source)
XLA Modules:
  0.0 30.0 jit_solution(1176023810169349640)
XLA Ops:
  0.6 2.0 %fir.1 = bf16[16,8,640]{2,1,0:T(8,128)(2,1)S(1)} custom-call(s32[8]{0:T(128)} %offset_hbm.1, s32[8]{0:T(128)} %track_hbm.1, bf16[256,128]{1,0:T(8,128)(2,1)} %bitcast.1, f32[8,32]{1,0:T(8,128)} %sway_hbm.1, f32[8,32]{1,0:T(8,128)} %gain_hbm.1), custom_call_target="tpu_custom_call" | custom-call | tf_op jit(solution)/shard_map/fir/pallas_call | solution.py:167
  2.7 12.8 %all_to_all.10.share_ref = bf16[16,8,640]{2,1,0:T(8,128)(2,1)S(1)} all-to-all(bf16[16,8,640]{2,1,0:T(8,128)(2,1)S(1)} %fir.1), channel_id=1, replica_groups=mesh['range'=2,'far'=2,'near'=8] {'range','near'}, dimensions={0} | all-to-all | bytes 327680 | tf_op jit(solution)/shard_map/all_to_all | solution.py:341
  15.4 2.1 %image.1 = bf16[16,8,512]{2,1,0:T(8,128)(2,1)S(1)} custom-call(bf16[16,8,640]{2,1,0:T(8,128)(2,1)S(1)} %all_to_all.10.share_ref), custom_call_target="tpu_custom_call" | custom-call | tf_op jit(solution)/shard_map/image/pallas_call | solution.py:289
  17.5 11.7 %all_to_all.11.in_ref = bf16[16,8,512]{2,1,0:T(8,128)(2,1)S(1)} all-to-all(bf16[16,8,512]{2,1,0:T(8,128)(2,1)S(1)} %image.1), channel_id=1, replica_groups=mesh['range'=2,'far'=2,'near'=8] {'far','near'}, dimensions={0} | all-to-all | bytes 262144 | tf_op jit(solution)/shard_map/all_to_all | solution.py:352
  29.2 0.8 %turn.1 = (f32[128,128]{1,0:T(8,128)}, f32[128,128]{1,0:T(8,128)}) custom-call(bf16[16,8,512]{2,1,0:T(8,128)(2,1)S(1)} %all_to_all.11.in_ref), custom_call_target="tpu_custom_call" | custom-call | tf_op jit(solution)/shard_map/turn/pallas_call | solution.py:324

commit v5 on v4

--- a/solution.py
+++ b/solution.py
@@ -14,7 +14,7 @@
 LANES = 128
 SUB = 8
 MIB = 1024 * 1024
-FAR = 2
+FAR = 4
 
 
 def round_up(value, unit):

time: 30.2 us -> 31.7 us (1.050)
  blocking collectives: 24.5 us -> 25.5 us
  Pallas kernels: 4.86 us -> 5.29 us
    all_to_all x1, blocking collectives: 11.7 us -> 15.2 us  [shards(): image = lax.all_to_all(image, ('far', 'near'), 0, 0, tiled=True)]
    all_to_all x1, blocking collectives: 12.8 us -> 10.3 us  [shards(): share = lax.all_to_all(share, ('range', 'near'), 0, 0, tiled=True)]
    pallas_call x1, Pallas kernels: 2.07 us -> 2.5 us  [image_share(): pl.pallas_call(functools.partial(image_kernel, bands, scaling, near), out...]
where the time goes in v5:
time: 31.7 us; the launch traced here: 31.4 us
  blocking collectives  25.5 us (80%)
  Pallas kernels  5.29 us (17%)
  between operations  0.65 us (2%)
    all_to_all x1, blocking collectives, shards(): image = lax.all_to_all(image, ('far', 'near'), 0, 0, tiled=True)  15.2 us
    all_to_all x1, blocking collectives, shards(): share = lax.all_to_all(share, ('range', 'near'), 0, 0, tiled=True)  10.3 us
    pallas_call x1, Pallas kernels, image_share(): pl.pallas_call(functools.partial(image_kernel, bands, scaling, near), out...  2.5 us
    pallas_call x1, Pallas kernels, own_share(): pl.pallas_call(functools.partial(fir_kernel, bands, front, stack), out_sh...  2.03 us
    pallas_call x1, Pallas kernels, turned(): pl.pallas_call(functools.partial(turn_kernel, far, stack), out_shape=(out...  0.76 us

profile of v5, /device:TPU:0, one launch (start us, length us, event | category | flops | bytes accessed | tf_op | source)
XLA Modules:
  0.0 31.4 jit_solution(12993174523920469692)
XLA Ops:
  0.6 2.0 %fir.1 = bf16[8,8,1152]{2,1,0:T(8,128)(2,1)S(1)} custom-call(s32[8]{0:T(128)} %offset_hbm.1, s32[8]{0:T(128)} %track_hbm.1, bf16[256,128]{1,0:T(8,128)(2,1)} %bitcast.1, f32[8,32]{1,0:T(8,128)} %sway_hbm.1, f32[8,32]{1,0:T(8,128)} %gain_hbm.1), custom_call_target="tpu_custom_call" | custom-call | tf_op jit(solution)/shard_map/fir/pallas_call | solution.py:167
  2.7 10.3 %all_to_all.10.share_ref = bf16[8,8,1152]{2,1,0:T(8,128)(2,1)S(1)} all-to-all(bf16[8,8,1152]{2,1,0:T(8,128)(2,1)S(1)} %fir.1), channel_id=1, replica_groups=mesh['range'=2,'far'=4,'near'=4] {'range','near'}, dimensions={0} | all-to-all | bytes 294912 | tf_op jit(solution)/shard_map/all_to_all | solution.py:341
  13.0 2.5 %image.1 = bf16[16,8,1024]{2,1,0:T(8,128)(2,1)S(1)} custom-call(bf16[8,8,1152]{2,1,0:T(8,128)(2,1)S(1)} %all_to_all.10.share_ref), custom_call_target="tpu_custom_call" | custom-call | tf_op jit(solution)/shard_map/image/pallas_call | solution.py:289
  15.5 15.2 %all_to_all.11.in_ref = bf16[16,8,1024]{2,1,0:T(8,128)(2,1)S(1)} all-to-all(bf16[16,8,1024]{2,1,0:T(8,128)(2,1)S(1)} %image.1), channel_id=1, replica_groups=mesh['range'=2,'far'=4,'near'=4] {'far','near'}, dimensions={0} | all-to-all | bytes 524288 | tf_op jit(solution)/shard_map/all_to_all | solution.py:352
  30.7 0.8 %turn.1 = (f32[128,128]{1,0:T(8,128)}, f32[128,128]{1,0:T(8,128)}) custom-call(bf16[16,8,1024]{2,1,0:T(8,128)(2,1)S(1)} %all_to_all.11.in_ref), custom_call_target="tpu_custom_call" | custom-call | tf_op jit(solution)/shard_map/turn/pallas_call | solution.py:324

commit v6 on v4

--- a/solution.py
+++ b/solution.py
@@ -92,7 +92,7 @@
 
     sway = lane_row(sway_ref[...], lanes)
     gain = lane_row(gain_ref[...], lanes)
-    amplitude = jnp.sin(math.pi * jnp.minimum(sway, 1.0 - sway)) * gain * (1.0 / math.pi)
+    amplitude = sine_of_pi(jnp.minimum(sway, 1.0 - sway))[0] * gain * (1.0 / math.pi)
     for tile in range(lanes // LANES):
         cols = slice(tile * LANES, (tile + 1) * LANES)
         shift = tap_index.astype(jnp.float32) - (BAND / 2 - 1) - sway[:, cols]
@@ -191,37 +191,54 @@
     )
 
 
-def half_turn_sincos(turns):
-    angle = (turns - jnp.round(turns)) * math.pi
+def sine_of_pi(value):
+    angle = value * math.pi
     square = angle * angle
-    sin_sum, cos_sum = jnp.zeros_like(angle), jnp.zeros_like(angle)
+    sine, cosine = None, None
     for order in range(7, -1, -1):
-        sin_sum = sin_sum * square + (-1.0) ** order / math.factorial(2 * order + 1)
-        cos_sum = cos_sum * square + (-1.0) ** order / math.factorial(2 * order)
-    sine = sin_sum * angle
-    return 2.0 * sine * cos_sum, 1.0 - 2.0 * sine * sine
-
-
-def fill_table(bands, scaling, table_ref):
-    steps, depth, _ = table_ref.shape
+        sign = (-1.0) ** order
+        a, b = sign / math.factorial(2 * order + 1), sign / math.factorial(2 * order)
+        sine = jnp.full_like(angle, a) if sine is None else sine * square + a
+        cosine = jnp.full_like(angle, b) if cosine is None else cosine * square + b
+    return sine * angle, cosine
+
+
+def steer_values(bands, scaling, steps):
     band = lax.axis_index("range").astype(jnp.float32)
     spread = 0.5 * X * (1.0 + (band + 0.5) * (1.0 / bands))
     length = (steps + 1) * LANES
-    pack = 2 * SUB
-    lane = lax.broadcasted_iota(jnp.int32, (pack, length), 1) - (steps // 2 + 1) * LANES
-    row = lax.broadcasted_iota(jnp.int32, (pack, length), 0)
+    lane = lax.broadcasted_iota(jnp.int32, (SUB, length), 1) - (steps // 2 + 1) * LANES
+    row = lax.broadcasted_iota(jnp.int32, (SUB, length), 0)
     twice = (2 * lane - row).astype(jnp.float32)
     square = twice * twice
     weight = jnp.exp(square * (-0.125 * (8.0 / X) ** 2)) * scaling
-    sine, cosine = half_turn_sincos(square * (0.125 / spread))
-    parts = ((weight * cosine).astype(jnp.bfloat16), (weight * sine).astype(jnp.bfloat16))
-    for first in range(0, depth, pack):
-        for i, part in enumerate(parts):
-            moved = pltpu.roll(part, first // 2, 1) if first else part
-            for step in range(steps):
-                table_ref[step, first : first + pack, i * LANES : (i + 1) * LANES] = moved[
-                    :, (step + 1) * LANES : (step + 2) * LANES
-                ]
+    turns = square * (0.125 / spread)
+    sine, cosine = sine_of_pi(turns - jnp.round(turns))
+    parts = (weight * (1.0 - 2.0 * sine * sine), weight * (2.0 * sine * cosine))
+    tiles = []
+    for part in parts:
+        both = jnp.concatenate([part, pltpu.roll(part, SUB // 2, 1)], axis=0)
+        both = both.astype(jnp.bfloat16)
+        tiles.append([both[:, i * LANES : (i + 1) * LANES] for i in range(steps + 1)])
+    return tiles
+
+
+def fill_step(tiles, moved, step, table_ref):
+    depth = table_ref.shape[1]
+    pack = 2 * SUB
+    lane = lax.broadcasted_iota(jnp.int32, (pack, LANES), 1).astype(jnp.bfloat16)
+    for i, part in enumerate(tiles):
+        for first in range(0, depth, pack):
+            by = first // 2
+            if by == 0:
+                value = part[step + 1]
+            else:
+                if step == 0:
+                    moved[i, first] = pltpu.roll(part[0], by, 1)
+                new = pltpu.roll(part[step + 1], by, 1)
+                value = jnp.where(lane < float(by), moved[i, first], new)
+                moved[i, first] = new
+            table_ref[step, first : first + pack, i * LANES : (i + 1) * LANES] = value
 
 
 def image_kernel(bands, scaling, near, share_ref, out_ref, held_ref, table_ref):
@@ -233,11 +250,12 @@
     lanes = (share_ref.shape[2] - LANES) // stack
     tiles = lanes // LANES
     half = held_ref.shape[0] // rows
-    fill_table(bands, scaling, table_ref)
+    steps = table_ref.shape[0]
+    tiles_of, moved, filled = steer_values(bands, scaling, steps), {}, 0
 
     depth_row = lax.broadcasted_iota(jnp.int32, (depth, lanes), 0).astype(jnp.bfloat16)
     one, none = jnp.ones((), jnp.bfloat16), jnp.zeros((), jnp.bfloat16)
-    held = None
+    held, early = None, steps // 2
     for group in range(near):
         share = share_ref[group, :, : stack * lanes].astype(jnp.float32)
         for copy in range(1, copies):
@@ -258,12 +276,18 @@
             spread, hot, (((1,), (1,)), ((), ())), preferred_element_type=jnp.float32
         )
         held = part if held is None else held + part
+        while filled < (group + 1) * early // near:
+            fill_step(tiles_of, moved, filled, table_ref)
+            filled += 1
     held_ref[...] = held.astype(jnp.bfloat16)
 
     blocks = X // LANES
     image = [None] * blocks
     for step in range(-blocks, blocks):
         first, last = max(0, -step), min(blocks, blocks - 1 - step)
+        while filled < min(steps, early + 2 + step + blocks):
+            fill_step(tiles_of, moved, filled, table_ref)
+            filled += 1
         part = jnp.dot(
             held_ref[first * rows : (last + 1) * rows, :],
             table_ref[step + blocks],

time: 30.2 us -> 30.4 us (level)
  no operation moved by 1% of the time
where the time goes in v6:
time: 30.4 us; the launch traced here: 30.2 us
  blocking collectives  24.5 us (81%)
  Pallas kernels  5.06 us (17%)
  between operations  0.64 us (2%)
    all_to_all x1, blocking collectives, shards(): share = lax.all_to_all(share, ('range', 'near'), 0, 0, tiled=True)  12.8 us
    all_to_all x1, blocking collectives, shards(): image = lax.all_to_all(image, ('far', 'near'), 0, 0, tiled=True)  11.7 us
    pallas_call x1, Pallas kernels, image_share(): pl.pallas_call(functools.partial(image_kernel, bands, scaling, near), out...  2.29 us
    pallas_call x1, Pallas kernels, own_share(): pl.pallas_call(functools.partial(fir_kernel, bands, front, stack), out_sh...  2.02 us
    pallas_call x1, Pallas kernels, turned(): pl.pallas_call(functools.partial(turn_kernel, far, stack), out_shape=(out...  0.75 us

profile of v6, /device:TPU:0, one launch (start us, length us, event | category | flops | bytes accessed | tf_op | source)
XLA Modules:
  0.0 30.2 jit_solution(3597266051359774774)
XLA Ops:
  0.6 2.0 %fir.1 = bf16[16,8,640]{2,1,0:T(8,128)(2,1)S(1)} custom-call(s32[8]{0:T(128)} %offset_hbm.1, s32[8]{0:T(128)} %track_hbm.1, bf16[256,128]{1,0:T(8,128)(2,1)} %bitcast.1, f32[8,32]{1,0:T(8,128)} %sway_hbm.1, f32[8,32]{1,0:T(8,128)} %gain_hbm.1), custom_call_target="tpu_custom_call" | custom-call | tf_op jit(solution)/shard_map/fir/pallas_call | solution.py:167
  2.7 12.8 %all_to_all.10.share_ref = bf16[16,8,640]{2,1,0:T(8,128)(2,1)S(1)} all-to-all(bf16[16,8,640]{2,1,0:T(8,128)(2,1)S(1)} %fir.1), channel_id=1, replica_groups=mesh['range'=2,'far'=2,'near'=8] {'range','near'}, dimensions={0} | all-to-all | bytes 327680 | tf_op jit(solution)/shard_map/all_to_all | solution.py:365
  15.4 2.3 %image.1 = bf16[16,8,512]{2,1,0:T(8,128)(2,1)S(1)} custom-call(bf16[16,8,640]{2,1,0:T(8,128)(2,1)S(1)} %all_to_all.10.share_ref), custom_call_target="tpu_custom_call" | custom-call | tf_op jit(solution)/shard_map/image/pallas_call | solution.py:313
  17.7 11.7 %all_to_all.11.in_ref = bf16[16,8,512]{2,1,0:T(8,128)(2,1)S(1)} all-to-all(bf16[16,8,512]{2,1,0:T(8,128)(2,1)S(1)} %image.1), channel_id=1, replica_groups=mesh['range'=2,'far'=2,'near'=8] {'far','near'}, dimensions={0} | all-to-all | bytes 262144 | tf_op jit(solution)/shard_map/all_to_all | solution.py:376
  29.4 0.8 %turn.1 = (f32[128,128]{1,0:T(8,128)}, f32[128,128]{1,0:T(8,128)}) custom-call(bf16[16,8,512]{2,1,0:T(8,128)(2,1)S(1)} %all_to_all.11.in_ref), custom_call_target="tpu_custom_call" | custom-call | tf_op jit(solution)/shard_map/turn/pallas_call | solution.py:348

commit v7 on v4

--- a/solution.py
+++ b/solution.py
@@ -15,6 +15,7 @@
 SUB = 8
 MIB = 1024 * 1024
 FAR = 2
+DEEP = 4
 
 
 def round_up(value, unit):
@@ -49,7 +50,6 @@
     sway_ref,
     gain_ref,
     tap_ref,
-    copies_ref,
     placed_ref,
     sems,
 ):
@@ -79,10 +79,6 @@
     for tile in range(lanes // LANES):
         placed_ref[tile, :front, :] = jnp.zeros((front, LANES), jnp.float32)
         placed_ref[tile, front + ext :, :] = jnp.zeros((tail, LANES), jnp.float32)
-    edge = jnp.zeros((SUB, lanes), jnp.float32)
-    for s in range(SUB):
-        copies_ref[s, 0:SUB, :] = edge
-        copies_ref[s, samples : samples + SUB, :] = edge
     tap_index = lax.broadcasted_iota(jnp.int32, (BAND, LANES), 0)
     window = 0.5 - 0.5 * jnp.cos(2.0 * math.pi * (tap_index.astype(jnp.float32) + 0.5) / BAND)
     window = jnp.where(tap_index % 2 == 0, window, -window)
@@ -92,7 +88,7 @@
 
     sway = lane_row(sway_ref[...], lanes)
     gain = lane_row(gain_ref[...], lanes)
-    amplitude = jnp.sin(math.pi * jnp.minimum(sway, 1.0 - sway)) * gain * (1.0 / math.pi)
+    amplitude = sine_of_pi(jnp.minimum(sway, 1.0 - sway))[0] * gain * (1.0 / math.pi)
     for tile in range(lanes // LANES):
         cols = slice(tile * LANES, (tile + 1) * LANES)
         shift = tap_index.astype(jnp.float32) - (BAND / 2 - 1) - sway[:, cols]
@@ -102,29 +98,32 @@
         tap_ref[:, cols] = scaled * window
 
     echo = jnp.transpose(echo_ref[...].astype(jnp.float32))
-    for s in range(SUB):
-        copies_ref[s, SUB - s : SUB - s + samples, :] = echo
-
-    group = 8
     blocks = ext // SUB
     for tile in range(lanes // LANES):
         cols = slice(tile * LANES, (tile + 1) * LANES)
-        for first in range(0, blocks, group):
-            members = range(first, min(first + group, blocks))
-            total = {j: None for j in members}
-            for k in range(BAND):
-                used = [j for j in members if -SUB < j * SUB - (BAND - 1) + k < samples]
-                if not used:
-                    continue
-                tap = jnp.broadcast_to(tap_ref[k : k + 1, cols], (SUB, LANES))
-                for j in used:
-                    row = j * SUB - (BAND - 1) + k + SUB
-                    s = row % SUB
-                    term = copies_ref[s, row - s : row - s + SUB, cols] * tap
+        edge = jnp.zeros((SUB, LANES), jnp.float32)
+        padded = jnp.concatenate([edge, echo[:, cols], edge], axis=0)
+        height = padded.shape[0]
+        total = [None] * blocks
+        for s in range(SUB):
+            moved = pltpu.roll(padded, height - s, 0) if s else padded
+            first_tap = (BAND - 1 - SUB + s) % SUB
+            taps = {
+                k: jnp.broadcast_to(tap_ref[k : k + 1, cols], (SUB, LANES))
+                for k in range(first_tap, BAND, SUB)
+            }
+            for a in range(0, samples + (SUB if s else 1), SUB):
+                value = moved[a : a + SUB]
+                for k, tap in taps.items():
+                    at = a + s - SUB + BAND - 1 - k
+                    if at % SUB or not 0 <= at < ext:
+                        continue
+                    j = at // SUB
+                    term = value * tap
                     total[j] = term if total[j] is None else total[j] + term
-            for j in members:
-                value = jnp.zeros((SUB, LANES), jnp.float32) if total[j] is None else total[j]
-                placed_ref[tile, front + j * SUB : front + (j + 1) * SUB, :] = value
+        for j in range(blocks):
+            value = jnp.zeros((SUB, LANES), jnp.float32) if total[j] is None else total[j]
+            placed_ref[tile, front + j * SUB : front + (j + 1) * SUB, :] = value
 
     tiles = lanes // LANES
     lane = lax.broadcasted_iota(jnp.int32, (rows, LANES), 1)
@@ -176,7 +175,6 @@
             pltpu.VMEM((pings, channels), jnp.float32),
             pltpu.VMEM((pings, channels), jnp.float32),
             pltpu.VMEM((BAND, lanes), jnp.float32),
-            pltpu.VMEM((SUB, samples + SUB, lanes), jnp.float32),
             pltpu.VMEM((lanes // LANES, height, LANES), jnp.float32),
             pltpu.SemaphoreType.DMA((5,)),
         ],
@@ -191,15 +189,16 @@
     )
 
 
-def half_turn_sincos(turns):
-    angle = (turns - jnp.round(turns)) * math.pi
+def sine_of_pi(value):
+    angle = value * math.pi
     square = angle * angle
-    sin_sum, cos_sum = jnp.zeros_like(angle), jnp.zeros_like(angle)
+    sine, cosine = None, None
     for order in range(7, -1, -1):
-        sin_sum = sin_sum * square + (-1.0) ** order / math.factorial(2 * order + 1)
-        cos_sum = cos_sum * square + (-1.0) ** order / math.factorial(2 * order)
-    sine = sin_sum * angle
-    return 2.0 * sine * cos_sum, 1.0 - 2.0 * sine * sine
+        sign = (-1.0) ** order
+        a, b = sign / math.factorial(2 * order + 1), sign / math.factorial(2 * order)
+        sine = jnp.full_like(angle, a) if sine is None else sine * square + a
+        cosine = jnp.full_like(angle, b) if cosine is None else cosine * square + b
+    return sine * angle, cosine
 
 
 def fill_table(bands, scaling, table_ref):
@@ -208,15 +207,18 @@
     spread = 0.5 * X * (1.0 + (band + 0.5) * (1.0 / bands))
     length = (steps + 1) * LANES
     pack = 2 * SUB
-    lane = lax.broadcasted_iota(jnp.int32, (pack, length), 1) - (steps // 2 + 1) * LANES
-    row = lax.broadcasted_iota(jnp.int32, (pack, length), 0)
+    lane = lax.broadcasted_iota(jnp.int32, (SUB, length), 1) - (steps // 2 + 1) * LANES
+    row = lax.broadcasted_iota(jnp.int32, (SUB, length), 0)
     twice = (2 * lane - row).astype(jnp.float32)
     square = twice * twice
     weight = jnp.exp(square * (-0.125 * (8.0 / X) ** 2)) * scaling
-    sine, cosine = half_turn_sincos(square * (0.125 / spread))
-    parts = ((weight * cosine).astype(jnp.bfloat16), (weight * sine).astype(jnp.bfloat16))
-    for first in range(0, depth, pack):
-        for i, part in enumerate(parts):
+    turns = square * (0.125 / spread)
+    sine, cosine = sine_of_pi(turns - jnp.round(turns))
+    parts = (weight * (1.0 - 2.0 * sine * sine), weight * (2.0 * sine * cosine))
+    for i, part in enumerate(parts):
+        part = jnp.concatenate([part, pltpu.roll(part, SUB // 2, 1)], axis=0)
+        part = part.astype(jnp.bfloat16)
+        for first in range(0, depth, pack):
             moved = pltpu.roll(part, first // 2, 1) if first else part
             for step in range(steps):
                 table_ref[step, first : first + pack, i * LANES : (i + 1) * LANES] = moved[
@@ -224,7 +226,9 @@
                 ]
 
 
-def image_kernel(bands, scaling, near, share_ref, out_ref, held_ref, table_ref):
+def image_kernel(
+    bands, scaling, near, share_ref, out_ref, spread_ref, hot_ref, held_ref, table_ref
+):
     groups = out_ref.shape[0]
     copies = share_ref.shape[0] // near
     depth = 2 * LANES
@@ -232,12 +236,12 @@
     rows = stack * SUB
     lanes = (share_ref.shape[2] - LANES) // stack
     tiles = lanes // LANES
-    half = held_ref.shape[0] // rows
+    half = spread_ref.shape[0] // rows
+    deep = held_ref.shape[1] // depth
     fill_table(bands, scaling, table_ref)
 
     depth_row = lax.broadcasted_iota(jnp.int32, (depth, lanes), 0).astype(jnp.bfloat16)
     one, none = jnp.ones((), jnp.bfloat16), jnp.zeros((), jnp.bfloat16)
-    held = None
     for group in range(near):
         share = share_ref[group, :, : stack * lanes].astype(jnp.float32)
         for copy in range(1, copies):
@@ -250,23 +254,32 @@
         block = jnp.concatenate([place[i : i + 1] for i in range(tiles)], axis=1)
         inside = jnp.concatenate([place[tiles + i : tiles + i + 1] for i in range(tiles)], axis=1)
         block = jnp.broadcast_to(block, share.shape)
-        spread = jnp.concatenate(
-            [jnp.where(block == float(k), share, none) for k in range(half)], axis=0
-        )
-        hot = jnp.where(depth_row == inside, one, none)
-        part = lax.dot_general(
-            spread, hot, (((1,), (1,)), ((), ())), preferred_element_type=jnp.float32
-        )
-        held = part if held is None else held + part
-    held_ref[...] = held.astype(jnp.bfloat16)
+        cols = slice(group * lanes, (group + 1) * lanes)
+        for k in range(half):
+            spread_ref[k * rows : (k + 1) * rows, cols] = jnp.where(block == float(k), share, none)
+        hot_ref[:, cols] = jnp.where(depth_row == inside, one, none)
+    held = lax.dot_general(
+        spread_ref[...],
+        hot_ref[...],
+        (((1,), (1,)), ((), ())),
+        preferred_element_type=jnp.float32,
+    ).astype(jnp.bfloat16)
+    for i in range(deep):
+        cols = slice(i * depth, (i + 1) * depth)
+        if i:
+            held_ref[: i * rows, cols] = jnp.zeros((i * rows, depth), jnp.bfloat16)
+        held_ref[i * rows : (i + half) * rows, cols] = held
+        left = held_ref.shape[0] - (i + half) * rows
+        if left:
+            held_ref[(i + half) * rows :, cols] = jnp.zeros((left, depth), jnp.bfloat16)
 
     blocks = X // LANES
     image = [None] * blocks
-    for step in range(-blocks, blocks):
-        first, last = max(0, -step), min(blocks, blocks - 1 - step)
+    for step in range(-blocks, blocks, deep):
+        first, last = max(0, -step), min(half + deep - 2, blocks - 1 - step)
         part = jnp.dot(
             held_ref[first * rows : (last + 1) * rows, :],
-            table_ref[step + blocks],
+            table_ref[step + blocks : step + blocks + deep].reshape(deep * depth, depth),
             preferred_element_type=jnp.float32,
         )
         for k in range(first, last + 1):
@@ -285,6 +298,7 @@
     groups = far * near
     blocks = X // LANES
     depth = 2 * LANES
+    lanes = (share.shape[2] - LANES) // stack
     vmem = pl.BlockSpec(memory_space=pltpu.VMEM)
     return pl.pallas_call(
         functools.partial(image_kernel, bands, scaling, near),
@@ -294,7 +308,9 @@
         in_specs=[vmem],
         out_specs=vmem,
         scratch_shapes=[
-            pltpu.VMEM(((blocks + 1) * stack * SUB, depth), jnp.bfloat16),
+            pltpu.VMEM(((blocks + 1) * stack * SUB, near * lanes), jnp.bfloat16),
+            pltpu.VMEM((depth, near * lanes), jnp.bfloat16),
+            pltpu.VMEM(((blocks + DEEP) * stack * SUB, DEEP * depth), jnp.bfloat16),
             pltpu.VMEM((2 * blocks, depth, depth), jnp.bfloat16),
         ],
         compiler_params=pltpu.CompilerParams(vmem_limit_bytes=16 * MIB),

time: 30.2 us -> 30.4 us (level)
  no operation moved by 1% of the time
where the time goes in v7:
time: 30.4 us; the launch traced here: 30.2 us
  blocking collectives  24.5 us (81%)
  Pallas kernels  5.07 us (17%)
  between operations  0.65 us (2%)
    all_to_all x1, blocking collectives, shards(): share = lax.all_to_all(share, ('range', 'near'), 0, 0, tiled=True)  12.8 us
    all_to_all x1, blocking collectives, shards(): image = lax.all_to_all(image, ('far', 'near'), 0, 0, tiled=True)  11.7 us
    pallas_call x1, Pallas kernels, image_share(): pl.pallas_call(functools.partial(image_kernel, bands, scaling, near), out...  2.37 us
    pallas_call x1, Pallas kernels, own_share(): pl.pallas_call(functools.partial(fir_kernel, bands, front, stack), out_sh...  1.95 us
    pallas_call x1, Pallas kernels, turned(): pl.pallas_call(functools.partial(turn_kernel, far, stack), out_shape=(out...  0.75 us

profile of v7, /device:TPU:0, one launch (start us, length us, event | category | flops | bytes accessed | tf_op | source)
XLA Modules:
  0.0 30.2 jit_solution(15747206831509656058)
XLA Ops:
  0.6 1.9 %fir.1 = bf16[16,8,640]{2,1,0:T(8,128)(2,1)S(1)} custom-call(s32[8]{0:T(128)} %offset_hbm.1, s32[8]{0:T(128)} %track_hbm.1, bf16[256,128]{1,0:T(8,128)(2,1)} %bitcast.1, f32[8,32]{1,0:T(8,128)} %sway_hbm.1, f32[8,32]{1,0:T(8,128)} %gain_hbm.1), custom_call_target="tpu_custom_call" | custom-call | tf_op jit(solution)/shard_map/fir/pallas_call | solution.py:166
  2.6 12.8 %all_to_all.10.share_ref = bf16[16,8,640]{2,1,0:T(8,128)(2,1)S(1)} all-to-all(bf16[16,8,640]{2,1,0:T(8,128)(2,1)S(1)} %fir.1), channel_id=1, replica_groups=mesh['range'=2,'far'=2,'near'=8] {'range','near'}, dimensions={0} | all-to-all | bytes 327680 | tf_op jit(solution)/shard_map/all_to_all | solution.py:357
  15.4 2.4 %image.1 = bf16[16,8,512]{2,1,0:T(8,128)(2,1)S(1)} custom-call(bf16[16,8,640]{2,1,0:T(8,128)(2,1)S(1)} %all_to_all.10.share_ref), custom_call_target="tpu_custom_call" | custom-call | tf_op jit(solution)/shard_map/image/pallas_call | solution.py:303
  17.7 11.7 %all_to_all.11.in_ref = bf16[16,8,512]{2,1,0:T(8,128)(2,1)S(1)} all-to-all(bf16[16,8,512]{2,1,0:T(8,128)(2,1)S(1)} %image.1), channel_id=1, replica_groups=mesh['range'=2,'far'=2,'near'=8] {'far','near'}, dimensions={0} | all-to-all | bytes 262144 | tf_op jit(solution)/shard_map/all_to_all | solution.py:368
  29.4 0.8 %turn.1 = (f32[128,128]{1,0:T(8,128)}, f32[128,128]{1,0:T(8,128)}) custom-call(bf16[16,8,512]{2,1,0:T(8,128)(2,1)S(1)} %all_to_all.11.in_ref), custom_call_target="tpu_custom_call" | custom-call | tf_op jit(solution)/shard_map/turn/pallas_call | solution.py:340

commit v8 on v7

--- a/solution.py
+++ b/solution.py
@@ -15,7 +15,6 @@
 SUB = 8
 MIB = 1024 * 1024
 FAR = 2
-DEEP = 4
 
 
 def round_up(value, unit):
@@ -226,9 +225,7 @@
                 ]
 
 
-def image_kernel(
-    bands, scaling, near, share_ref, out_ref, spread_ref, hot_ref, held_ref, table_ref
-):
+def image_kernel(bands, scaling, near, share_ref, out_ref, held_ref, table_ref):
     groups = out_ref.shape[0]
     copies = share_ref.shape[0] // near
     depth = 2 * LANES
@@ -236,12 +233,12 @@
     rows = stack * SUB
     lanes = (share_ref.shape[2] - LANES) // stack
     tiles = lanes // LANES
-    half = spread_ref.shape[0] // rows
-    deep = held_ref.shape[1] // depth
+    half = held_ref.shape[0] // rows
     fill_table(bands, scaling, table_ref)
 
     depth_row = lax.broadcasted_iota(jnp.int32, (depth, lanes), 0).astype(jnp.bfloat16)
     one, none = jnp.ones((), jnp.bfloat16), jnp.zeros((), jnp.bfloat16)
+    held = None
     for group in range(near):
         share = share_ref[group, :, : stack * lanes].astype(jnp.float32)
         for copy in range(1, copies):
@@ -254,32 +251,23 @@
         block = jnp.concatenate([place[i : i + 1] for i in range(tiles)], axis=1)
         inside = jnp.concatenate([place[tiles + i : tiles + i + 1] for i in range(tiles)], axis=1)
         block = jnp.broadcast_to(block, share.shape)
-        cols = slice(group * lanes, (group + 1) * lanes)
-        for k in range(half):
-            spread_ref[k * rows : (k + 1) * rows, cols] = jnp.where(block == float(k), share, none)
-        hot_ref[:, cols] = jnp.where(depth_row == inside, one, none)
-    held = lax.dot_general(
-        spread_ref[...],
-        hot_ref[...],
-        (((1,), (1,)), ((), ())),
-        preferred_element_type=jnp.float32,
-    ).astype(jnp.bfloat16)
-    for i in range(deep):
-        cols = slice(i * depth, (i + 1) * depth)
-        if i:
-            held_ref[: i * rows, cols] = jnp.zeros((i * rows, depth), jnp.bfloat16)
-        held_ref[i * rows : (i + half) * rows, cols] = held
-        left = held_ref.shape[0] - (i + half) * rows
-        if left:
-            held_ref[(i + half) * rows :, cols] = jnp.zeros((left, depth), jnp.bfloat16)
+        spread = jnp.concatenate(
+            [jnp.where(block == float(k), share, none) for k in range(half)], axis=0
+        )
+        hot = jnp.where(depth_row == inside, one, none)
+        part = lax.dot_general(
+            spread, hot, (((1,), (1,)), ((), ())), preferred_element_type=jnp.float32
+        )
+        held = part if held is None else held + part
+    held_ref[...] = held.astype(jnp.bfloat16)
 
     blocks = X // LANES
     image = [None] * blocks
-    for step in range(-blocks, blocks, deep):
-        first, last = max(0, -step), min(half + deep - 2, blocks - 1 - step)
+    for step in range(-blocks, blocks):
+        first, last = max(0, -step), min(blocks, blocks - 1 - step)
         part = jnp.dot(
             held_ref[first * rows : (last + 1) * rows, :],
-            table_ref[step + blocks : step + blocks + deep].reshape(deep * depth, depth),
+            table_ref[step + blocks],
             preferred_element_type=jnp.float32,
         )
         for k in range(first, last + 1):
@@ -298,7 +286,6 @@
     groups = far * near
     blocks = X // LANES
     depth = 2 * LANES
-    lanes = (share.shape[2] - LANES) // stack
     vmem = pl.BlockSpec(memory_space=pltpu.VMEM)
     return pl.pallas_call(
         functools.partial(image_kernel, bands, scaling, near),
@@ -308,9 +295,7 @@
         in_specs=[vmem],
         out_specs=vmem,
         scratch_shapes=[
-            pltpu.VMEM(((blocks + 1) * stack * SUB, near * lanes), jnp.bfloat16),
-            pltpu.VMEM((depth, near * lanes), jnp.bfloat16),
-            pltpu.VMEM(((blocks + DEEP) * stack * SUB, DEEP * depth), jnp.bfloat16),
+            pltpu.VMEM(((blocks + 1) * stack * SUB, depth), jnp.bfloat16),
             pltpu.VMEM((2 * blocks, depth, depth), jnp.bfloat16),
         ],
         compiler_params=pltpu.CompilerParams(vmem_limit_bytes=16 * MIB),

time: 30.4 us -> 30.3 us (level)
  no operation moved by 1% of the time
where the time goes in v8:
time: 30.3 us; the launch traced here: 30.1 us
  blocking collectives  24.5 us (81%)
  Pallas kernels  4.97 us (16%)
  between operations  0.64 us (2%)
    all_to_all x1, blocking collectives, shards(): share = lax.all_to_all(share, ('range', 'near'), 0, 0, tiled=True)  12.8 us
    all_to_all x1, blocking collectives, shards(): image = lax.all_to_all(image, ('far', 'near'), 0, 0, tiled=True)  11.7 us
    pallas_call x1, Pallas kernels, image_share(): pl.pallas_call(functools.partial(image_kernel, bands, scaling, near), out...  2.27 us
    pallas_call x1, Pallas kernels, own_share(): pl.pallas_call(functools.partial(fir_kernel, bands, front, stack), out_sh...  1.94 us
    pallas_call x1, Pallas kernels, turned(): pl.pallas_call(functools.partial(turn_kernel, far, stack), out_shape=(out...  0.75 us

profile of v8, /device:TPU:0, one launch (start us, length us, event | category | flops | bytes accessed | tf_op | source)
XLA Modules:
  0.0 30.1 jit_solution(9299968174397130867)
XLA Ops:
  0.6 1.9 %fir.1 = bf16[16,8,640]{2,1,0:T(8,128)(2,1)S(1)} custom-call(s32[8]{0:T(128)} %offset_hbm.1, s32[8]{0:T(128)} %track_hbm.1, bf16[256,128]{1,0:T(8,128)(2,1)} %bitcast.1, f32[8,32]{1,0:T(8,128)} %sway_hbm.1, f32[8,32]{1,0:T(8,128)} %gain_hbm.1), custom_call_target="tpu_custom_call" | custom-call | tf_op jit(solution)/shard_map/fir/pallas_call | solution.py:165
  2.6 12.8 %all_to_all.10.share_ref = bf16[16,8,640]{2,1,0:T(8,128)(2,1)S(1)} all-to-all(bf16[16,8,640]{2,1,0:T(8,128)(2,1)S(1)} %fir.1), channel_id=1, replica_groups=mesh['range'=2,'far'=2,'near'=8] {'range','near'}, dimensions={0} | all-to-all | bytes 327680 | tf_op jit(solution)/shard_map/all_to_all | solution.py:342
  15.4 2.3 %image.1 = bf16[16,8,512]{2,1,0:T(8,128)(2,1)S(1)} custom-call(bf16[16,8,640]{2,1,0:T(8,128)(2,1)S(1)} %all_to_all.10.share_ref), custom_call_target="tpu_custom_call" | custom-call | tf_op jit(solution)/shard_map/image/pallas_call | solution.py:290
  17.6 11.7 %all_to_all.11.in_ref = bf16[16,8,512]{2,1,0:T(8,128)(2,1)S(1)} all-to-all(bf16[16,8,512]{2,1,0:T(8,128)(2,1)S(1)} %image.1), channel_id=1, replica_groups=mesh['range'=2,'far'=2,'near'=8] {'far','near'}, dimensions={0} | all-to-all | bytes 262144 | tf_op jit(solution)/shard_map/all_to_all | solution.py:353
  29.3 0.8 %turn.1 = (f32[128,128]{1,0:T(8,128)}, f32[128,128]{1,0:T(8,128)}) custom-call(bf16[16,8,512]{2,1,0:T(8,128)(2,1)S(1)} %all_to_all.11.in_ref), custom_call_target="tpu_custom_call" | custom-call | tf_op jit(solution)/shard_map/turn/pallas_call | solution.py:325

commit v9 on v8

--- a/solution.py
+++ b/solution.py
@@ -37,12 +37,14 @@
     bands,
     front,
     stack,
+    scaling,
     offset_hbm,
     track_hbm,
     echo_hbm,
     sway_hbm,
     gain_hbm,
     out_ref,
+    table_ref,
     offset_ref,
     track_ref,
     echo_ref,
@@ -82,6 +84,7 @@
     window = 0.5 - 0.5 * jnp.cos(2.0 * math.pi * (tap_index.astype(jnp.float32) + 0.5) / BAND)
     window = jnp.where(tap_index % 2 == 0, window, -window)
 
+    fill_table(bands, scaling, table_ref)
     for fetch in fetches:
         fetch.wait()
 
@@ -155,7 +158,9 @@
     out_ref[:, :, stack * lanes :] = place.astype(jnp.bfloat16)
 
 
-def own_share(echoes, band_offset, track_bin, sway_delay, channel_gain, bands, near):
+def own_share(
+    echoes, band_offset, track_bin, sway_delay, channel_gain, bands, near, scaling
+):
     pings, channels, samples = echoes.shape
     lanes = pings * channels
     chunks = near * min(bands, 3)
@@ -163,10 +168,13 @@
     front = round_up(samples + HALO - BAND + 1, SUB)
     height = round_up(front + 2 * samples + HALO - 1, SUB)
     return pl.pallas_call(
-        functools.partial(fir_kernel, bands, front, stack),
-        out_shape=pltpu.VMEM((chunks, SUB, stack * lanes + LANES), jnp.bfloat16),
+        functools.partial(fir_kernel, bands, front, stack, scaling),
+        out_shape=(
+            pltpu.VMEM((chunks, SUB, stack * lanes + LANES), jnp.bfloat16),
+            pltpu.VMEM((2 * X // LANES, 2 * LANES, 2 * LANES), jnp.bfloat16),
+        ),
         in_specs=[pl.BlockSpec(memory_space=pltpu.HBM)] * 5,
-        out_specs=pl.BlockSpec(memory_space=pltpu.VMEM),
+        out_specs=(pl.BlockSpec(memory_space=pltpu.VMEM),) * 2,
         scratch_shapes=[
             pltpu.SMEM((pings,), jnp.int32),
             pltpu.SMEM((pings,), jnp.int32),
@@ -177,7 +185,7 @@
             pltpu.VMEM((lanes // LANES, height, LANES), jnp.float32),
             pltpu.SemaphoreType.DMA((5,)),
         ],
-        compiler_params=pltpu.CompilerParams(vmem_limit_bytes=8 * MIB),
+        compiler_params=pltpu.CompilerParams(vmem_limit_bytes=16 * MIB),
         name="fir",
     )(
         in_hbm(band_offset),
@@ -206,8 +214,8 @@
     spread = 0.5 * X * (1.0 + (band + 0.5) * (1.0 / bands))
     length = (steps + 1) * LANES
     pack = 2 * SUB
-    lane = lax.broadcasted_iota(jnp.int32, (SUB, length), 1) - (steps // 2 + 1) * LANES
-    row = lax.broadcasted_iota(jnp.int32, (SUB, length), 0)
+    lane = lax.broadcasted_iota(jnp.int32, (pack, length), 1) - (steps // 2 + 1) * LANES
+    row = lax.broadcasted_iota(jnp.int32, (pack, length), 0)
     twice = (2 * lane - row).astype(jnp.float32)
     square = twice * twice
     weight = jnp.exp(square * (-0.125 * (8.0 / X) ** 2)) * scaling
@@ -215,7 +223,6 @@
     sine, cosine = sine_of_pi(turns - jnp.round(turns))
     parts = (weight * (1.0 - 2.0 * sine * sine), weight * (2.0 * sine * cosine))
     for i, part in enumerate(parts):
-        part = jnp.concatenate([part, pltpu.roll(part, SUB // 2, 1)], axis=0)
         part = part.astype(jnp.bfloat16)
         for first in range(0, depth, pack):
             moved = pltpu.roll(part, first // 2, 1) if first else part
@@ -225,7 +232,7 @@
                 ]
 
 
-def image_kernel(bands, scaling, near, share_ref, out_ref, held_ref, table_ref):
+def image_kernel(near, share_ref, table_ref, out_ref, held_ref):
     groups = out_ref.shape[0]
     copies = share_ref.shape[0] // near
     depth = 2 * LANES
@@ -234,7 +241,6 @@
     lanes = (share_ref.shape[2] - LANES) // stack
     tiles = lanes // LANES
     half = held_ref.shape[0] // rows
-    fill_table(bands, scaling, table_ref)
 
     depth_row = lax.broadcasted_iota(jnp.int32, (depth, lanes), 0).astype(jnp.bfloat16)
     one, none = jnp.ones((), jnp.bfloat16), jnp.zeros((), jnp.bfloat16)
@@ -282,25 +288,22 @@
             out_ref[group, :, at : at + depth] = value[i * SUB : (i + 1) * SUB]
 
 
-def image_share(share, bands, scaling, far, near, stack):
+def image_share(share, table, far, near, stack):
     groups = far * near
     blocks = X // LANES
     depth = 2 * LANES
     vmem = pl.BlockSpec(memory_space=pltpu.VMEM)
     return pl.pallas_call(
-        functools.partial(image_kernel, bands, scaling, near),
+        functools.partial(image_kernel, near),
         out_shape=jax.ShapeDtypeStruct(
             (groups, SUB, stack * (blocks // groups) * depth), jnp.bfloat16
         ),
-        in_specs=[vmem],
+        in_specs=[vmem, vmem],
         out_specs=vmem,
-        scratch_shapes=[
-            pltpu.VMEM(((blocks + 1) * stack * SUB, depth), jnp.bfloat16),
-            pltpu.VMEM((2 * blocks, depth, depth), jnp.bfloat16),
-        ],
+        scratch_shapes=[pltpu.VMEM(((blocks + 1) * stack * SUB, depth), jnp.bfloat16)],
         compiler_params=pltpu.CompilerParams(vmem_limit_bytes=16 * MIB),
         name="image",
-    )(share)
+    )(share, pltpu.with_memory_space_constraint(table, pltpu.VMEM))
 
 
 def turn_kernel(far, stack, in_ref, real_ref, imag_ref):
@@ -337,7 +340,9 @@
     bands, far, near = (lax.axis_size(axis) for axis in ("range", "far", "near"))
     stack = samples // near // SUB
     scaling = 1.0 / math.sqrt(far * near * pings * channels)
-    share = own_share(echoes, band_offset, track_bin, sway_delay, channel_gain, bands, near)
+    share, table = own_share(
+        echoes, band_offset, track_bin, sway_delay, channel_gain, bands, near, scaling
+    )
     if bands <= 2:
         share = lax.all_to_all(share, ("range", "near"), 0, 0, tiled=True)
     else:
@@ -349,7 +354,7 @@
         share = jnp.concatenate(
             [lax.all_to_all(a, "near", 0, 0, tiled=True) for a in (own, from_low, from_high)]
         )
-    image = image_share(share, bands, scaling, far, near, stack)
+    image = image_share(share, table, far, near, stack)
     image = lax.all_to_all(image, ("far", "near"), 0, 0, tiled=True)
     return turned(image, X // (far * near), samples, far, stack)
 

time: 30.3 us -> 31.4 us (1.036)
  Pallas kernels: 4.97 us -> 6.05 us
    pallas_call x2, Pallas kernels: 4.21 us -> 5.3 us  [the longest x1 3.43 us: own_share(): pl.pallas_call(functools.partial(fir_kernel, bands, front, stack, scaling...]
where the time goes in v9:
time: 31.4 us; the launch traced here: 31.2 us
  blocking collectives  24.5 us (78%)
  Pallas kernels  6.05 us (19%)
  between operations  0.64 us (2%)
    all_to_all x1, blocking collectives, shards(): share = lax.all_to_all(share, ('range', 'near'), 0, 0, tiled=True)  12.8 us
    all_to_all x1, blocking collectives, shards(): image = lax.all_to_all(image, ('far', 'near'), 0, 0, tiled=True)  11.7 us
    pallas_call x1, Pallas kernels, own_share(): pl.pallas_call(functools.partial(fir_kernel, bands, front, stack, scaling...  3.43 us
    pallas_call x1, Pallas kernels, image_share(): pl.pallas_call(functools.partial(image_kernel, near), out_shape=jax.Shape...  1.86 us
    pallas_call x1, Pallas kernels, turned(): pl.pallas_call(functools.partial(turn_kernel, far, stack), out_shape=(out...  0.75 us

profile of v9, /device:TPU:0, one launch (start us, length us, event | category | flops | bytes accessed | tf_op | source)
XLA Modules:
  0.0 31.2 jit_solution(12392946232449976763)
XLA Ops:
  0.6 3.4 %fir.1 = (bf16[16,8,640]{2,1,0:T(8,128)(2,1)S(1)}, bf16[32,256,256]{2,1,0:T(8,128)(2,1)S(1)}) custom-call(s32[8]{0:T(128)} %offset_hbm.1, s32[8]{0:T(128)} %track_hbm.1, bf16[256,128]{1,0:T(8,128)(2,1)} %bitcast.1, f32[8,32]{1,0:T(8,128)} %sway_hbm.1, f32[8,32]{1,0:T(8,128)} %gain_hbm.1), custom_call_target="tpu_custom_call" | custom-call | tf_op jit(solution)/shard_map/fir/pallas_call | solution.py:170
  4.1 12.8 %all_to_all.10.share_ref = bf16[16,8,640]{2,1,0:T(8,128)(2,1)S(1)} all-to-all(bf16[16,8,640]{2,1,0:T(8,128)(2,1)S(1)} %get-tuple-element.4), channel_id=1, replica_groups=mesh['range'=2,'far'=2,'near'=8] {'range','near'}, dimensions={0} | all-to-all | bytes 327680 | tf_op jit(solution)/shard_map/all_to_all | solution.py:347
  16.8 1.9 %image.1 = bf16[16,8,512]{2,1,0:T(8,128)(2,1)S(1)} custom-call(bf16[16,8,640]{2,1,0:T(8,128)(2,1)S(1)} %all_to_all.10.share_ref, bf16[32,256,256]{2,1,0:T(8,128)(2,1)S(1)} %get-tuple-element.5.table_ref), custom_call_target="tpu_custom_call" | custom-call | tf_op jit(solution)/shard_map/image/pallas_call | solution.py:296
  18.7 11.7 %all_to_all.11.in_ref = bf16[16,8,512]{2,1,0:T(8,128)(2,1)S(1)} all-to-all(bf16[16,8,512]{2,1,0:T(8,128)(2,1)S(1)} %image.1), channel_id=1, replica_groups=mesh['range'=2,'far'=2,'near'=8] {'far','near'}, dimensions={0} | all-to-all | bytes 262144 | tf_op jit(solution)/shard_map/all_to_all | solution.py:358
  30.4 0.8 %turn.1 = (f32[128,128]{1,0:T(8,128)}, f32[128,128]{1,0:T(8,128)}) custom-call(bf16[16,8,512]{2,1,0:T(8,128)(2,1)S(1)} %all_to_all.11.in_ref), custom_call_target="tpu_custom_call" | custom-call | tf_op jit(solution)/shard_map/turn/pallas_call | solution.py:328

commit v10 on v8

--- a/solution.py
+++ b/solution.py
@@ -15,6 +15,7 @@
 SUB = 8
 MIB = 1024 * 1024
 FAR = 2
+SPAN = 64
 
 
 def round_up(value, unit):
@@ -87,7 +88,7 @@
 
     sway = lane_row(sway_ref[...], lanes)
     gain = lane_row(gain_ref[...], lanes)
-    amplitude = sine_of_pi(jnp.minimum(sway, 1.0 - sway))[0] * gain * (1.0 / math.pi)
+    amplitude = sine_of_pi(jnp.minimum(sway, 1.0 - sway)) * gain * (1.0 / math.pi)
     for tile in range(lanes // LANES):
         cols = slice(tile * LANES, (tile + 1) * LANES)
         shift = tap_index.astype(jnp.float32) - (BAND / 2 - 1) - sway[:, cols]
@@ -191,49 +192,60 @@
 def sine_of_pi(value):
     angle = value * math.pi
     square = angle * angle
-    sine, cosine = None, None
+    total = None
     for order in range(7, -1, -1):
-        sign = (-1.0) ** order
-        a, b = sign / math.factorial(2 * order + 1), sign / math.factorial(2 * order)
-        sine = jnp.full_like(angle, a) if sine is None else sine * square + a
-        cosine = jnp.full_like(angle, b) if cosine is None else cosine * square + b
-    return sine * angle, cosine
+        term = (-1.0) ** order / math.factorial(2 * order + 1)
+        total = jnp.full_like(angle, term) if total is None else total * square + term
+    return total * angle
 
 
 def fill_table(bands, scaling, table_ref):
-    steps, depth, _ = table_ref.shape
+    quads = table_ref.shape[0]
+    blocks = 4 * quads
     band = lax.axis_index("range").astype(jnp.float32)
     spread = 0.5 * X * (1.0 + (band + 0.5) * (1.0 / bands))
-    length = (steps + 1) * LANES
     pack = 2 * SUB
-    lane = lax.broadcasted_iota(jnp.int32, (SUB, length), 1) - (steps // 2 + 1) * LANES
-    row = lax.broadcasted_iota(jnp.int32, (SUB, length), 0)
-    twice = (2 * lane - row).astype(jnp.float32)
+    length = (blocks + 1) * LANES
+    lane = lax.broadcasted_iota(jnp.int32, (pack, length), 1)
+    row = lax.broadcasted_iota(jnp.int32, (pack, length), 0)
+    inside = lane % LANES
+    column = (lane // LANES - (blocks // 2 + 1)) * SPAN + inside % SPAN
+    twice = (2 * column - row).astype(jnp.float32)
     square = twice * twice
     weight = jnp.exp(square * (-0.125 * (8.0 / X) ** 2)) * scaling
     turns = square * (0.125 / spread)
-    sine, cosine = sine_of_pi(turns - jnp.round(turns))
-    parts = (weight * (1.0 - 2.0 * sine * sine), weight * (2.0 * sine * cosine))
-    for i, part in enumerate(parts):
-        part = jnp.concatenate([part, pltpu.roll(part, SUB // 2, 1)], axis=0)
-        part = part.astype(jnp.bfloat16)
-        for first in range(0, depth, pack):
-            moved = pltpu.roll(part, first // 2, 1) if first else part
-            for step in range(steps):
-                table_ref[step, first : first + pack, i * LANES : (i + 1) * LANES] = moved[
-                    :, (step + 1) * LANES : (step + 2) * LANES
-                ]
-
-
-def image_kernel(bands, scaling, near, share_ref, out_ref, held_ref, table_ref):
+    turns = turns - jnp.round(turns) - jnp.where(inside < SPAN, 0.0, 0.25)
+    sine = sine_of_pi(turns - jnp.round(turns))
+    values = (weight * (1.0 - 2.0 * sine * sine)).astype(jnp.bfloat16)
+    lane16 = lax.broadcasted_iota(jnp.int32, (pack, LANES), 1) % SPAN
+    lane16 = lane16.astype(jnp.bfloat16)
+    for first in range(0, LANES, pack):
+        by, before = first // 2, None
+        for block in range(blocks + 1):
+            tile = values[:, block * LANES : (block + 1) * LANES]
+            if block:
+                value = tile
+                if by:
+                    value = jnp.where(lane16 < float(by), before, pltpu.roll(tile, by, 1))
+                quad, place = (block - 1) // 4, (block - 1) % 4
+                top = (1 - place % 2) * LANES + first
+                left = place // 2 * LANES
+                table_ref[quad, top : top + pack, left : left + LANES] = value
+            if by:
+                before = pltpu.roll(tile, by + SPAN, 1)
+
+
+def image_kernel(bands, scaling, near, share_ref, out_ref, window_ref, table_ref):
     groups = out_ref.shape[0]
     copies = share_ref.shape[0] // near
     depth = 2 * LANES
-    stack = out_ref.shape[2] // (X // groups // LANES * depth)
+    blocks = X // SPAN
+    share_blocks = blocks // groups
+    stack = out_ref.shape[2] // (share_blocks * LANES)
     rows = stack * SUB
     lanes = (share_ref.shape[2] - LANES) // stack
     tiles = lanes // LANES
-    half = held_ref.shape[0] // rows
+    half = window_ref.shape[0] // rows // 2
     fill_table(bands, scaling, table_ref)
 
     depth_row = lax.broadcasted_iota(jnp.int32, (depth, lanes), 0).astype(jnp.bfloat16)
@@ -259,44 +271,50 @@
             spread, hot, (((1,), (1,)), ((), ())), preferred_element_type=jnp.float32
         )
         held = part if held is None else held + part
-    held_ref[...] = held.astype(jnp.bfloat16)
-
-    blocks = X // LANES
+    held = held.astype(jnp.bfloat16).reshape(half, rows, depth)
+    windows = window_ref.reshape(half, 2, rows, depth)
+    windows[:, 1] = held
+    windows[:, 0, :, LANES:] = held[:, :, :LANES]
+    windows[0, 0, :, :LANES] = jnp.zeros((rows, LANES), jnp.bfloat16)
+    windows[1:, 0, :, :LANES] = held[:-1, :, LANES:]
+
     image = [None] * blocks
-    for step in range(-blocks, blocks):
-        first, last = max(0, -step), min(blocks, blocks - 1 - step)
+    for quad in range(blocks // 2):
+        step = 4 * quad - blocks
+        first, last = max(0, -step - 2), min(2 * half - 1, blocks - 1 - step)
         part = jnp.dot(
-            held_ref[first * rows : (last + 1) * rows, :],
-            table_ref[step + blocks],
+            window_ref[first * rows : (last + 1) * rows, :],
+            table_ref[quad],
             preferred_element_type=jnp.float32,
         )
         for k in range(first, last + 1):
-            term = part[(k - first) * rows : (k - first + 1) * rows]
-            image[k + step] = term if image[k + step] is None else image[k + step] + term
-    share_rows = blocks // groups
+            for block, left in ((k + step, 0), (k + step + 2, LANES)):
+                if not 0 <= block < blocks:
+                    continue
+                term = part[(k - first) * rows : (k - first + 1) * rows, left : left + LANES]
+                image[block] = term if image[block] is None else image[block] + term
     for block in range(blocks):
-        group, within = block // share_rows, block % share_rows
+        group, within = block // share_blocks, block % share_blocks
         value = image[block].astype(jnp.bfloat16)
         for i in range(stack):
-            at = (i * share_rows + within) * depth
-            out_ref[group, :, at : at + depth] = value[i * SUB : (i + 1) * SUB]
-
-
-def image_share(share, bands, scaling, far, near, stack):
+            at = (i * share_blocks + within) * LANES
+            out_ref[group, :, at : at + LANES] = value[i * SUB : (i + 1) * SUB]
+
+
+def image_share(share, bands, scaling, far, near, stack, channels):
     groups = far * near
-    blocks = X // LANES
+    blocks = X // SPAN
     depth = 2 * LANES
+    half = -(-(2 * (X - 1) + channels) // depth)
     vmem = pl.BlockSpec(memory_space=pltpu.VMEM)
     return pl.pallas_call(
         functools.partial(image_kernel, bands, scaling, near),
-        out_shape=jax.ShapeDtypeStruct(
-            (groups, SUB, stack * (blocks // groups) * depth), jnp.bfloat16
-        ),
+        out_shape=jax.ShapeDtypeStruct((groups, SUB, stack * (blocks // groups) * LANES), jnp.bfloat16),
         in_specs=[vmem],
         out_specs=vmem,
         scratch_shapes=[
-            pltpu.VMEM(((blocks + 1) * stack * SUB, depth), jnp.bfloat16),
-            pltpu.VMEM((2 * blocks, depth, depth), jnp.bfloat16),
+            pltpu.VMEM((2 * half * stack * SUB, depth), jnp.bfloat16),
+            pltpu.VMEM((blocks // 2, depth, depth), jnp.bfloat16),
         ],
         compiler_params=pltpu.CompilerParams(vmem_limit_bytes=16 * MIB),
         name="image",
@@ -312,11 +330,11 @@
     part = width // stack
     whole = jnp.stack([whole[:, :, i * part : (i + 1) * part] for i in range(stack)], axis=1)
     whole = whole.reshape(near * stack * sub, part)
-    for block in range(part // (2 * LANES)):
-        rows = slice(block * LANES, (block + 1) * LANES)
-        at = block * 2 * LANES
-        real_ref[rows, :] = jnp.transpose(whole[:, at : at + LANES])
-        imag_ref[rows, :] = jnp.transpose(whole[:, at + LANES : at + 2 * LANES])
+    for block in range(part // LANES):
+        rows = slice(block * SPAN, (block + 1) * SPAN)
+        both = jnp.transpose(whole[:, block * LANES : (block + 1) * LANES])
+        real_ref[rows, :] = both[:SPAN]
+        imag_ref[rows, :] = both[SPAN:]
 
 
 def turned(image, rows, samples, far, stack):
@@ -349,7 +367,7 @@
         share = jnp.concatenate(
             [lax.all_to_all(a, "near", 0, 0, tiled=True) for a in (own, from_low, from_high)]
         )
-    image = image_share(share, bands, scaling, far, near, stack)
+    image = image_share(share, bands, scaling, far, near, stack, channels)
     image = lax.all_to_all(image, ("far", "near"), 0, 0, tiled=True)
     return turned(image, X // (far * near), samples, far, stack)
 

time: 30.3 us -> 30.1 us (level)
  no operation moved by 1% of the time
where the time goes in v10:
time: 30.1 us; the launch traced here: 29.8 us
  blocking collectives  24.5 us (81%)
  Pallas kernels  4.72 us (16%)
  between operations  0.64 us (2%)
    all_to_all x1, blocking collectives, shards(): share = lax.all_to_all(share, ('range', 'near'), 0, 0, tiled=True)  12.8 us
    all_to_all x1, blocking collectives, shards(): image = lax.all_to_all(image, ('far', 'near'), 0, 0, tiled=True)  11.7 us
    pallas_call x1, Pallas kernels, image_share(): pl.pallas_call(functools.partial(image_kernel, bands, scaling, near), out...  2.04 us
    pallas_call x1, Pallas kernels, own_share(): pl.pallas_call(functools.partial(fir_kernel, bands, front, stack), out_sh...  1.94 us
    pallas_call x1, Pallas kernels, turned(): pl.pallas_call(functools.partial(turn_kernel, far, stack), out_shape=(out...  0.74 us

profile of v10, /device:TPU:0, one launch (start us, length us, event | category | flops | bytes accessed | tf_op | source)
XLA Modules:
  0.0 29.8 jit_solution(14533266612287206668)
XLA Ops:
  0.6 1.9 %fir.1 = bf16[16,8,640]{2,1,0:T(8,128)(2,1)S(1)} custom-call(s32[8]{0:T(128)} %offset_hbm.1, s32[8]{0:T(128)} %track_hbm.1, bf16[256,128]{1,0:T(8,128)(2,1)} %bitcast.1, f32[8,32]{1,0:T(8,128)} %sway_hbm.1, f32[8,32]{1,0:T(8,128)} %gain_hbm.1), custom_call_target="tpu_custom_call" | custom-call | tf_op jit(solution)/shard_map/fir/pallas_call | solution.py:166
  2.6 12.8 %all_to_all.10.share_ref = bf16[16,8,640]{2,1,0:T(8,128)(2,1)S(1)} all-to-all(bf16[16,8,640]{2,1,0:T(8,128)(2,1)S(1)} %fir.1), channel_id=1, replica_groups=mesh['range'=2,'far'=2,'near'=8] {'range','near'}, dimensions={0} | all-to-all | bytes 327680 | tf_op jit(solution)/shard_map/all_to_all | solution.py:360
  15.3 2.0 %image.1 = bf16[16,8,512]{2,1,0:T(8,128)(2,1)S(1)} custom-call(bf16[16,8,640]{2,1,0:T(8,128)(2,1)S(1)} %all_to_all.10.share_ref), custom_call_target="tpu_custom_call" | custom-call | tf_op jit(solution)/shard_map/image/pallas_call | solution.py:310
  17.4 11.7 %all_to_all.11.in_ref = bf16[16,8,512]{2,1,0:T(8,128)(2,1)S(1)} all-to-all(bf16[16,8,512]{2,1,0:T(8,128)(2,1)S(1)} %image.1), channel_id=1, replica_groups=mesh['range'=2,'far'=2,'near'=8] {'far','near'}, dimensions={0} | all-to-all | bytes 262144 | tf_op jit(solution)/shard_map/all_to_all | solution.py:371
  29.1 0.7 %turn.1 = (f32[128,128]{1,0:T(8,128)}, f32[128,128]{1,0:T(8,128)}) custom-call(bf16[16,8,512]{2,1,0:T(8,128)(2,1)S(1)} %all_to_all.11.in_ref), custom_call_target="tpu_custom_call" | custom-call | tf_op jit(solution)/shard_map/turn/pallas_call | solution.py:343

commit v11 on v10

--- a/solution.py
+++ b/solution.py
@@ -125,12 +125,8 @@
             value = jnp.zeros((SUB, LANES), jnp.float32) if total[j] is None else total[j]
             placed_ref[tile, front + j * SUB : front + (j + 1) * SUB, :] = value
 
-    tiles = lanes // LANES
     lane = lax.broadcasted_iota(jnp.int32, (rows, LANES), 1)
-    where_row = lax.broadcasted_iota(jnp.int32, (SUB, LANES), 0)
-    place = jnp.zeros((SUB, LANES), jnp.float32)
-    for tile in range(tiles):
-        cols = slice(tile * LANES, (tile + 1) * LANES)
+    for tile in range(lanes // LANES):
         value = None
         for ping in range(pings):
             low, high = ping * channels - tile * LANES, (ping + 1) * channels - tile * LANES
@@ -138,22 +134,22 @@
                 continue
             start = base + offset_ref[ping] + (front + BAND - 1)
             moved = placed_ref[tile, pl.ds(start, rows), :]
-            at = lane[:SUB] + (2 * track_ref[ping] - low)
-            if value is None:
-                value, meets = moved, at
-            else:
-                value = jnp.where(lane >= low, moved, value)
-                meets = jnp.where(lane[:SUB] >= low, at, meets)
+            value = moved if value is None else jnp.where(lane >= low, moved, value)
         value = value.astype(jnp.bfloat16).reshape(chunks, stack, SUB, LANES)
         for more in range(stack):
             at = more * lanes + tile * LANES
             out_ref[:, :, at : at + LANES] = value[:, more]
-        block = (meets // (2 * LANES)).astype(jnp.float32)
-        inside = (meets % (2 * LANES)).astype(jnp.float32)
-        place = jnp.where(where_row == tile, block, place)
-        place = jnp.where(where_row == tiles + tile, inside, place)
-    place = jnp.broadcast_to(place[None], (chunks, SUB, LANES))
-    out_ref[:, :, stack * lanes :] = place.astype(jnp.bfloat16)
+
+    row = lax.broadcasted_iota(jnp.int32, (SUB, LANES), 0)
+    for first in range(0, pings, SUB):
+        coded = jnp.zeros((SUB, LANES), jnp.int32)
+        for ping in range(first, min(first + SUB, pings)):
+            track = track_ref[ping]
+            code = (LANES + (track & (LANES - 1))) << (track >> (LANES.bit_length() - 1))
+            coded = jnp.where(row == ping - first, code, coded)
+        coded = jnp.broadcast_to(coded.astype(jnp.float32)[None], (chunks, SUB, LANES))
+        at = stack * lanes + first // SUB * LANES
+        out_ref[:, :, at : at + LANES] = coded.astype(jnp.bfloat16)
 
 
 def own_share(echoes, band_offset, track_bin, sway_delay, channel_gain, bands, near):
@@ -161,11 +157,12 @@
     lanes = pings * channels
     chunks = near * min(bands, 3)
     stack = samples // near // SUB
+    extra = round_up(pings, SUB) // SUB * LANES
     front = round_up(samples + HALO - BAND + 1, SUB)
     height = round_up(front + 2 * samples + HALO - 1, SUB)
     return pl.pallas_call(
         functools.partial(fir_kernel, bands, front, stack),
-        out_shape=pltpu.VMEM((chunks, SUB, stack * lanes + LANES), jnp.bfloat16),
+        out_shape=pltpu.VMEM((chunks, SUB, stack * lanes + extra), jnp.bfloat16),
         in_specs=[pl.BlockSpec(memory_space=pltpu.HBM)] * 5,
         out_specs=pl.BlockSpec(memory_space=pltpu.VMEM),
         scratch_shapes=[
@@ -235,7 +232,9 @@
                 before = pltpu.roll(tile, by + SPAN, 1)
 
 
-def image_kernel(bands, scaling, near, share_ref, out_ref, window_ref, table_ref):
+def image_kernel(
+    bands, scaling, near, pings, channels, share_ref, out_ref, window_ref, table_ref
+):
     groups = out_ref.shape[0]
     copies = share_ref.shape[0] // near
     depth = 2 * LANES
@@ -243,13 +242,16 @@
     share_blocks = blocks // groups
     stack = out_ref.shape[2] // (share_blocks * LANES)
     rows = stack * SUB
-    lanes = (share_ref.shape[2] - LANES) // stack
-    tiles = lanes // LANES
+    lanes = pings * channels
     half = window_ref.shape[0] // rows // 2
     fill_table(bands, scaling, table_ref)
 
-    depth_row = lax.broadcasted_iota(jnp.int32, (depth, lanes), 0).astype(jnp.bfloat16)
     one, none = jnp.ones((), jnp.bfloat16), jnp.zeros((), jnp.bfloat16)
+    column = lax.broadcasted_iota(jnp.int32, (channels, depth), 1)
+    column = (column - lax.broadcasted_iota(jnp.int32, (channels, depth), 0)) & (depth - 1)
+    column = column.astype(jnp.float32).astype(jnp.bfloat16)
+    lane = lax.broadcasted_iota(jnp.int32, (SUB, LANES), 1)
+    channel = (lane % channels).astype(jnp.float32)
     held = None
     for group in range(near):
         share = share_ref[group, :, : stack * lanes].astype(jnp.float32)
@@ -259,16 +261,43 @@
         share = jnp.concatenate(
             [share[:, i * lanes : (i + 1) * lanes] for i in range(stack)], axis=0
         ).astype(jnp.bfloat16)
-        place = share_ref[group, :, stack * lanes :]
-        block = jnp.concatenate([place[i : i + 1] for i in range(tiles)], axis=1)
-        inside = jnp.concatenate([place[tiles + i : tiles + i + 1] for i in range(tiles)], axis=1)
-        block = jnp.broadcast_to(block, share.shape)
+        hot, block = [], [None] * (lanes // LANES)
+        for first in range(0, pings, SUB):
+            at = stack * lanes + first // SUB * LANES
+            code = share_ref[group, :, at : at + LANES].astype(jnp.float32)
+            whole = jnp.zeros_like(code)
+            for power in (8, 4, 2, 1):
+                big = code >= float(LANES << power)
+                code = jnp.where(big, code * 0.5**power, code)
+                whole = jnp.where(big, whole + float(power), whole)
+            inside = 2.0 * (code - float(LANES))
+            whole = jnp.where(inside + channel >= float(depth), whole + 1.0, whole)
+            for ping in range(first, min(first + SUB, pings)):
+                own = ping - first
+                meets = jnp.broadcast_to(inside[own : own + 1], (channels, LANES))
+                meets = meets.astype(jnp.bfloat16)
+                hot.append(
+                    jnp.concatenate(
+                        [
+                            jnp.where(column[:, i : i + LANES] == meets, one, none)
+                            for i in range(0, depth, LANES)
+                        ],
+                        axis=1,
+                    )
+                )
+                tile, low = ping * channels // LANES, ping * channels % LANES
+                one_block = jnp.broadcast_to(whole[own : own + 1], (rows, LANES))
+                if block[tile] is None:
+                    block[tile] = one_block
+                else:
+                    at_lane = lax.broadcasted_iota(jnp.int32, (rows, LANES), 1)
+                    block[tile] = jnp.where(at_lane >= low, one_block, block[tile])
+        block = jnp.concatenate(block, axis=1).astype(jnp.bfloat16)
         spread = jnp.concatenate(
             [jnp.where(block == float(k), share, none) for k in range(half)], axis=0
         )
-        hot = jnp.where(depth_row == inside, one, none)
-        part = lax.dot_general(
-            spread, hot, (((1,), (1,)), ((), ())), preferred_element_type=jnp.float32
+        part = jnp.dot(
+            spread, jnp.concatenate(hot, axis=0), preferred_element_type=jnp.float32
         )
         held = part if held is None else held + part
     held = held.astype(jnp.bfloat16).reshape(half, rows, depth)
@@ -301,14 +330,14 @@
             out_ref[group, :, at : at + LANES] = value[i * SUB : (i + 1) * SUB]
 
 
-def image_share(share, bands, scaling, far, near, stack, channels):
+def image_share(share, bands, scaling, far, near, stack, pings, channels):
     groups = far * near
     blocks = X // SPAN
     depth = 2 * LANES
     half = -(-(2 * (X - 1) + channels) // depth)
     vmem = pl.BlockSpec(memory_space=pltpu.VMEM)
     return pl.pallas_call(
-        functools.partial(image_kernel, bands, scaling, near),
+        functools.partial(image_kernel, bands, scaling, near, pings, channels),
         out_shape=jax.ShapeDtypeStruct((groups, SUB, stack * (blocks // groups) * LANES), jnp.bfloat16),
         in_specs=[vmem],
         out_specs=vmem,
@@ -367,7 +396,7 @@
         share = jnp.concatenate(
             [lax.all_to_all(a, "near", 0, 0, tiled=True) for a in (own, from_low, from_high)]
         )
-    image = image_share(share, bands, scaling, far, near, stack, channels)
+    image = image_share(share, bands, scaling, far, near, stack, pings, channels)
     image = lax.all_to_all(image, ("far", "near"), 0, 0, tiled=True)
     return turned(image, X // (far * near), samples, far, stack)
 

time: 30.1 us -> 30 us (level)
  no operation moved by 1% of the time
where the time goes in v11:
time: 30 us; the launch traced here: 29.8 us
  blocking collectives  24.5 us (82%)
  Pallas kernels  4.64 us (15%)
  between operations  0.64 us (2%)
    all_to_all x1, blocking collectives, shards(): share = lax.all_to_all(share, ('range', 'near'), 0, 0, tiled=True)  12.8 us
    all_to_all x1, blocking collectives, shards(): image = lax.all_to_all(image, ('far', 'near'), 0, 0, tiled=True)  11.7 us
    pallas_call x1, Pallas kernels, image_share(): pl.pallas_call(functools.partial(image_kernel, bands, scaling, near, ping...  2.02 us
    pallas_call x1, Pallas kernels, own_share(): pl.pallas_call(functools.partial(fir_kernel, bands, front, stack), out_sh...  1.89 us
    pallas_call x1, Pallas kernels, turned(): pl.pallas_call(functools.partial(turn_kernel, far, stack), out_shape=(out...  0.74 us

profile of v11, /device:TPU:0, one launch (start us, length us, event | category | flops | bytes accessed | tf_op | source)
XLA Modules:
  0.0 29.8 jit_solution(11012393997310601418)
XLA Ops:
  0.6 1.9 %fir.1 = bf16[16,8,640]{2,1,0:T(8,128)(2,1)S(1)} custom-call(s32[8]{0:T(128)} %offset_hbm.1, s32[8]{0:T(128)} %track_hbm.1, bf16[256,128]{1,0:T(8,128)(2,1)} %bitcast.1, f32[8,32]{1,0:T(8,128)} %sway_hbm.1, f32[8,32]{1,0:T(8,128)} %gain_hbm.1), custom_call_target="tpu_custom_call" | custom-call | tf_op jit(solution)/shard_map/fir/pallas_call | solution.py:163
  2.5 12.8 %all_to_all.10.share_ref = bf16[16,8,640]{2,1,0:T(8,128)(2,1)S(1)} all-to-all(bf16[16,8,640]{2,1,0:T(8,128)(2,1)S(1)} %fir.1), channel_id=1, replica_groups=mesh['range'=2,'far'=2,'near'=8] {'range','near'}, dimensions={0} | all-to-all | bytes 327680 | tf_op jit(solution)/shard_map/all_to_all | solution.py:389
  15.3 2.0 %image.1 = bf16[16,8,512]{2,1,0:T(8,128)(2,1)S(1)} custom-call(bf16[16,8,640]{2,1,0:T(8,128)(2,1)S(1)} %all_to_all.10.share_ref), custom_call_target="tpu_custom_call" | custom-call | tf_op jit(solution)/shard_map/image/pallas_call | solution.py:339
  17.3 11.7 %all_to_all.11.in_ref = bf16[16,8,512]{2,1,0:T(8,128)(2,1)S(1)} all-to-all(bf16[16,8,512]{2,1,0:T(8,128)(2,1)S(1)} %image.1), channel_id=1, replica_groups=mesh['range'=2,'far'=2,'near'=8] {'far','near'}, dimensions={0} | all-to-all | bytes 262144 | tf_op jit(solution)/shard_map/all_to_all | solution.py:400
  29.0 0.7 %turn.1 = (f32[128,128]{1,0:T(8,128)}, f32[128,128]{1,0:T(8,128)}) custom-call(bf16[16,8,512]{2,1,0:T(8,128)(2,1)S(1)} %all_to_all.11.in_ref), custom_call_target="tpu_custom_call" | custom-call | tf_op jit(solution)/shard_map/turn/pallas_call | solution.py:372

commit v12 on v11

--- a/solution.py
+++ b/solution.py
@@ -196,44 +196,55 @@
     return total * angle
 
 
-def fill_table(bands, scaling, table_ref):
-    quads = table_ref.shape[0]
-    blocks = 4 * quads
+def fill_table(bands, scaling, line_ref, table_ref):
+    tiles = line_ref.shape[1]
+    pack = 2 * SUB
+    packs = 2 * X // pack
+    turn = LANES // (2 * pack)
+    first_tile = -(packs // 2 // turn) - 1
     band = lax.axis_index("range").astype(jnp.float32)
     spread = 0.5 * X * (1.0 + (band + 0.5) * (1.0 / bands))
-    pack = 2 * SUB
-    length = (blocks + 1) * LANES
-    lane = lax.broadcasted_iota(jnp.int32, (pack, length), 1)
-    row = lax.broadcasted_iota(jnp.int32, (pack, length), 0)
-    inside = lane % LANES
-    column = (lane // LANES - (blocks // 2 + 1)) * SPAN + inside % SPAN
-    twice = (2 * column - row).astype(jnp.float32)
-    square = twice * twice
+    shape = (tiles, LANES)
+    index = lax.broadcasted_iota(jnp.int32, shape, 0) + first_tile
+    index = index * LANES + lax.broadcasted_iota(jnp.int32, shape, 1)
+    index = index.astype(jnp.float32)
+    square = index * index
     weight = jnp.exp(square * (-0.125 * (8.0 / X) ** 2)) * scaling
     turns = square * (0.125 / spread)
-    turns = turns - jnp.round(turns) - jnp.where(inside < SPAN, 0.0, 0.25)
-    sine = sine_of_pi(turns - jnp.round(turns))
-    values = (weight * (1.0 - 2.0 * sine * sine)).astype(jnp.bfloat16)
-    lane16 = lax.broadcasted_iota(jnp.int32, (pack, LANES), 1) % SPAN
+    turns = turns - jnp.round(turns)
+    for part, back in ((0, 0.0), (1, 0.25)):
+        moved = turns - back
+        sine = sine_of_pi(moved - jnp.round(moved))
+        line_ref[part] = weight * (1.0 - 2.0 * sine * sine)
+
+    lane = lax.broadcasted_iota(jnp.int32, (SUB, LANES), 1)
+    row = lax.broadcasted_iota(jnp.int32, (SUB, LANES), 0)
+    lane16 = lax.broadcasted_iota(jnp.int32, (pack, LANES), 1).astype(jnp.float32)
     lane16 = lane16.astype(jnp.bfloat16)
-    for first in range(0, LANES, pack):
-        by, before = first // 2, None
-        for block in range(blocks + 1):
-            tile = values[:, block * LANES : (block + 1) * LANES]
-            if block:
-                value = tile
-                if by:
-                    value = jnp.where(lane16 < float(by), before, pltpu.roll(tile, by, 1))
-                quad, place = (block - 1) // 4, (block - 1) % 4
-                top = (1 - place % 2) * LANES + first
-                left = place // 2 * LANES
-                table_ref[quad, top : top + pack, left : left + LANES] = value
-            if by:
-                before = pltpu.roll(tile, by + SPAN, 1)
+    for part in range(2):
+        before, wide = None, None
+        for tile in range(1 - first_tile + packs // 2 // turn):
+            line = jnp.broadcast_to(line_ref[part, tile : tile + 1, :], (SUB, LANES))
+            now = [
+                pltpu.roll(line, 2 * SUB * i, 1, stride=2, stride_axis=0) for i in range(2)
+            ]
+            if tile:
+                both = [
+                    jnp.where(lane < 2 * (row + SUB * i), before[i], now[i]) for i in range(2)
+                ]
+                both = jnp.concatenate(both, axis=0).astype(jnp.bfloat16)
+                wide_now = [pltpu.roll(both, 2 * pack * i, 1) if i else both for i in range(turn)]
+                whole = -(tile + first_tile)
+                for i in range(turn if wide is not None else 0):
+                    value = jnp.where(lane16 < float(2 * pack * i), wide[i], wide_now[i])
+                    at = (turn * whole + i + packs // 2) * pack
+                    table_ref[part, at : at + pack, :] = value if i else both
+                wide = wide_now
+            before = now
 
 
 def image_kernel(
-    bands, scaling, near, pings, channels, share_ref, out_ref, window_ref, table_ref
+    bands, scaling, near, pings, channels, share_ref, out_ref, window_ref, line_ref, table_ref
 ):
     groups = out_ref.shape[0]
     copies = share_ref.shape[0] // near
@@ -244,7 +255,7 @@
     rows = stack * SUB
     lanes = pings * channels
     half = window_ref.shape[0] // rows // 2
-    fill_table(bands, scaling, table_ref)
+    fill_table(bands, scaling, line_ref, table_ref)
 
     one, none = jnp.ones((), jnp.bfloat16), jnp.zeros((), jnp.bfloat16)
     column = lax.broadcasted_iota(jnp.int32, (channels, depth), 1)
@@ -311,9 +322,17 @@
     for quad in range(blocks // 2):
         step = 4 * quad - blocks
         first, last = max(0, -step - 2), min(2 * half - 1, blocks - 1 - step)
-        part = jnp.dot(
+        right = []
+        for more in (0, 2):
+            at = [(step + more + i + blocks) * SPAN for i in (1, 0)]
+            for half_turn in range(2):
+                right.append(
+                    jnp.concatenate([table_ref[half_turn, i : i + SPAN, :] for i in at], axis=1)
+                )
+        part = lax.dot_general(
             window_ref[first * rows : (last + 1) * rows, :],
-            table_ref[quad],
+            jnp.concatenate(right, axis=0),
+            (((1,), (1,)), ((), ())),
             preferred_element_type=jnp.float32,
         )
         for k in range(first, last + 1):
@@ -343,7 +362,8 @@
         out_specs=vmem,
         scratch_shapes=[
             pltpu.VMEM((2 * half * stack * SUB, depth), jnp.bfloat16),
-            pltpu.VMEM((blocks // 2, depth, depth), jnp.bfloat16),
+            pltpu.VMEM((2, round_up(2 * blocks + 2, SUB), LANES), jnp.float32),
+            pltpu.VMEM((2, 2 * X, LANES), jnp.bfloat16),
         ],
         compiler_params=pltpu.CompilerParams(vmem_limit_bytes=16 * MIB),
         name="image",

time: 30 us -> 30.1 us (level)
  no operation moved by 1% of the time
where the time goes in v12:
time: 30.1 us; the launch traced here: 29.8 us
  blocking collectives  24.5 us (81%)
  Pallas kernels  4.71 us (16%)
  between operations  0.65 us (2%)
    all_to_all x1, blocking collectives, shards(): share = lax.all_to_all(share, ('range', 'near'), 0, 0, tiled=True)  12.8 us
    all_to_all x1, blocking collectives, shards(): image = lax.all_to_all(image, ('far', 'near'), 0, 0, tiled=True)  11.7 us
    pallas_call x1, Pallas kernels, image_share(): pl.pallas_call(functools.partial(image_kernel, bands, scaling, near, ping...  2.09 us
    pallas_call x1, Pallas kernels, own_share(): pl.pallas_call(functools.partial(fir_kernel, bands, front, stack), out_sh...  1.89 us
    pallas_call x1, Pallas kernels, turned(): pl.pallas_call(functools.partial(turn_kernel, far, stack), out_shape=(out...  0.74 us

profile of v12, /device:TPU:0, one launch (start us, length us, event | category | flops | bytes accessed | tf_op | source)
XLA Modules:
  0.0 29.8 jit_solution(17064624602959451720)
XLA Ops:
  0.6 1.9 %fir.1 = bf16[16,8,640]{2,1,0:T(8,128)(2,1)S(1)} custom-call(s32[8]{0:T(128)} %offset_hbm.1, s32[8]{0:T(128)} %track_hbm.1, bf16[256,128]{1,0:T(8,128)(2,1)} %bitcast.1, f32[8,32]{1,0:T(8,128)} %sway_hbm.1, f32[8,32]{1,0:T(8,128)} %gain_hbm.1), custom_call_target="tpu_custom_call" | custom-call | tf_op jit(solution)/shard_map/fir/pallas_call | solution.py:163
  2.5 12.8 %all_to_all.10.share_ref = bf16[16,8,640]{2,1,0:T(8,128)(2,1)S(1)} all-to-all(bf16[16,8,640]{2,1,0:T(8,128)(2,1)S(1)} %fir.1), channel_id=1, replica_groups=mesh['range'=2,'far'=2,'near'=8] {'range','near'}, dimensions={0} | all-to-all | bytes 327680 | tf_op jit(solution)/shard_map/all_to_all | solution.py:409
  15.3 2.1 %image.1 = bf16[16,8,512]{2,1,0:T(8,128)(2,1)S(1)} custom-call(bf16[16,8,640]{2,1,0:T(8,128)(2,1)S(1)} %all_to_all.10.share_ref), custom_call_target="tpu_custom_call" | custom-call | tf_op jit(solution)/shard_map/image/pallas_call | solution.py:358
  17.4 11.7 %all_to_all.11.in_ref = bf16[16,8,512]{2,1,0:T(8,128)(2,1)S(1)} all-to-all(bf16[16,8,512]{2,1,0:T(8,128)(2,1)S(1)} %image.1), channel_id=1, replica_groups=mesh['range'=2,'far'=2,'near'=8] {'far','near'}, dimensions={0} | all-to-all | bytes 262144 | tf_op jit(solution)/shard_map/all_to_all | solution.py:420
  29.1 0.7 %turn.1 = (f32[128,128]{1,0:T(8,128)}, f32[128,128]{1,0:T(8,128)}) custom-call(bf16[16,8,512]{2,1,0:T(8,128)(2,1)S(1)} %all_to_all.11.in_ref), custom_call_target="tpu_custom_call" | custom-call | tf_op jit(solution)/shard_map/turn/pallas_call | solution.py:392

commit v13 on v11

--- a/solution.py
+++ b/solution.py
@@ -20,6 +20,17 @@
 
 def round_up(value, unit):
     return -(-value // unit) * unit
+
+
+def slot_of(chunk, bands, chunks):
+    if bands <= 2:
+        return chunks - 1 - chunk
+    near = chunks // 3
+    return chunk // near * near + near - 1 - chunk % near
+
+
+def backward(size):
+    return [list(range(size))[::-1]]
 
 
 def in_hbm(array):
@@ -136,9 +147,11 @@
             moved = placed_ref[tile, pl.ds(start, rows), :]
             value = moved if value is None else jnp.where(lane >= low, moved, value)
         value = value.astype(jnp.bfloat16).reshape(chunks, stack, SUB, LANES)
-        for more in range(stack):
-            at = more * lanes + tile * LANES
-            out_ref[:, :, at : at + LANES] = value[:, more]
+        for chunk in range(chunks):
+            for more in range(stack):
+                at = more * lanes + tile * LANES
+                to = slot_of(chunk, bands, chunks)
+                out_ref[to, :, at : at + LANES] = value[chunk, more]
 
     row = lax.broadcasted_iota(jnp.int32, (SUB, LANES), 0)
     for first in range(0, pings, SUB):
@@ -327,7 +340,7 @@
         value = image[block].astype(jnp.bfloat16)
         for i in range(stack):
             at = (i * share_blocks + within) * LANES
-            out_ref[group, :, at : at + LANES] = value[i * SUB : (i + 1) * SUB]
+            out_ref[groups - 1 - group, :, at : at + LANES] = value[i * SUB : (i + 1) * SUB]
 
 
 def image_share(share, bands, scaling, far, near, stack, pings, channels):
@@ -357,8 +370,14 @@
     for i in range(1, far):
         whole = whole + in_ref[i * near : (i + 1) * near].astype(jnp.float32)
     part = width // stack
-    whole = jnp.stack([whole[:, :, i * part : (i + 1) * part] for i in range(stack)], axis=1)
-    whole = whole.reshape(near * stack * sub, part)
+    whole = jnp.concatenate(
+        [
+            whole[source, :, i * part : (i + 1) * part]
+            for source in reversed(range(near))
+            for i in range(stack)
+        ],
+        axis=0,
+    )
     for block in range(part // LANES):
         rows = slice(block * SPAN, (block + 1) * SPAN)
         both = jnp.transpose(whole[:, block * LANES : (block + 1) * LANES])
@@ -386,18 +405,27 @@
     scaling = 1.0 / math.sqrt(far * near * pings * channels)
     share = own_share(echoes, band_offset, track_bin, sway_delay, channel_gain, bands, near)
     if bands <= 2:
-        share = lax.all_to_all(share, ("range", "near"), 0, 0, tiled=True)
+        order = backward(bands * near)
+        share = lax.all_to_all(
+            share, ("range", "near"), 0, 0, axis_index_groups=order, tiled=True
+        )
     else:
         low, own, high = jnp.split(share, 3)
         up = [(i, i + 1) for i in range(bands - 1)]
         down = [(target, source) for source, target in up]
         from_low = lax.ppermute(high, "range", up)
         from_high = lax.ppermute(low, "range", down)
+        order = backward(near)
         share = jnp.concatenate(
-            [lax.all_to_all(a, "near", 0, 0, tiled=True) for a in (own, from_low, from_high)]
+            [
+                lax.all_to_all(a, "near", 0, 0, axis_index_groups=order, tiled=True)
+                for a in (own, from_low, from_high)
+            ]
         )
     image = image_share(share, bands, scaling, far, near, stack, pings, channels)
-    image = lax.all_to_all(image, ("far", "near"), 0, 0, tiled=True)
+    image = lax.all_to_all(
+        image, ("far", "near"), 0, 0, axis_index_groups=backward(far * near), tiled=True
+    )
     return turned(image, X // (far * near), samples, far, stack)
 
 

time: 30 us -> 26.4 us (0.88)
  blocking collectives: 24.5 us -> 20.9 us
    all_to_all x2, blocking collectives: 24.5 us -> 20.9 us  [the longest x1 10.6 us: shards(): lax.all_to_all(image, ('far', 'near'), 0, 0, axis_index_groups=backward(f...]
where the time goes in v13:
time: 26.4 us; the launch traced here: 26.2 us
  blocking collectives  20.9 us (79%)
  Pallas kernels  4.64 us (18%)
  between operations  0.64 us (2%)
    all_to_all x1, blocking collectives, shards(): lax.all_to_all(image, ('far', 'near'), 0, 0, axis_index_groups=backward(f...  10.6 us
    all_to_all x1, blocking collectives, shards(): lax.all_to_all(share, ('range', 'near'), 0, 0, axis_index_groups=order, t...  10.3 us
    pallas_call x1, Pallas kernels, image_share(): pl.pallas_call(functools.partial(image_kernel, bands, scaling, near, ping...  2.02 us
    pallas_call x1, Pallas kernels, own_share(): pl.pallas_call(functools.partial(fir_kernel, bands, front, stack), out_sh...  1.88 us
    pallas_call x1, Pallas kernels, turned(): pl.pallas_call(functools.partial(turn_kernel, far, stack), out_shape=(out...  0.74 us

profile of v13, /device:TPU:0, one launch (start us, length us, event | category | flops | bytes accessed | tf_op | source)
XLA Modules:
  0.0 26.2 jit_solution(16641764219810707545)
XLA Ops:
  0.6 1.9 %fir.1 = bf16[16,8,640]{2,1,0:T(8,128)(2,1)S(1)} custom-call(s32[8]{0:T(128)} %offset_hbm.1, s32[8]{0:T(128)} %track_hbm.1, bf16[256,128]{1,0:T(8,128)(2,1)} %bitcast.1, f32[8,32]{1,0:T(8,128)} %sway_hbm.1, f32[8,32]{1,0:T(8,128)} %gain_hbm.1), custom_call_target="tpu_custom_call" | custom-call | tf_op jit(solution)/shard_map/fir/pallas_call | solution.py:176
  2.5 10.3 %all_to_all.10.share_ref = bf16[16,8,640]{2,1,0:T(8,128)(2,1)S(1)} all-to-all(bf16[16,8,640]{2,1,0:T(8,128)(2,1)S(1)} %fir.1), channel_id=1, replica_groups={{23,22,21,20,19,18,17,16,7,6,5,4,3,2,1,0},{31,30,29,28,27,26,25,24,15,1..., dimensions={0} | all-to-all | bytes 327680 | tf_op jit(solution)/shard_map/all_to_all | solution.py:409
  12.8 2.0 %image.1 = bf16[16,8,512]{2,1,0:T(8,128)(2,1)S(1)} custom-call(bf16[16,8,640]{2,1,0:T(8,128)(2,1)S(1)} %all_to_all.10.share_ref), custom_call_target="tpu_custom_call" | custom-call | tf_op jit(solution)/shard_map/image/pallas_call | solution.py:352
  14.9 10.6 %all_to_all.11.in_ref = bf16[16,8,512]{2,1,0:T(8,128)(2,1)S(1)} all-to-all(bf16[16,8,512]{2,1,0:T(8,128)(2,1)S(1)} %image.1), channel_id=1, replica_groups={{15,14,13,12,11,10,9,8,7,6,5,4,3,2,1,0},{31,30,29,28,27,26,25,24,23,22,..., dimensions={0} | all-to-all | bytes 262144 | tf_op jit(solution)/shard_map/all_to_all | solution.py:426
  25.4 0.7 %turn.1 = (f32[128,128]{1,0:T(8,128)}, f32[128,128]{1,0:T(8,128)}) custom-call(bf16[16,8,512]{2,1,0:T(8,128)(2,1)S(1)} %all_to_all.11.in_ref), custom_call_target="tpu_custom_call" | custom-call | tf_op jit(solution)/shard_map/turn/pallas_call | solution.py:391

commit v14 on v13

--- a/solution.py
+++ b/solution.py
@@ -22,15 +22,19 @@
     return -(-value // unit) * unit
 
 
-def slot_of(chunk, bands, chunks):
+def listed(size):
+    return [size - 1, *range(size - 1)]
+
+
+def slots(size):
+    order = listed(size)
+    return [order.index(device) for device in range(size)]
+
+
+def share_slots(bands, near):
     if bands <= 2:
-        return chunks - 1 - chunk
-    near = chunks // 3
-    return chunk // near * near + near - 1 - chunk % near
-
-
-def backward(size):
-    return [list(range(size))[::-1]]
+        return slots(bands * near)
+    return [band * near + slot for band in range(3) for slot in slots(near)]
 
 
 def in_hbm(array):
@@ -147,11 +151,10 @@
             moved = placed_ref[tile, pl.ds(start, rows), :]
             value = moved if value is None else jnp.where(lane >= low, moved, value)
         value = value.astype(jnp.bfloat16).reshape(chunks, stack, SUB, LANES)
-        for chunk in range(chunks):
+        for chunk, slot in enumerate(share_slots(bands, chunks // min(bands, 3))):
             for more in range(stack):
                 at = more * lanes + tile * LANES
-                to = slot_of(chunk, bands, chunks)
-                out_ref[to, :, at : at + LANES] = value[chunk, more]
+                out_ref[slot, :, at : at + LANES] = value[chunk, more]
 
     row = lax.broadcasted_iota(jnp.int32, (SUB, LANES), 0)
     for first in range(0, pings, SUB):
@@ -265,11 +268,11 @@
     column = column.astype(jnp.float32).astype(jnp.bfloat16)
     lane = lax.broadcasted_iota(jnp.int32, (SUB, LANES), 1)
     channel = (lane % channels).astype(jnp.float32)
-    held = None
+    held, come = None, share_slots(bands, near)
     for group in range(near):
-        share = share_ref[group, :, : stack * lanes].astype(jnp.float32)
+        share = share_ref[come[group], :, : stack * lanes].astype(jnp.float32)
         for copy in range(1, copies):
-            more = share_ref[copy * near + group, :, : stack * lanes]
+            more = share_ref[come[copy * near + group], :, : stack * lanes]
             share = share + more.astype(jnp.float32)
         share = jnp.concatenate(
             [share[:, i * lanes : (i + 1) * lanes] for i in range(stack)], axis=0
@@ -277,7 +280,7 @@
         hot, block = [], [None] * (lanes // LANES)
         for first in range(0, pings, SUB):
             at = stack * lanes + first // SUB * LANES
-            code = share_ref[group, :, at : at + LANES].astype(jnp.float32)
+            code = share_ref[come[group], :, at : at + LANES].astype(jnp.float32)
             whole = jnp.zeros_like(code)
             for power in (8, 4, 2, 1):
                 big = code >= float(LANES << power)
@@ -335,12 +338,13 @@
                     continue
                 term = part[(k - first) * rows : (k - first + 1) * rows, left : left + LANES]
                 image[block] = term if image[block] is None else image[block] + term
+    go = slots(groups)
     for block in range(blocks):
         group, within = block // share_blocks, block % share_blocks
         value = image[block].astype(jnp.bfloat16)
         for i in range(stack):
             at = (i * share_blocks + within) * LANES
-            out_ref[groups - 1 - group, :, at : at + LANES] = value[i * SUB : (i + 1) * SUB]
+            out_ref[go[group], :, at : at + LANES] = value[i * SUB : (i + 1) * SUB]
 
 
 def image_share(share, bands, scaling, far, near, stack, pings, channels):
@@ -366,15 +370,17 @@
 def turn_kernel(far, stack, in_ref, real_ref, imag_ref):
     groups, sub, width = in_ref.shape
     near = groups // far
-    whole = in_ref[:near].astype(jnp.float32)
-    for i in range(1, far):
-        whole = whole + in_ref[i * near : (i + 1) * near].astype(jnp.float32)
+    come = slots(groups)
+    whole = []
+    for source in range(near):
+        total = in_ref[come[source]].astype(jnp.float32)
+        for i in range(1, far):
+            total = total + in_ref[come[i * near + source]].astype(jnp.float32)
+        whole.append(total)
     part = width // stack
     whole = jnp.concatenate(
         [
-            whole[source, :, i * part : (i + 1) * part]
-            for source in reversed(range(near))
-            for i in range(stack)
+            total[:, i * part : (i + 1) * part] for total in whole for i in range(stack)
         ],
         axis=0,
     )
@@ -405,7 +411,7 @@
     scaling = 1.0 / math.sqrt(far * near * pings * channels)
     share = own_share(echoes, band_offset, track_bin, sway_delay, channel_gain, bands, near)
     if bands <= 2:
-        order = backward(bands * near)
+        order = [listed(bands * near)]
         share = lax.all_to_all(
             share, ("range", "near"), 0, 0, axis_index_groups=order, tiled=True
         )
@@ -415,7 +421,7 @@
         down = [(target, source) for source, target in up]
         from_low = lax.ppermute(high, "range", up)
         from_high = lax.ppermute(low, "range", down)
-        order = backward(near)
+        order = [listed(near)]
         share = jnp.concatenate(
             [
                 lax.all_to_all(a, "near", 0, 0, axis_index_groups=order, tiled=True)
@@ -424,7 +430,7 @@
         )
     image = image_share(share, bands, scaling, far, near, stack, pings, channels)
     image = lax.all_to_all(
-        image, ("far", "near"), 0, 0, axis_index_groups=backward(far * near), tiled=True
+        image, ("far", "near"), 0, 0, axis_index_groups=[listed(far * near)], tiled=True
     )
     return turned(image, X // (far * near), samples, far, stack)
 

time: 26.4 us -> 26 us (0.985)
  blocking collectives: 20.9 us -> 20.4 us
    all_to_all x1, blocking collectives: 10.6 us -> 10.3 us  [shards(): lax.all_to_all(image, ('far', 'near'), 0, 0, axis_index_groups=[listed(fa...]
where the time goes in v14:
time: 26 us; the launch traced here: 25.7 us
  blocking collectives  20.4 us (78%)
  Pallas kernels  4.65 us (18%)
  between operations  0.64 us (2%)
    all_to_all x1, blocking collectives, shards(): lax.all_to_all(image, ('far', 'near'), 0, 0, axis_index_groups=[listed(fa...  10.3 us
    all_to_all x1, blocking collectives, shards(): lax.all_to_all(share, ('range', 'near'), 0, 0, axis_index_groups=order, t...  10.2 us
    pallas_call x1, Pallas kernels, image_share(): pl.pallas_call(functools.partial(image_kernel, bands, scaling, near, ping...  2.02 us
    pallas_call x1, Pallas kernels, own_share(): pl.pallas_call(functools.partial(fir_kernel, bands, front, stack), out_sh...  1.89 us
    pallas_call x1, Pallas kernels, turned(): pl.pallas_call(functools.partial(turn_kernel, far, stack), out_shape=(out...  0.74 us

profile of v14, /device:TPU:0, one launch (start us, length us, event | category | flops | bytes accessed | tf_op | source)
XLA Modules:
  0.0 25.7 jit_solution(10534575712971855616)
XLA Ops:
  0.6 1.9 %fir.1 = bf16[16,8,640]{2,1,0:T(8,128)(2,1)S(1)} custom-call(s32[8]{0:T(128)} %offset_hbm.1, s32[8]{0:T(128)} %track_hbm.1, bf16[256,128]{1,0:T(8,128)(2,1)} %bitcast.1, f32[8,32]{1,0:T(8,128)} %sway_hbm.1, f32[8,32]{1,0:T(8,128)} %gain_hbm.1), custom_call_target="tpu_custom_call" | custom-call | tf_op jit(solution)/shard_map/fir/pallas_call | solution.py:179
  2.5 10.2 %all_to_all.10.share_ref = bf16[16,8,640]{2,1,0:T(8,128)(2,1)S(1)} all-to-all(bf16[16,8,640]{2,1,0:T(8,128)(2,1)S(1)} %fir.1), channel_id=1, replica_groups={{23,0,1,2,3,4,5,6,7,16,17,18,19,20,21,22},{31,8,9,10,11,12,13,14,15,24,..., dimensions={0} | all-to-all | bytes 327680 | tf_op jit(solution)/shard_map/all_to_all | solution.py:415
  12.7 2.0 %image.1 = bf16[16,8,512]{2,1,0:T(8,128)(2,1)S(1)} custom-call(bf16[16,8,640]{2,1,0:T(8,128)(2,1)S(1)} %all_to_all.10.share_ref), custom_call_target="tpu_custom_call" | custom-call | tf_op jit(solution)/shard_map/image/pallas_call | solution.py:356
  14.7 10.3 %all_to_all.11.in_ref = bf16[16,8,512]{2,1,0:T(8,128)(2,1)S(1)} all-to-all(bf16[16,8,512]{2,1,0:T(8,128)(2,1)S(1)} %image.1), channel_id=1, replica_groups={{15,0,1,2,3,4,5,6,7,8,9,10,11,12,13,14},{31,16,17,18,19,20,21,22,23,24,..., dimensions={0} | all-to-all | bytes 262144 | tf_op jit(solution)/shard_map/all_to_all | solution.py:432
  25.0 0.7 %turn.1 = (f32[128,128]{1,0:T(8,128)}, f32[128,128]{1,0:T(8,128)}) custom-call(bf16[16,8,512]{2,1,0:T(8,128)(2,1)S(1)} %all_to_all.11.in_ref), custom_call_target="tpu_custom_call" | custom-call | tf_op jit(solution)/shard_map/turn/pallas_call | solution.py:397

commit v15 on v14

--- a/solution.py
+++ b/solution.py
@@ -23,7 +23,9 @@
 
 
 def listed(size):
-    return [size - 1, *range(size - 1)]
+    half = size // 2
+    mixed = [device for i in range(half) for device in (i, half + i)] if size % 2 == 0 else range(size)
+    return [size - 1, *(device for device in mixed if device != size - 1)]
 
 
 def slots(size):
@@ -367,7 +369,7 @@
     )(share)
 
 
-def turn_kernel(far, stack, in_ref, real_ref, imag_ref):
+def turn_kernel(far, stack, in_ref, real_hbm, imag_hbm, real_ref, imag_ref, sems):
     groups, sub, width = in_ref.shape
     near = groups // far
     come = slots(groups)
@@ -384,21 +386,33 @@
         ],
         axis=0,
     )
+    copies = []
     for block in range(part // LANES):
-        rows = slice(block * SPAN, (block + 1) * SPAN)
+        rows = pl.ds(block * SPAN, SPAN)
         both = jnp.transpose(whole[:, block * LANES : (block + 1) * LANES])
         real_ref[rows, :] = both[:SPAN]
         imag_ref[rows, :] = both[SPAN:]
+        for i, (held, hbm) in enumerate(((real_ref, real_hbm), (imag_ref, imag_hbm))):
+            copies.append(
+                pltpu.make_async_copy(held.at[rows, :], hbm.at[rows, :], sems.at[block, i])
+            )
+            copies[-1].start()
+    for copy in copies:
+        copy.wait()
 
 
 def turned(image, rows, samples, far, stack):
-    vmem = pl.BlockSpec(memory_space=pltpu.VMEM)
-    out = jax.ShapeDtypeStruct((rows, samples), jnp.float32)
+    hbm = pl.BlockSpec(memory_space=pltpu.HBM)
     return pl.pallas_call(
         functools.partial(turn_kernel, far, stack),
-        out_shape=(out, out),
-        in_specs=[vmem],
-        out_specs=(vmem, vmem),
+        out_shape=(pltpu.HBM((rows, samples), jnp.float32),) * 2,
+        in_specs=[pl.BlockSpec(memory_space=pltpu.VMEM)],
+        out_specs=(hbm, hbm),
+        scratch_shapes=[
+            pltpu.VMEM((rows, samples), jnp.float32),
+            pltpu.VMEM((rows, samples), jnp.float32),
+            pltpu.SemaphoreType.DMA((rows // SPAN, 2)),
+        ],
         compiler_params=pltpu.CompilerParams(vmem_limit_bytes=4 * MIB),
         name="turn",
     )(image)

time: 26 us -> 26.8 us (1.031)
  blocking collectives: 20.4 us -> 21.3 us
    all_to_all x1, blocking collectives: 10.3 us -> 11.1 us  [shards(): lax.all_to_all(image, ('far', 'near'), 0, 0, axis_index_groups=[listed(fa...]
where the time goes in v15:
time: 26.8 us; the launch traced here: 26.6 us
  blocking collectives  21.3 us (79%)
  Pallas kernels  4.68 us (17%)
  between operations  0.64 us (2%)
    all_to_all x1, blocking collectives, shards(): lax.all_to_all(image, ('far', 'near'), 0, 0, axis_index_groups=[listed(fa...  11.1 us
    all_to_all x1, blocking collectives, shards(): lax.all_to_all(share, ('range', 'near'), 0, 0, axis_index_groups=order, t...  10.1 us
    pallas_call x1, Pallas kernels, image_share(): pl.pallas_call(functools.partial(image_kernel, bands, scaling, near, ping...  2.02 us
    pallas_call x1, Pallas kernels, own_share(): pl.pallas_call(functools.partial(fir_kernel, bands, front, stack), out_sh...  1.89 us
    pallas_call x1, Pallas kernels, turned(): pl.pallas_call(functools.partial(turn_kernel, far, stack), out_shape=(plt...  0.77 us

profile of v15, /device:TPU:0, one launch (start us, length us, event | category | flops | bytes accessed | tf_op | source)
XLA Modules:
  0.0 26.6 jit_solution(2461122746601992585)
XLA Ops:
  0.6 1.9 %fir.1 = bf16[16,8,640]{2,1,0:T(8,128)(2,1)S(1)} custom-call(s32[8]{0:T(128)} %offset_hbm.1, s32[8]{0:T(128)} %track_hbm.1, bf16[256,128]{1,0:T(8,128)(2,1)} %bitcast.1, f32[8,32]{1,0:T(8,128)} %sway_hbm.1, f32[8,32]{1,0:T(8,128)} %gain_hbm.1), custom_call_target="tpu_custom_call" | custom-call | tf_op jit(solution)/shard_map/fir/pallas_call | solution.py:181
  2.5 10.1 %all_to_all.10.share_ref = bf16[16,8,640]{2,1,0:T(8,128)(2,1)S(1)} all-to-all(bf16[16,8,640]{2,1,0:T(8,128)(2,1)S(1)} %fir.1), channel_id=1, replica_groups={{23,0,16,1,17,2,18,3,19,4,20,5,21,6,22,7},{31,8,24,9,25,10,26,11,27,12,..., dimensions={0} | all-to-all | bytes 327680 | tf_op jit(solution)/shard_map/all_to_all | solution.py:429
  12.7 2.0 %image.1 = bf16[16,8,512]{2,1,0:T(8,128)(2,1)S(1)} custom-call(bf16[16,8,640]{2,1,0:T(8,128)(2,1)S(1)} %all_to_all.10.share_ref), custom_call_target="tpu_custom_call" | custom-call | tf_op jit(solution)/shard_map/image/pallas_call | solution.py:358
  14.7 11.1 %all_to_all.11.in_ref = bf16[16,8,512]{2,1,0:T(8,128)(2,1)S(1)} all-to-all(bf16[16,8,512]{2,1,0:T(8,128)(2,1)S(1)} %image.1), channel_id=1, replica_groups={{15,0,8,1,9,2,10,3,11,4,12,5,13,6,14,7},{31,16,24,17,25,18,26,19,27,20,..., dimensions={0} | all-to-all | bytes 262144 | tf_op jit(solution)/shard_map/all_to_all | solution.py:446
  25.8 0.8 %turn.1 = (f32[128,128]{1,0:T(8,128)}, f32[128,128]{1,0:T(8,128)}) custom-call(bf16[16,8,512]{2,1,0:T(8,128)(2,1)S(1)} %all_to_all.11.in_ref), custom_call_target="tpu_custom_call" | custom-call | tf_op jit(solution)/shard_map/turn/pallas_call | solution.py:406

commit v16 on v14

--- a/solution.py
+++ b/solution.py
@@ -35,6 +35,12 @@
     if bands <= 2:
         return slots(bands * near)
     return [band * near + slot for band in range(3) for slot in slots(near)]
+
+
+def share_slot(bands, near, place):
+    if bands <= 2:
+        return lax.rem(place + 1, bands * near)
+    return place // near * near + lax.rem(lax.rem(place, near) + 1, near)
 
 
 def in_hbm(array):
@@ -110,21 +116,24 @@
         whole = shift == 0.0
         signed = jnp.where(tap_index % 2 == 0, gain[:, cols], -gain[:, cols])
         scaled = jnp.where(whole, signed, amplitude[:, cols] / jnp.where(whole, 1.0, shift))
-        tap_ref[:, cols] = scaled * window
-
-    echo = jnp.transpose(echo_ref[...].astype(jnp.float32))
+        tap_ref[tile] = scaled * window
+
     blocks = ext // SUB
-    for tile in range(lanes // LANES):
-        cols = slice(tile * LANES, (tile + 1) * LANES)
+    tile_pings = LANES // channels
+    lane = lax.broadcasted_iota(jnp.int32, (rows, LANES), 1)
+    go = share_slots(bands, chunks // min(bands, 3))
+
+    def one_tile(tile, carry):
+        own = echo_ref[pl.ds(pl.multiple_of(tile * LANES, LANES), LANES), :]
         edge = jnp.zeros((SUB, LANES), jnp.float32)
-        padded = jnp.concatenate([edge, echo[:, cols], edge], axis=0)
+        padded = jnp.concatenate([edge, jnp.transpose(own.astype(jnp.float32)), edge], axis=0)
         height = padded.shape[0]
         total = [None] * blocks
         for s in range(SUB):
             moved = pltpu.roll(padded, height - s, 0) if s else padded
             first_tap = (BAND - 1 - SUB + s) % SUB
             taps = {
-                k: jnp.broadcast_to(tap_ref[k : k + 1, cols], (SUB, LANES))
+                k: jnp.broadcast_to(tap_ref[tile, k : k + 1, :], (SUB, LANES))
                 for k in range(first_tap, BAND, SUB)
             }
             for a in range(0, samples + (SUB if s else 1), SUB):
@@ -140,21 +149,19 @@
             value = jnp.zeros((SUB, LANES), jnp.float32) if total[j] is None else total[j]
             placed_ref[tile, front + j * SUB : front + (j + 1) * SUB, :] = value
 
-    lane = lax.broadcasted_iota(jnp.int32, (rows, LANES), 1)
-    for tile in range(lanes // LANES):
         value = None
-        for ping in range(pings):
-            low, high = ping * channels - tile * LANES, (ping + 1) * channels - tile * LANES
-            if high <= 0 or low >= LANES:
-                continue
-            start = base + offset_ref[ping] + (front + BAND - 1)
+        for i in range(tile_pings):
+            start = base + offset_ref[tile * tile_pings + i] + (front + BAND - 1)
             moved = placed_ref[tile, pl.ds(start, rows), :]
-            value = moved if value is None else jnp.where(lane >= low, moved, value)
+            value = moved if value is None else jnp.where(lane >= i * channels, moved, value)
         value = value.astype(jnp.bfloat16).reshape(chunks, stack, SUB, LANES)
-        for chunk, slot in enumerate(share_slots(bands, chunks // min(bands, 3))):
+        for chunk, slot in enumerate(go):
             for more in range(stack):
-                at = more * lanes + tile * LANES
-                out_ref[slot, :, at : at + LANES] = value[chunk, more]
+                at = pl.multiple_of(more * lanes + tile * LANES, LANES)
+                out_ref[slot, :, pl.ds(at, LANES)] = value[chunk, more]
+        return carry
+
+    lax.fori_loop(0, lanes // LANES, one_tile, 0)
 
     row = lax.broadcasted_iota(jnp.int32, (SUB, LANES), 0)
     for first in range(0, pings, SUB):
@@ -187,7 +194,7 @@
             pltpu.VMEM((lanes, samples), jnp.bfloat16),
             pltpu.VMEM((pings, channels), jnp.float32),
             pltpu.VMEM((pings, channels), jnp.float32),
-            pltpu.VMEM((BAND, lanes), jnp.float32),
+            pltpu.VMEM((lanes // LANES, BAND, LANES), jnp.float32),
             pltpu.VMEM((lanes // LANES, height, LANES), jnp.float32),
             pltpu.SemaphoreType.DMA((5,)),
         ],
@@ -249,7 +256,7 @@
 
 
 def image_kernel(
-    bands, scaling, near, pings, channels, share_ref, out_ref, window_ref, table_ref
+    bands, scaling, near, pings, channels, share_ref, out_ref, held_ref, window_ref, table_ref
 ):
     groups = out_ref.shape[0]
     copies = share_ref.shape[0] // near
@@ -268,19 +275,21 @@
     column = column.astype(jnp.float32).astype(jnp.bfloat16)
     lane = lax.broadcasted_iota(jnp.int32, (SUB, LANES), 1)
     channel = (lane % channels).astype(jnp.float32)
-    held, come = None, share_slots(bands, near)
-    for group in range(near):
-        share = share_ref[come[group], :, : stack * lanes].astype(jnp.float32)
-        for copy in range(1, copies):
-            more = share_ref[come[copy * near + group], :, : stack * lanes]
-            share = share + more.astype(jnp.float32)
+    held_ref[...] = jnp.zeros(held_ref.shape, jnp.float32)
+
+    def one_group(group, carry):
+        share = None
+        for copy in range(copies):
+            come = share_slot(bands, near, copy * near + group)
+            more = share_ref[come, :, : stack * lanes].astype(jnp.float32)
+            share = more if share is None else share + more
         share = jnp.concatenate(
             [share[:, i * lanes : (i + 1) * lanes] for i in range(stack)], axis=0
         ).astype(jnp.bfloat16)
         hot, block = [], [None] * (lanes // LANES)
         for first in range(0, pings, SUB):
             at = stack * lanes + first // SUB * LANES
-            code = share_ref[come[group], :, at : at + LANES].astype(jnp.float32)
+            code = share_ref[share_slot(bands, near, group), :, at : at + LANES].astype(jnp.float32)
             whole = jnp.zeros_like(code)
             for power in (8, 4, 2, 1):
                 big = code >= float(LANES << power)
@@ -315,7 +324,11 @@
         part = jnp.dot(
             spread, jnp.concatenate(hot, axis=0), preferred_element_type=jnp.float32
         )
-        held = part if held is None else held + part
+        held_ref[...] += part
+        return carry
+
+    lax.fori_loop(0, near, one_group, 0)
+    held = held_ref[...]
     held = held.astype(jnp.bfloat16).reshape(half, rows, depth)
     windows = window_ref.reshape(half, 2, rows, depth)
     windows[:, 1] = held
@@ -359,6 +372,7 @@
         in_specs=[vmem],
         out_specs=vmem,
         scratch_shapes=[
+            pltpu.VMEM((half * stack * SUB, depth), jnp.float32),
             pltpu.VMEM((2 * half * stack * SUB, depth), jnp.bfloat16),
             pltpu.VMEM((blocks // 2, depth, depth), jnp.bfloat16),
         ],

time: 26 us -> 28.1 us (1.081)
  Pallas kernels: 4.65 us -> 6.75 us
    pallas_call x1, Pallas kernels: 2.02 us -> 4.11 us  [image_share(): pl.pallas_call(functools.partial(image_kernel, bands, scaling, near, ping...]
where the time goes in v16:
time: 28.1 us; the launch traced here: 27.9 us
  blocking collectives  20.5 us (73%)
  Pallas kernels  6.75 us (24%)
  between operations  0.64 us (2%)
    all_to_all x1, blocking collectives, shards(): lax.all_to_all(image, ('far', 'near'), 0, 0, axis_index_groups=[listed(fa...  10.3 us
    all_to_all x1, blocking collectives, shards(): lax.all_to_all(share, ('range', 'near'), 0, 0, axis_index_groups=order, t...  10.1 us
    pallas_call x1, Pallas kernels, image_share(): pl.pallas_call(functools.partial(image_kernel, bands, scaling, near, ping...  4.11 us
    pallas_call x1, Pallas kernels, own_share(): pl.pallas_call(functools.partial(fir_kernel, bands, front, stack), out_sh...  1.91 us
    pallas_call x1, Pallas kernels, turned(): pl.pallas_call(functools.partial(turn_kernel, far, stack), out_shape=(out...  0.74 us

profile of v16, /device:TPU:0, one launch (start us, length us, event | category | flops | bytes accessed | tf_op | source)
XLA Modules:
  0.0 27.9 jit_solution(17561272220696748597)
XLA Ops:
  0.6 1.9 %fir.1 = bf16[16,8,640]{2,1,0:T(8,128)(2,1)S(1)} custom-call(s32[8]{0:T(128)} %offset_hbm.1, s32[8]{0:T(128)} %track_hbm.1, bf16[256,128]{1,0:T(8,128)(2,1)} %bitcast.1, f32[8,32]{1,0:T(8,128)} %sway_hbm.1, f32[8,32]{1,0:T(8,128)} %gain_hbm.1), custom_call_target="tpu_custom_call" | custom-call | tf_op jit(solution)/shard_map/fir/pallas_call | solution.py:186
  2.5 10.1 %all_to_all.10.share_ref = bf16[16,8,640]{2,1,0:T(8,128)(2,1)S(1)} all-to-all(bf16[16,8,640]{2,1,0:T(8,128)(2,1)S(1)} %fir.1), channel_id=1, replica_groups={{23,0,1,2,3,4,5,6,7,16,17,18,19,20,21,22},{31,8,9,10,11,12,13,14,15,24,..., dimensions={0} | all-to-all | bytes 327680 | tf_op jit(solution)/shard_map/all_to_all | solution.py:429
  12.7 4.1 %image.1 = bf16[16,8,512]{2,1,0:T(8,128)(2,1)S(1)} custom-call(bf16[16,8,640]{2,1,0:T(8,128)(2,1)S(1)} %all_to_all.10.share_ref), custom_call_target="tpu_custom_call" | custom-call | tf_op jit(solution)/shard_map/image/pallas_call | solution.py:369
  16.8 10.3 %all_to_all.11.in_ref = bf16[16,8,512]{2,1,0:T(8,128)(2,1)S(1)} all-to-all(bf16[16,8,512]{2,1,0:T(8,128)(2,1)S(1)} %image.1), channel_id=1, replica_groups={{15,0,1,2,3,4,5,6,7,8,9,10,11,12,13,14},{31,16,17,18,19,20,21,22,23,24,..., dimensions={0} | all-to-all | bytes 262144 | tf_op jit(solution)/shard_map/all_to_all | solution.py:446
  27.1 0.7 %turn.1 = (f32[128,128]{1,0:T(8,128)}, f32[128,128]{1,0:T(8,128)}) custom-call(bf16[16,8,512]{2,1,0:T(8,128)(2,1)S(1)} %all_to_all.11.in_ref), custom_call_target="tpu_custom_call" | custom-call | tf_op jit(solution)/shard_map/turn/pallas_call | solution.py:411

commit v17 on v14

--- a/solution.py
+++ b/solution.py
@@ -41,12 +41,16 @@
     return pltpu.with_memory_space_constraint(array, pltpu.HBM)
 
 
-def lane_row(values, lanes):
+def lane_rows(values):
     pings, channels = values.shape
-    spread = jnp.concatenate([values] * pings, axis=1)
-    owner = lax.broadcasted_iota(jnp.int32, (pings, lanes), 1) // channels
-    row = lax.broadcasted_iota(jnp.int32, (pings, lanes), 0)
-    return jnp.sum(jnp.where(owner == row, spread, 0.0), axis=0, keepdims=True)
+    share = LANES // channels
+    wide = jnp.concatenate([values] * share, axis=1)
+    row = lax.broadcasted_iota(jnp.int32, wide.shape, 0)
+    column = lax.broadcasted_iota(jnp.int32, wide.shape, 1) // channels
+    return [
+        jnp.sum(jnp.where(row == column + tile * share, wide, 0.0), axis=0, keepdims=True)
+        for tile in range(pings // share)
+    ]
 
 
 def fir_kernel(
@@ -69,15 +73,16 @@
     sems,
 ):
     pairs = (
-        (echo_hbm, echo_ref),
         (sway_hbm, sway_ref),
         (gain_hbm, gain_ref),
+        (echo_hbm, echo_ref),
         (offset_hbm, offset_ref),
         (track_hbm, track_ref),
     )
     fetches = [pltpu.make_async_copy(a, b, sems.at[i]) for i, (a, b) in enumerate(pairs)]
     for fetch in fetches:
         fetch.start()
+    of_sway, of_gain, of_echo, of_offset, of_track = fetches
     pings, channels = sway_ref.shape
     lanes, samples = echo_ref.shape
     chunks = out_ref.shape[0]
@@ -98,20 +103,19 @@
     window = 0.5 - 0.5 * jnp.cos(2.0 * math.pi * (tap_index.astype(jnp.float32) + 0.5) / BAND)
     window = jnp.where(tap_index % 2 == 0, window, -window)
 
-    for fetch in fetches:
-        fetch.wait()
-
-    sway = lane_row(sway_ref[...], lanes)
-    gain = lane_row(gain_ref[...], lanes)
-    amplitude = sine_of_pi(jnp.minimum(sway, 1.0 - sway)) * gain * (1.0 / math.pi)
-    for tile in range(lanes // LANES):
+    of_sway.wait()
+    of_gain.wait()
+
+    for tile, (sway, gain) in enumerate(zip(lane_rows(sway_ref[...]), lane_rows(gain_ref[...]))):
         cols = slice(tile * LANES, (tile + 1) * LANES)
-        shift = tap_index.astype(jnp.float32) - (BAND / 2 - 1) - sway[:, cols]
+        amplitude = sine_of_pi(jnp.minimum(sway, 1.0 - sway)) * gain * (1.0 / math.pi)
+        shift = tap_index.astype(jnp.float32) - (BAND / 2 - 1) - sway
         whole = shift == 0.0
-        signed = jnp.where(tap_index % 2 == 0, gain[:, cols], -gain[:, cols])
-        scaled = jnp.where(whole, signed, amplitude[:, cols] / jnp.where(whole, 1.0, shift))
+        signed = jnp.where(tap_index % 2 == 0, gain, -gain)
+        scaled = jnp.where(whole, signed, amplitude / jnp.where(whole, 1.0, shift))
         tap_ref[:, cols] = scaled * window
 
+    of_echo.wait()
     echo = jnp.transpose(echo_ref[...].astype(jnp.float32))
     blocks = ext // SUB
     for tile in range(lanes // LANES):
@@ -140,6 +144,7 @@
             value = jnp.zeros((SUB, LANES), jnp.float32) if total[j] is None else total[j]
             placed_ref[tile, front + j * SUB : front + (j + 1) * SUB, :] = value
 
+    of_offset.wait()
     lane = lax.broadcasted_iota(jnp.int32, (rows, LANES), 1)
     for tile in range(lanes // LANES):
         value = None
@@ -156,6 +161,7 @@
                 at = more * lanes + tile * LANES
                 out_ref[slot, :, at : at + LANES] = value[chunk, more]
 
+    of_track.wait()
     row = lax.broadcasted_iota(jnp.int32, (SUB, LANES), 0)
     for first in range(0, pings, SUB):
         coded = jnp.zeros((SUB, LANES), jnp.int32)

time: 26 us -> 26 us (level)
  no operation moved by 1% of the time
where the time goes in v17:
time: 26 us; the launch traced here: 25.8 us
  blocking collectives  20.5 us (79%)
  Pallas kernels  4.68 us (18%)
  between operations  0.64 us (2%)
    all_to_all x1, blocking collectives, shards(): lax.all_to_all(image, ('far', 'near'), 0, 0, axis_index_groups=[listed(fa...  10.3 us
    all_to_all x1, blocking collectives, shards(): lax.all_to_all(share, ('range', 'near'), 0, 0, axis_index_groups=order, t...  10.2 us
    pallas_call x1, Pallas kernels, image_share(): pl.pallas_call(functools.partial(image_kernel, bands, scaling, near, ping...  2.02 us
    pallas_call x1, Pallas kernels, own_share(): pl.pallas_call(functools.partial(fir_kernel, bands, front, stack), out_sh...  1.92 us
    pallas_call x1, Pallas kernels, turned(): pl.pallas_call(functools.partial(turn_kernel, far, stack), out_shape=(out...  0.74 us

profile of v17, /device:TPU:0, one launch (start us, length us, event | category | flops | bytes accessed | tf_op | source)
XLA Modules:
  0.0 25.8 jit_solution(481677807332465858)
XLA Ops:
  0.6 1.9 %fir.1 = bf16[16,8,640]{2,1,0:T(8,128)(2,1)S(1)} custom-call(s32[8]{0:T(128)} %offset_hbm.1, s32[8]{0:T(128)} %track_hbm.1, bf16[256,128]{1,0:T(8,128)(2,1)} %bitcast.1, f32[8,32]{1,0:T(8,128)} %sway_hbm.1, f32[8,32]{1,0:T(8,128)} %gain_hbm.1), custom_call_target="tpu_custom_call" | custom-call | tf_op jit(solution)/shard_map/fir/pallas_call | solution.py:185
  2.6 10.2 %all_to_all.10.share_ref = bf16[16,8,640]{2,1,0:T(8,128)(2,1)S(1)} all-to-all(bf16[16,8,640]{2,1,0:T(8,128)(2,1)S(1)} %fir.1), channel_id=1, replica_groups={{23,0,1,2,3,4,5,6,7,16,17,18,19,20,21,22},{31,8,9,10,11,12,13,14,15,24,..., dimensions={0} | all-to-all | bytes 327680 | tf_op jit(solution)/shard_map/all_to_all | solution.py:421
  12.7 2.0 %image.1 = bf16[16,8,512]{2,1,0:T(8,128)(2,1)S(1)} custom-call(bf16[16,8,640]{2,1,0:T(8,128)(2,1)S(1)} %all_to_all.10.share_ref), custom_call_target="tpu_custom_call" | custom-call | tf_op jit(solution)/shard_map/image/pallas_call | solution.py:362
  14.8 10.3 %all_to_all.11.in_ref = bf16[16,8,512]{2,1,0:T(8,128)(2,1)S(1)} all-to-all(bf16[16,8,512]{2,1,0:T(8,128)(2,1)S(1)} %image.1), channel_id=1, replica_groups={{15,0,1,2,3,4,5,6,7,8,9,10,11,12,13,14},{31,16,17,18,19,20,21,22,23,24,..., dimensions={0} | all-to-all | bytes 262144 | tf_op jit(solution)/shard_map/all_to_all | solution.py:438
  25.0 0.7 %turn.1 = (f32[128,128]{1,0:T(8,128)}, f32[128,128]{1,0:T(8,128)}) custom-call(bf16[16,8,512]{2,1,0:T(8,128)(2,1)S(1)} %all_to_all.11.in_ref), custom_call_target="tpu_custom_call" | custom-call | tf_op jit(solution)/shard_map/turn/pallas_call | solution.py:403

commit v18 on v14

--- a/solution.py
+++ b/solution.py
@@ -52,7 +52,6 @@
 def fir_kernel(
     bands,
     front,
-    stack,
     offset_hbm,
     track_hbm,
     echo_hbm,
@@ -80,8 +79,8 @@
         fetch.start()
     pings, channels = sway_ref.shape
     lanes, samples = echo_ref.shape
-    chunks = out_ref.shape[0]
-    rows = chunks * stack * SUB
+    chunks, depth, _ = out_ref.shape
+    rows = chunks * depth
     if bands == 1:
         base = 0
     elif bands == 2:
@@ -150,11 +149,11 @@
             start = base + offset_ref[ping] + (front + BAND - 1)
             moved = placed_ref[tile, pl.ds(start, rows), :]
             value = moved if value is None else jnp.where(lane >= low, moved, value)
-        value = value.astype(jnp.bfloat16).reshape(chunks, stack, SUB, LANES)
+        value = value.astype(jnp.bfloat16)
         for chunk, slot in enumerate(share_slots(bands, chunks // min(bands, 3))):
-            for more in range(stack):
-                at = more * lanes + tile * LANES
-                out_ref[slot, :, at : at + LANES] = value[chunk, more]
+            out_ref[slot, :, tile * LANES : (tile + 1) * LANES] = value[
+                chunk * depth : (chunk + 1) * depth
+            ]
 
     row = lax.broadcasted_iota(jnp.int32, (SUB, LANES), 0)
     for first in range(0, pings, SUB):
@@ -163,22 +162,23 @@
             track = track_ref[ping]
             code = (LANES + (track & (LANES - 1))) << (track >> (LANES.bit_length() - 1))
             coded = jnp.where(row == ping - first, code, coded)
-        coded = jnp.broadcast_to(coded.astype(jnp.float32)[None], (chunks, SUB, LANES))
-        at = stack * lanes + first // SUB * LANES
-        out_ref[:, :, at : at + LANES] = coded.astype(jnp.bfloat16)
+        coded = jnp.concatenate([coded] * (depth // SUB), axis=0).astype(jnp.float32)
+        coded = coded.astype(jnp.bfloat16)
+        at = lanes + first // SUB * LANES
+        for chunk in range(chunks):
+            out_ref[chunk, :, at : at + LANES] = coded
 
 
 def own_share(echoes, band_offset, track_bin, sway_delay, channel_gain, bands, near):
     pings, channels, samples = echoes.shape
     lanes = pings * channels
     chunks = near * min(bands, 3)
-    stack = samples // near // SUB
     extra = round_up(pings, SUB) // SUB * LANES
     front = round_up(samples + HALO - BAND + 1, SUB)
     height = round_up(front + 2 * samples + HALO - 1, SUB)
     return pl.pallas_call(
-        functools.partial(fir_kernel, bands, front, stack),
-        out_shape=pltpu.VMEM((chunks, SUB, stack * lanes + extra), jnp.bfloat16),
+        functools.partial(fir_kernel, bands, front),
+        out_shape=pltpu.VMEM((chunks, samples // near, lanes + extra), jnp.bfloat16),
         in_specs=[pl.BlockSpec(memory_space=pltpu.HBM)] * 5,
         out_specs=pl.BlockSpec(memory_space=pltpu.VMEM),
         scratch_shapes=[
@@ -256,8 +256,7 @@
     depth = 2 * LANES
     blocks = X // SPAN
     share_blocks = blocks // groups
-    stack = out_ref.shape[2] // (share_blocks * LANES)
-    rows = stack * SUB
+    rows = out_ref.shape[1]
     lanes = pings * channels
     half = window_ref.shape[0] // rows // 2
     fill_table(bands, scaling, table_ref)
@@ -270,17 +269,14 @@
     channel = (lane % channels).astype(jnp.float32)
     held, come = None, share_slots(bands, near)
     for group in range(near):
-        share = share_ref[come[group], :, : stack * lanes].astype(jnp.float32)
+        share = share_ref[come[group], :, :lanes].astype(jnp.float32)
         for copy in range(1, copies):
-            more = share_ref[come[copy * near + group], :, : stack * lanes]
-            share = share + more.astype(jnp.float32)
-        share = jnp.concatenate(
-            [share[:, i * lanes : (i + 1) * lanes] for i in range(stack)], axis=0
-        ).astype(jnp.bfloat16)
+            share = share + share_ref[come[copy * near + group], :, :lanes].astype(jnp.float32)
+        share = share.astype(jnp.bfloat16)
         hot, block = [], [None] * (lanes // LANES)
         for first in range(0, pings, SUB):
-            at = stack * lanes + first // SUB * LANES
-            code = share_ref[come[group], :, at : at + LANES].astype(jnp.float32)
+            at = lanes + first // SUB * LANES
+            code = share_ref[come[group], :, at : at + LANES].astype(jnp.float32)[:SUB]
             whole = jnp.zeros_like(code)
             for power in (8, 4, 2, 1):
                 big = code >= float(LANES << power)
@@ -342,24 +338,23 @@
     for block in range(blocks):
         group, within = block // share_blocks, block % share_blocks
         value = image[block].astype(jnp.bfloat16)
-        for i in range(stack):
-            at = (i * share_blocks + within) * LANES
-            out_ref[go[group], :, at : at + LANES] = value[i * SUB : (i + 1) * SUB]
-
-
-def image_share(share, bands, scaling, far, near, stack, pings, channels):
+        out_ref[go[group], :, within * LANES : (within + 1) * LANES] = value
+
+
+def image_share(share, bands, scaling, far, near, pings, channels):
     groups = far * near
+    rows = share.shape[1]
     blocks = X // SPAN
     depth = 2 * LANES
     half = -(-(2 * (X - 1) + channels) // depth)
     vmem = pl.BlockSpec(memory_space=pltpu.VMEM)
     return pl.pallas_call(
         functools.partial(image_kernel, bands, scaling, near, pings, channels),
-        out_shape=jax.ShapeDtypeStruct((groups, SUB, stack * (blocks // groups) * LANES), jnp.bfloat16),
+        out_shape=jax.ShapeDtypeStruct((groups, rows, blocks // groups * LANES), jnp.bfloat16),
         in_specs=[vmem],
         out_specs=vmem,
         scratch_shapes=[
-            pltpu.VMEM((2 * half * stack * SUB, depth), jnp.bfloat16),
+            pltpu.VMEM((2 * half * rows, depth), jnp.bfloat16),
             pltpu.VMEM((blocks // 2, depth, depth), jnp.bfloat16),
         ],
         compiler_params=pltpu.CompilerParams(vmem_limit_bytes=16 * MIB),
@@ -367,8 +362,8 @@
     )(share)
 
 
-def turn_kernel(far, stack, in_ref, real_ref, imag_ref):
-    groups, sub, width = in_ref.shape
+def turn_kernel(far, in_ref, real_ref, imag_ref):
+    groups, _, width = in_ref.shape
     near = groups // far
     come = slots(groups)
     whole = []
@@ -377,25 +372,19 @@
         for i in range(1, far):
             total = total + in_ref[come[i * near + source]].astype(jnp.float32)
         whole.append(total)
-    part = width // stack
-    whole = jnp.concatenate(
-        [
-            total[:, i * part : (i + 1) * part] for total in whole for i in range(stack)
-        ],
-        axis=0,
-    )
-    for block in range(part // LANES):
+    whole = jnp.concatenate(whole, axis=0)
+    for block in range(width // LANES):
         rows = slice(block * SPAN, (block + 1) * SPAN)
         both = jnp.transpose(whole[:, block * LANES : (block + 1) * LANES])
         real_ref[rows, :] = both[:SPAN]
         imag_ref[rows, :] = both[SPAN:]
 
 
-def turned(image, rows, samples, far, stack):
+def turned(image, rows, samples, far):
     vmem = pl.BlockSpec(memory_space=pltpu.VMEM)
     out = jax.ShapeDtypeStruct((rows, samples), jnp.float32)
     return pl.pallas_call(
-        functools.partial(turn_kernel, far, stack),
+        functools.partial(turn_kernel, far),
         out_shape=(out, out),
         in_specs=[vmem],
         out_specs=(vmem, vmem),
@@ -407,7 +396,6 @@
 def shards(echoes, band_offset, sway_delay, channel_gain, track_bin):
     pings, channels, samples = echoes.shape
     bands, far, near = (lax.axis_size(axis) for axis in ("range", "far", "near"))
-    stack = samples // near // SUB
     scaling = 1.0 / math.sqrt(far * near * pings * channels)
     share = own_share(echoes, band_offset, track_bin, sway_delay, channel_gain, bands, near)
     if bands <= 2:
@@ -428,11 +416,11 @@
                 for a in (own, from_low, from_high)
             ]
         )
-    image = image_share(share, bands, scaling, far, near, stack, pings, channels)
+    image = image_share(share, bands, scaling, far, near, pings, channels)
     image = lax.all_to_all(
         image, ("far", "near"), 0, 0, axis_index_groups=[listed(far * near)], tiled=True
     )
-    return turned(image, X // (far * near), samples, far, stack)
+    return turned(image, X // (far * near), samples, far)
 
 
 def solution(mesh):

time: 26 us -> 26.3 us (1.012)
  blocking collectives: 20.4 us -> 20.8 us
    all_to_all x1, blocking collectives: 10.2 us -> 10.6 us  [shards(): lax.all_to_all(share, ('range', 'near'), 0, 0, axis_index_groups=order, t...]
where the time goes in v18:
time: 26.3 us; the launch traced here: 26.1 us
  blocking collectives  20.8 us (79%)
  Pallas kernels  4.64 us (18%)
  between operations  0.64 us (2%)
    all_to_all x1, blocking collectives, shards(): lax.all_to_all(share, ('range', 'near'), 0, 0, axis_index_groups=order, t...  10.6 us
    all_to_all x1, blocking collectives, shards(): lax.all_to_all(image, ('far', 'near'), 0, 0, axis_index_groups=[listed(fa...  10.2 us
    pallas_call x1, Pallas kernels, image_share(): pl.pallas_call(functools.partial(image_kernel, bands, scaling, near, ping...  2.02 us
    pallas_call x1, Pallas kernels, own_share(): pl.pallas_call(functools.partial(fir_kernel, bands, front), out_shape=plt...  1.88 us
    pallas_call x1, Pallas kernels, turned(): pl.pallas_call(functools.partial(turn_kernel, far), out_shape=(out, out),...  0.74 us

profile of v18, /device:TPU:0, one launch (start us, length us, event | category | flops | bytes accessed | tf_op | source)
XLA Modules:
  0.0 26.1 jit_solution(5094489575537626717)
XLA Ops:
  0.6 1.9 %fir.1 = bf16[16,16,384]{2,1,0:T(8,128)(2,1)S(1)} custom-call(s32[8]{0:T(128)} %offset_hbm.1, s32[8]{0:T(128)} %track_hbm.1, bf16[256,128]{1,0:T(8,128)(2,1)} %bitcast.1, f32[8,32]{1,0:T(8,128)} %sway_hbm.1, f32[8,32]{1,0:T(8,128)} %gain_hbm.1), custom_call_target="tpu_custom_call" | custom-call | tf_op jit(solution)/shard_map/fir/pallas_call | solution.py:179
  2.5 10.6 %all_to_all.10.share_ref = bf16[16,16,384]{2,1,0:T(8,128)(2,1)S(1)} all-to-all(bf16[16,16,384]{2,1,0:T(8,128)(2,1)S(1)} %fir.1), channel_id=1, replica_groups={{23,0,1,2,3,4,5,6,7,16,17,18,19,20,21,22},{31,8,9,10,11,12,13,14,15,24,..., dimensions={0} | all-to-all | bytes 393216 | tf_op jit(solution)/shard_map/all_to_all | solution.py:403
  13.1 2.0 %image.1 = bf16[16,16,256]{2,1,0:T(8,128)(2,1)S(1)} custom-call(bf16[16,16,384]{2,1,0:T(8,128)(2,1)S(1)} %all_to_all.10.share_ref), custom_call_target="tpu_custom_call" | custom-call | tf_op jit(solution)/shard_map/image/pallas_call | solution.py:351
  15.1 10.2 %all_to_all.11.in_ref = bf16[16,16,256]{2,1,0:T(8,128)(2,1)S(1)} all-to-all(bf16[16,16,256]{2,1,0:T(8,128)(2,1)S(1)} %image.1), channel_id=1, replica_groups={{15,0,1,2,3,4,5,6,7,8,9,10,11,12,13,14},{31,16,17,18,19,20,21,22,23,24,..., dimensions={0} | all-to-all | bytes 262144 | tf_op jit(solution)/shard_map/all_to_all | solution.py:420
  25.4 0.7 %turn.1 = (f32[128,128]{1,0:T(8,128)}, f32[128,128]{1,0:T(8,128)}) custom-call(bf16[16,16,256]{2,1,0:T(8,128)(2,1)S(1)} %all_to_all.11.in_ref), custom_call_target="tpu_custom_call" | custom-call | tf_op jit(solution)/shard_map/turn/pallas_call | solution.py:386

commit v19 on v14

--- a/solution.py
+++ b/solution.py
@@ -23,7 +23,7 @@
 
 
 def listed(size):
-    return [size - 1, *range(size - 1)]
+    return [size - 1, *range(size // 2, size - 1), *range(size // 2)]
 
 
 def slots(size):

time: 26 us -> 26.4 us (1.015)
  blocking collectives: 20.4 us -> 20.9 us
    all_to_all x1, blocking collectives: 10.3 us -> 10.7 us  [shards(): lax.all_to_all(image, ('far', 'near'), 0, 0, axis_index_groups=[listed(fa...]
where the time goes in v19:
time: 26.4 us; the launch traced here: 26.1 us
  blocking collectives  20.9 us (79%)
  Pallas kernels  4.64 us (18%)
  between operations  0.64 us (2%)
    all_to_all x1, blocking collectives, shards(): lax.all_to_all(image, ('far', 'near'), 0, 0, axis_index_groups=[listed(fa...  10.7 us
    all_to_all x1, blocking collectives, shards(): lax.all_to_all(share, ('range', 'near'), 0, 0, axis_index_groups=order, t...  10.2 us
    pallas_call x1, Pallas kernels, image_share(): pl.pallas_call(functools.partial(image_kernel, bands, scaling, near, ping...  2.02 us
    pallas_call x1, Pallas kernels, own_share(): pl.pallas_call(functools.partial(fir_kernel, bands, front, stack), out_sh...  1.88 us
    pallas_call x1, Pallas kernels, turned(): pl.pallas_call(functools.partial(turn_kernel, far, stack), out_shape=(out...  0.74 us

profile of v19, /device:TPU:0, one launch (start us, length us, event | category | flops | bytes accessed | tf_op | source)
XLA Modules:
  0.0 26.1 jit_solution(18439367763248605074)
XLA Ops:
  0.6 1.9 %fir.1 = bf16[16,8,640]{2,1,0:T(8,128)(2,1)S(1)} custom-call(s32[8]{0:T(128)} %offset_hbm.1, s32[8]{0:T(128)} %track_hbm.1, bf16[256,128]{1,0:T(8,128)(2,1)} %bitcast.1, f32[8,32]{1,0:T(8,128)} %sway_hbm.1, f32[8,32]{1,0:T(8,128)} %gain_hbm.1), custom_call_target="tpu_custom_call" | custom-call | tf_op jit(solution)/shard_map/fir/pallas_call | solution.py:179
  2.5 10.2 %all_to_all.10.share_ref = bf16[16,8,640]{2,1,0:T(8,128)(2,1)S(1)} all-to-all(bf16[16,8,640]{2,1,0:T(8,128)(2,1)S(1)} %fir.1), channel_id=1, replica_groups={{23,16,17,18,19,20,21,22,0,1,2,3,4,5,6,7},{31,24,25,26,27,28,29,30,8,9,..., dimensions={0} | all-to-all | bytes 327680 | tf_op jit(solution)/shard_map/all_to_all | solution.py:415
  12.7 2.0 %image.1 = bf16[16,8,512]{2,1,0:T(8,128)(2,1)S(1)} custom-call(bf16[16,8,640]{2,1,0:T(8,128)(2,1)S(1)} %all_to_all.10.share_ref), custom_call_target="tpu_custom_call" | custom-call | tf_op jit(solution)/shard_map/image/pallas_call | solution.py:356
  14.7 10.7 %all_to_all.11.in_ref = bf16[16,8,512]{2,1,0:T(8,128)(2,1)S(1)} all-to-all(bf16[16,8,512]{2,1,0:T(8,128)(2,1)S(1)} %image.1), channel_id=1, replica_groups={{15,8,9,10,11,12,13,14,0,1,2,3,4,5,6,7},{31,24,25,26,27,28,29,30,16,17,..., dimensions={0} | all-to-all | bytes 262144 | tf_op jit(solution)/shard_map/all_to_all | solution.py:432
  25.4 0.7 %turn.1 = (f32[128,128]{1,0:T(8,128)}, f32[128,128]{1,0:T(8,128)}) custom-call(bf16[16,8,512]{2,1,0:T(8,128)(2,1)S(1)} %all_to_all.11.in_ref), custom_call_target="tpu_custom_call" | custom-call | tf_op jit(solution)/shard_map/turn/pallas_call | solution.py:397

commit v20 on v14

--- a/solution.py
+++ b/solution.py
@@ -268,7 +268,7 @@
     column = column.astype(jnp.float32).astype(jnp.bfloat16)
     lane = lax.broadcasted_iota(jnp.int32, (SUB, LANES), 1)
     channel = (lane % channels).astype(jnp.float32)
-    held, come = None, share_slots(bands, near)
+    held, come, waiting = None, share_slots(bands, near), []
     for group in range(near):
         share = share_ref[come[group], :, : stack * lanes].astype(jnp.float32)
         for copy in range(1, copies):
@@ -312,10 +312,15 @@
         spread = jnp.concatenate(
             [jnp.where(block == float(k), share, none) for k in range(half)], axis=0
         )
+        waiting.append((spread, jnp.concatenate(hot, axis=0)))
+        if len(waiting) < 2 and group < near - 1:
+            continue
         part = jnp.dot(
-            spread, jnp.concatenate(hot, axis=0), preferred_element_type=jnp.float32
+            jnp.concatenate([left for left, _ in waiting], axis=1),
+            jnp.concatenate([right for _, right in waiting], axis=0),
+            preferred_element_type=jnp.float32,
         )
-        held = part if held is None else held + part
+        held, waiting = part if held is None else held + part, []
     held = held.astype(jnp.bfloat16).reshape(half, rows, depth)
     windows = window_ref.reshape(half, 2, rows, depth)
     windows[:, 1] = held
@@ -324,20 +329,25 @@
     windows[1:, 0, :, :LANES] = held[:-1, :, LANES:]
 
     image = [None] * blocks
-    for quad in range(blocks // 2):
-        step = 4 * quad - blocks
-        first, last = max(0, -step - 2), min(2 * half - 1, blocks - 1 - step)
-        part = jnp.dot(
-            window_ref[first * rows : (last + 1) * rows, :],
-            table_ref[quad],
-            preferred_element_type=jnp.float32,
-        )
-        for k in range(first, last + 1):
-            for block, left in ((k + step, 0), (k + step + 2, LANES)):
-                if not 0 <= block < blocks:
-                    continue
-                term = part[(k - first) * rows : (k - first + 1) * rows, left : left + LANES]
-                image[block] = term if image[block] is None else image[block] + term
+    part_blocks = blocks // 2
+    for start in range(0, blocks, part_blocks):
+        stop = start + part_blocks
+        for quad in range(blocks // 2):
+            step = 4 * quad - blocks
+            first, last = max(0, start - step - 2), min(2 * half - 1, stop - 1 - step)
+            if first > last:
+                continue
+            part = jnp.dot(
+                window_ref[first * rows : (last + 1) * rows, :],
+                table_ref[quad],
+                preferred_element_type=jnp.float32,
+            )
+            for k in range(first, last + 1):
+                for block, left in ((k + step, 0), (k + step + 2, LANES)):
+                    if not start <= block < stop:
+                        continue
+                    term = part[(k - first) * rows : (k - first + 1) * rows, left : left + LANES]
+                    image[block] = term if image[block] is None else image[block] + term
     go = slots(groups)
     for block in range(blocks):
         group, within = block // share_blocks, block % share_blocks

time: 26 us -> 26 us (level)
  no operation moved by 1% of the time
where the time goes in v20:
time: 26 us; the launch traced here: 25.8 us
  blocking collectives  20.4 us (78%)
  Pallas kernels  4.69 us (18%)
  between operations  0.64 us (2%)
    all_to_all x1, blocking collectives, shards(): lax.all_to_all(image, ('far', 'near'), 0, 0, axis_index_groups=[listed(fa...  10.3 us
    all_to_all x1, blocking collectives, shards(): lax.all_to_all(share, ('range', 'near'), 0, 0, axis_index_groups=order, t...  10.2 us
    pallas_call x1, Pallas kernels, image_share(): pl.pallas_call(functools.partial(image_kernel, bands, scaling, near, ping...  2.07 us
    pallas_call x1, Pallas kernels, own_share(): pl.pallas_call(functools.partial(fir_kernel, bands, front, stack), out_sh...  1.89 us
    pallas_call x1, Pallas kernels, turned(): pl.pallas_call(functools.partial(turn_kernel, far, stack), out_shape=(out...  0.74 us

profile of v20, /device:TPU:0, one launch (start us, length us, event | category | flops | bytes accessed | tf_op | source)
XLA Modules:
  0.0 25.8 jit_solution(17095884709025678949)
XLA Ops:
  0.6 1.9 %fir.1 = bf16[16,8,640]{2,1,0:T(8,128)(2,1)S(1)} custom-call(s32[8]{0:T(128)} %offset_hbm.1, s32[8]{0:T(128)} %track_hbm.1, bf16[256,128]{1,0:T(8,128)(2,1)} %bitcast.1, f32[8,32]{1,0:T(8,128)} %sway_hbm.1, f32[8,32]{1,0:T(8,128)} %gain_hbm.1), custom_call_target="tpu_custom_call" | custom-call | tf_op jit(solution)/shard_map/fir/pallas_call | solution.py:179
  2.5 10.2 %all_to_all.10.share_ref = bf16[16,8,640]{2,1,0:T(8,128)(2,1)S(1)} all-to-all(bf16[16,8,640]{2,1,0:T(8,128)(2,1)S(1)} %fir.1), channel_id=1, replica_groups={{23,0,1,2,3,4,5,6,7,16,17,18,19,20,21,22},{31,8,9,10,11,12,13,14,15,24,..., dimensions={0} | all-to-all | bytes 327680 | tf_op jit(solution)/shard_map/all_to_all | solution.py:425
  12.7 2.1 %image.1 = bf16[16,8,512]{2,1,0:T(8,128)(2,1)S(1)} custom-call(bf16[16,8,640]{2,1,0:T(8,128)(2,1)S(1)} %all_to_all.10.share_ref), custom_call_target="tpu_custom_call" | custom-call | tf_op jit(solution)/shard_map/image/pallas_call | solution.py:366
  14.8 10.3 %all_to_all.11.in_ref = bf16[16,8,512]{2,1,0:T(8,128)(2,1)S(1)} all-to-all(bf16[16,8,512]{2,1,0:T(8,128)(2,1)S(1)} %image.1), channel_id=1, replica_groups={{15,0,1,2,3,4,5,6,7,8,9,10,11,12,13,14},{31,16,17,18,19,20,21,22,23,24,..., dimensions={0} | all-to-all | bytes 262144 | tf_op jit(solution)/shard_map/all_to_all | solution.py:442
  25.0 0.7 %turn.1 = (f32[128,128]{1,0:T(8,128)}, f32[128,128]{1,0:T(8,128)}) custom-call(bf16[16,8,512]{2,1,0:T(8,128)(2,1)S(1)} %all_to_all.11.in_ref), custom_call_target="tpu_custom_call" | custom-call | tf_op jit(solution)/shard_map/turn/pallas_call | solution.py:407

commit v21 on v14

--- a/solution.py
+++ b/solution.py
@@ -107,7 +107,7 @@
     for tile in range(lanes // LANES):
         cols = slice(tile * LANES, (tile + 1) * LANES)
         shift = tap_index.astype(jnp.float32) - (BAND / 2 - 1) - sway[:, cols]
-        whole = shift == 0.0
+        whole = jnp.abs(shift) < 1e-20
         signed = jnp.where(tap_index % 2 == 0, gain[:, cols], -gain[:, cols])
         scaled = jnp.where(whole, signed, amplitude[:, cols] / jnp.where(whole, 1.0, shift))
         tap_ref[:, cols] = scaled * window
@@ -316,24 +316,27 @@
             spread, jnp.concatenate(hot, axis=0), preferred_element_type=jnp.float32
         )
         held = part if held is None else held + part
-    held = held.astype(jnp.bfloat16).reshape(half, rows, depth)
-    windows = window_ref.reshape(half, 2, rows, depth)
-    windows[:, 1] = held
-    windows[:, 0, :, LANES:] = held[:, :, :LANES]
-    windows[0, 0, :, :LANES] = jnp.zeros((rows, LANES), jnp.bfloat16)
-    windows[1:, 0, :, :LANES] = held[:-1, :, LANES:]
+    held = held.astype(jnp.bfloat16)
+    for k in range(half):
+        block = held[k * rows : (k + 1) * rows]
+        odd, even = (2 * k + 1) * rows, 2 * k * rows
+        window_ref[odd : odd + rows, :] = block
+        window_ref[even : even + rows, LANES:] = block[:, :LANES]
+        before = held[(k - 1) * rows : k * rows, LANES:] if k else jnp.zeros_like(block[:, LANES:])
+        window_ref[even : even + rows, :LANES] = before
 
     image = [None] * blocks
-    for quad in range(blocks // 2):
+    for quad in range(0, blocks // 2, 2):
         step = 4 * quad - blocks
-        first, last = max(0, -step - 2), min(2 * half - 1, blocks - 1 - step)
+        first, last = max(0, -step - 6), min(2 * half - 1, blocks - 1 - step)
         part = jnp.dot(
             window_ref[first * rows : (last + 1) * rows, :],
-            table_ref[quad],
+            jnp.concatenate([table_ref[quad], table_ref[quad + 1]], axis=1),
             preferred_element_type=jnp.float32,
         )
         for k in range(first, last + 1):
-            for block, left in ((k + step, 0), (k + step + 2, LANES)):
+            for more in range(4):
+                block, left = k + step + 2 * more, more * LANES
                 if not 0 <= block < blocks:
                     continue
                 term = part[(k - first) * rows : (k - first + 1) * rows, left : left + LANES]

time: 26 us -> 26.1 us (level)
  no operation moved by 1% of the time
where the time goes in v21:
time: 26.1 us; the launch traced here: 25.9 us
  blocking collectives  20.4 us (78%)
  Pallas kernels  4.76 us (18%)
  between operations  0.65 us (2%)
    all_to_all x1, blocking collectives, shards(): lax.all_to_all(image, ('far', 'near'), 0, 0, axis_index_groups=[listed(fa...  10.3 us
    all_to_all x1, blocking collectives, shards(): lax.all_to_all(share, ('range', 'near'), 0, 0, axis_index_groups=order, t...  10.2 us
    pallas_call x1, Pallas kernels, image_share(): pl.pallas_call(functools.partial(image_kernel, bands, scaling, near, ping...  2.13 us
    pallas_call x1, Pallas kernels, own_share(): pl.pallas_call(functools.partial(fir_kernel, bands, front, stack), out_sh...  1.89 us
    pallas_call x1, Pallas kernels, turned(): pl.pallas_call(functools.partial(turn_kernel, far, stack), out_shape=(out...  0.74 us

profile of v21, /device:TPU:0, one launch (start us, length us, event | category | flops | bytes accessed | tf_op | source)
XLA Modules:
  0.0 25.9 jit_solution(13919325103218435161)
XLA Ops:
  0.6 1.9 %fir.1 = bf16[16,8,640]{2,1,0:T(8,128)(2,1)S(1)} custom-call(s32[8]{0:T(128)} %offset_hbm.1, s32[8]{0:T(128)} %track_hbm.1, bf16[256,128]{1,0:T(8,128)(2,1)} %bitcast.1, f32[8,32]{1,0:T(8,128)} %sway_hbm.1, f32[8,32]{1,0:T(8,128)} %gain_hbm.1), custom_call_target="tpu_custom_call" | custom-call | tf_op jit(solution)/shard_map/fir/pallas_call | solution.py:179
  2.5 10.2 %all_to_all.10.share_ref = bf16[16,8,640]{2,1,0:T(8,128)(2,1)S(1)} all-to-all(bf16[16,8,640]{2,1,0:T(8,128)(2,1)S(1)} %fir.1), channel_id=1, replica_groups={{23,0,1,2,3,4,5,6,7,16,17,18,19,20,21,22},{31,8,9,10,11,12,13,14,15,24,..., dimensions={0} | all-to-all | bytes 327680 | tf_op jit(solution)/shard_map/all_to_all | solution.py:418
  12.7 2.1 %image.1 = bf16[16,8,512]{2,1,0:T(8,128)(2,1)S(1)} custom-call(bf16[16,8,640]{2,1,0:T(8,128)(2,1)S(1)} %all_to_all.10.share_ref), custom_call_target="tpu_custom_call" | custom-call | tf_op jit(solution)/shard_map/image/pallas_call | solution.py:359
  14.8 10.3 %all_to_all.11.in_ref = bf16[16,8,512]{2,1,0:T(8,128)(2,1)S(1)} all-to-all(bf16[16,8,512]{2,1,0:T(8,128)(2,1)S(1)} %image.1), channel_id=1, replica_groups={{15,0,1,2,3,4,5,6,7,8,9,10,11,12,13,14},{31,16,17,18,19,20,21,22,23,24,..., dimensions={0} | all-to-all | bytes 262144 | tf_op jit(solution)/shard_map/all_to_all | solution.py:435
  25.1 0.7 %turn.1 = (f32[128,128]{1,0:T(8,128)}, f32[128,128]{1,0:T(8,128)}) custom-call(bf16[16,8,512]{2,1,0:T(8,128)(2,1)S(1)} %all_to_all.11.in_ref), custom_call_target="tpu_custom_call" | custom-call | tf_op jit(solution)/shard_map/turn/pallas_call | solution.py:400

commit v22 on v21

--- a/solution.py
+++ b/solution.py
@@ -212,30 +212,44 @@
     return total * angle
 
 
-def fill_table(bands, scaling, table_ref):
-    quads = table_ref.shape[0]
-    blocks = 4 * quads
+def place_order(places):
+    return places // 16 * 16 + places % 8 * 2 + places % 16 // 8
+
+
+def fill_table(bands, scaling, line_ref, table_ref):
+    blocks = 4 * table_ref.shape[0]
     band = lax.axis_index("range").astype(jnp.float32)
     spread = 0.5 * X * (1.0 + (band + 0.5) * (1.0 / bands))
+    shape = line_ref.shape[1:]
+    inside = lax.broadcasted_iota(jnp.int32, shape, 1)
+    column = (lax.broadcasted_iota(jnp.int32, shape, 0) - (blocks // 2 + 1)) * SPAN + inside % SPAN
+    for odd in range(2):
+        index = (2 * column - odd).astype(jnp.float32)
+        square = index * index
+        weight = jnp.exp(square * (-0.125 * (8.0 / X) ** 2)) * scaling
+        turns = square * (0.125 / spread)
+        turns = turns - jnp.round(turns) - jnp.where(inside < SPAN, 0.0, 0.25)
+        sine = sine_of_pi(turns - jnp.round(turns))
+        line_ref[odd] = weight * (1.0 - 2.0 * sine * sine)
+
+    lane = lax.broadcasted_iota(jnp.int32, (SUB, LANES), 1) % SPAN
+    back = lane < lax.broadcasted_iota(jnp.int32, (SUB, LANES), 0)
+    tiles, before = [], [None, None]
+    for block in range(blocks + 1):
+        rows = []
+        for odd in range(2):
+            line = jnp.broadcast_to(line_ref[odd, block : block + 1, :], (SUB, LANES))
+            now = pltpu.roll(line, 0, 1, stride=1, stride_axis=0)
+            rows.append(jnp.where(back, before[odd], now) if block else now)
+            before[odd] = pltpu.roll(line, SPAN, 1, stride=1, stride_axis=0)
+        tiles.append(jnp.concatenate(rows, axis=0).astype(jnp.bfloat16))
+
     pack = 2 * SUB
-    length = (blocks + 1) * LANES
-    lane = lax.broadcasted_iota(jnp.int32, (pack, length), 1)
-    row = lax.broadcasted_iota(jnp.int32, (pack, length), 0)
-    inside = lane % LANES
-    column = (lane // LANES - (blocks // 2 + 1)) * SPAN + inside % SPAN
-    twice = (2 * column - row).astype(jnp.float32)
-    square = twice * twice
-    weight = jnp.exp(square * (-0.125 * (8.0 / X) ** 2)) * scaling
-    turns = square * (0.125 / spread)
-    turns = turns - jnp.round(turns) - jnp.where(inside < SPAN, 0.0, 0.25)
-    sine = sine_of_pi(turns - jnp.round(turns))
-    values = (weight * (1.0 - 2.0 * sine * sine)).astype(jnp.bfloat16)
     lane16 = lax.broadcasted_iota(jnp.int32, (pack, LANES), 1) % SPAN
     lane16 = lane16.astype(jnp.bfloat16)
     for first in range(0, LANES, pack):
         by, before = first // 2, None
-        for block in range(blocks + 1):
-            tile = values[:, block * LANES : (block + 1) * LANES]
+        for block, tile in enumerate(tiles):
             if block:
                 value = tile
                 if by:
@@ -249,7 +263,7 @@
 
 
 def image_kernel(
-    bands, scaling, near, pings, channels, share_ref, out_ref, window_ref, table_ref
+    bands, scaling, near, pings, channels, share_ref, out_ref, window_ref, line_ref, table_ref
 ):
     groups = out_ref.shape[0]
     copies = share_ref.shape[0] // near
@@ -260,10 +274,10 @@
     rows = stack * SUB
     lanes = pings * channels
     half = window_ref.shape[0] // rows // 2
-    fill_table(bands, scaling, table_ref)
+    fill_table(bands, scaling, line_ref, table_ref)
 
     one, none = jnp.ones((), jnp.bfloat16), jnp.zeros((), jnp.bfloat16)
-    column = lax.broadcasted_iota(jnp.int32, (channels, depth), 1)
+    column = place_order(lax.broadcasted_iota(jnp.int32, (channels, depth), 1))
     column = (column - lax.broadcasted_iota(jnp.int32, (channels, depth), 0)) & (depth - 1)
     column = column.astype(jnp.float32).astype(jnp.bfloat16)
     lane = lax.broadcasted_iota(jnp.int32, (SUB, LANES), 1)
@@ -326,17 +340,16 @@
         window_ref[even : even + rows, :LANES] = before
 
     image = [None] * blocks
-    for quad in range(0, blocks // 2, 2):
+    for quad in range(blocks // 2):
         step = 4 * quad - blocks
-        first, last = max(0, -step - 6), min(2 * half - 1, blocks - 1 - step)
+        first, last = max(0, -step - 2), min(2 * half - 1, blocks - 1 - step)
         part = jnp.dot(
             window_ref[first * rows : (last + 1) * rows, :],
-            jnp.concatenate([table_ref[quad], table_ref[quad + 1]], axis=1),
+            table_ref[quad],
             preferred_element_type=jnp.float32,
         )
         for k in range(first, last + 1):
-            for more in range(4):
-                block, left = k + step + 2 * more, more * LANES
+            for block, left in ((k + step, 0), (k + step + 2, LANES)):
                 if not 0 <= block < blocks:
                     continue
                 term = part[(k - first) * rows : (k - first + 1) * rows, left : left + LANES]
@@ -363,6 +376,7 @@
         out_specs=vmem,
         scratch_shapes=[
             pltpu.VMEM((2 * half * stack * SUB, depth), jnp.bfloat16),
+            pltpu.VMEM((2, round_up(2 * blocks + 1, SUB), LANES), jnp.float32),
             pltpu.VMEM((blocks // 2, depth, depth), jnp.bfloat16),
         ],
         compiler_params=pltpu.CompilerParams(vmem_limit_bytes=16 * MIB),

time: 26.1 us -> 25.8 us (0.989)
  no operation moved by 1% of the time
where the time goes in v22:
time: 25.8 us; the launch traced here: 25.6 us
  blocking collectives  20.4 us (79%)
  Pallas kernels  4.5 us (17%)
  between operations  0.64 us (2%)
    all_to_all x1, blocking collectives, shards(): lax.all_to_all(image, ('far', 'near'), 0, 0, axis_index_groups=[listed(fa...  10.3 us
    all_to_all x1, blocking collectives, shards(): lax.all_to_all(share, ('range', 'near'), 0, 0, axis_index_groups=order, t...  10.2 us
    pallas_call x1, Pallas kernels, own_share(): pl.pallas_call(functools.partial(fir_kernel, bands, front, stack), out_sh...  1.89 us
    pallas_call x1, Pallas kernels, image_share(): pl.pallas_call(functools.partial(image_kernel, bands, scaling, near, ping...  1.88 us
    pallas_call x1, Pallas kernels, turned(): pl.pallas_call(functools.partial(turn_kernel, far, stack), out_shape=(out...  0.74 us

profile of v22, /device:TPU:0, one launch (start us, length us, event | category | flops | bytes accessed | tf_op | source)
XLA Modules:
  0.0 25.6 jit_solution(15739279211704110634)
XLA Ops:
  0.6 1.9 %fir.1 = bf16[16,8,640]{2,1,0:T(8,128)(2,1)S(1)} custom-call(s32[8]{0:T(128)} %offset_hbm.1, s32[8]{0:T(128)} %track_hbm.1, bf16[256,128]{1,0:T(8,128)(2,1)} %bitcast.1, f32[8,32]{1,0:T(8,128)} %sway_hbm.1, f32[8,32]{1,0:T(8,128)} %gain_hbm.1), custom_call_target="tpu_custom_call" | custom-call | tf_op jit(solution)/shard_map/fir/pallas_call | solution.py:179
  2.5 10.2 %all_to_all.10.share_ref = bf16[16,8,640]{2,1,0:T(8,128)(2,1)S(1)} all-to-all(bf16[16,8,640]{2,1,0:T(8,128)(2,1)S(1)} %fir.1), channel_id=1, replica_groups={{23,0,1,2,3,4,5,6,7,16,17,18,19,20,21,22},{31,8,9,10,11,12,13,14,15,24,..., dimensions={0} | all-to-all | bytes 327680 | tf_op jit(solution)/shard_map/all_to_all | solution.py:432
  12.7 1.9 %image.1 = bf16[16,8,512]{2,1,0:T(8,128)(2,1)S(1)} custom-call(bf16[16,8,640]{2,1,0:T(8,128)(2,1)S(1)} %all_to_all.10.share_ref), custom_call_target="tpu_custom_call" | custom-call | tf_op jit(solution)/shard_map/image/pallas_call | solution.py:372
  14.6 10.3 %all_to_all.11.in_ref = bf16[16,8,512]{2,1,0:T(8,128)(2,1)S(1)} all-to-all(bf16[16,8,512]{2,1,0:T(8,128)(2,1)S(1)} %image.1), channel_id=1, replica_groups={{15,0,1,2,3,4,5,6,7,8,9,10,11,12,13,14},{31,16,17,18,19,20,21,22,23,24,..., dimensions={0} | all-to-all | bytes 262144 | tf_op jit(solution)/shard_map/all_to_all | solution.py:449
  24.9 0.7 %turn.1 = (f32[128,128]{1,0:T(8,128)}, f32[128,128]{1,0:T(8,128)}) custom-call(bf16[16,8,512]{2,1,0:T(8,128)(2,1)S(1)} %all_to_all.11.in_ref), custom_call_target="tpu_custom_call" | custom-call | tf_op jit(solution)/shard_map/turn/pallas_call | solution.py:414

commit v23 on v22

--- a/solution.py
+++ b/solution.py
@@ -274,7 +274,6 @@
     rows = stack * SUB
     lanes = pings * channels
     half = window_ref.shape[0] // rows // 2
-    fill_table(bands, scaling, line_ref, table_ref)
 
     one, none = jnp.ones((), jnp.bfloat16), jnp.zeros((), jnp.bfloat16)
     column = place_order(lax.broadcasted_iota(jnp.int32, (channels, depth), 1))
@@ -330,6 +329,8 @@
             spread, jnp.concatenate(hot, axis=0), preferred_element_type=jnp.float32
         )
         held = part if held is None else held + part
+    fill_table(bands, scaling, line_ref, table_ref)
+
     held = held.astype(jnp.bfloat16)
     for k in range(half):
         block = held[k * rows : (k + 1) * rows]

time: 25.8 us -> 25.8 us (level)
  no operation moved by 1% of the time
where the time goes in v23:
time: 25.8 us; the launch traced here: 25.6 us
  blocking collectives  20.5 us (79%)
  Pallas kernels  4.5 us (17%)
  between operations  0.64 us (2%)
    all_to_all x1, blocking collectives, shards(): lax.all_to_all(image, ('far', 'near'), 0, 0, axis_index_groups=[listed(fa...  10.3 us
    all_to_all x1, blocking collectives, shards(): lax.all_to_all(share, ('range', 'near'), 0, 0, axis_index_groups=order, t...  10.2 us
    pallas_call x1, Pallas kernels, own_share(): pl.pallas_call(functools.partial(fir_kernel, bands, front, stack), out_sh...  1.89 us
    pallas_call x1, Pallas kernels, image_share(): pl.pallas_call(functools.partial(image_kernel, bands, scaling, near, ping...  1.88 us
    pallas_call x1, Pallas kernels, turned(): pl.pallas_call(functools.partial(turn_kernel, far, stack), out_shape=(out...  0.74 us

profile of v23, /device:TPU:0, one launch (start us, length us, event | category | flops | bytes accessed | tf_op | source)
XLA Modules:
  0.0 25.6 jit_solution(15495583533564327759)
XLA Ops:
  0.6 1.9 %fir.1 = bf16[16,8,640]{2,1,0:T(8,128)(2,1)S(1)} custom-call(s32[8]{0:T(128)} %offset_hbm.1, s32[8]{0:T(128)} %track_hbm.1, bf16[256,128]{1,0:T(8,128)(2,1)} %bitcast.1, f32[8,32]{1,0:T(8,128)} %sway_hbm.1, f32[8,32]{1,0:T(8,128)} %gain_hbm.1), custom_call_target="tpu_custom_call" | custom-call | tf_op jit(solution)/shard_map/fir/pallas_call | solution.py:179
  2.5 10.2 %all_to_all.10.share_ref = bf16[16,8,640]{2,1,0:T(8,128)(2,1)S(1)} all-to-all(bf16[16,8,640]{2,1,0:T(8,128)(2,1)S(1)} %fir.1), channel_id=1, replica_groups={{23,0,1,2,3,4,5,6,7,16,17,18,19,20,21,22},{31,8,9,10,11,12,13,14,15,24,..., dimensions={0} | all-to-all | bytes 327680 | tf_op jit(solution)/shard_map/all_to_all | solution.py:433
  12.7 1.9 %image.1 = bf16[16,8,512]{2,1,0:T(8,128)(2,1)S(1)} custom-call(bf16[16,8,640]{2,1,0:T(8,128)(2,1)S(1)} %all_to_all.10.share_ref), custom_call_target="tpu_custom_call" | custom-call | tf_op jit(solution)/shard_map/image/pallas_call | solution.py:373
  14.6 10.3 %all_to_all.11.in_ref = bf16[16,8,512]{2,1,0:T(8,128)(2,1)S(1)} all-to-all(bf16[16,8,512]{2,1,0:T(8,128)(2,1)S(1)} %image.1), channel_id=1, replica_groups={{15,0,1,2,3,4,5,6,7,8,9,10,11,12,13,14},{31,16,17,18,19,20,21,22,23,24,..., dimensions={0} | all-to-all | bytes 262144 | tf_op jit(solution)/shard_map/all_to_all | solution.py:450
  24.9 0.7 %turn.1 = (f32[128,128]{1,0:T(8,128)}, f32[128,128]{1,0:T(8,128)}) custom-call(bf16[16,8,512]{2,1,0:T(8,128)(2,1)S(1)} %all_to_all.11.in_ref), custom_call_target="tpu_custom_call" | custom-call | tf_op jit(solution)/shard_map/turn/pallas_call | solution.py:415

commit v24 on v22

--- a/solution.py
+++ b/solution.py
@@ -65,6 +65,7 @@
     sway_ref,
     gain_ref,
     tap_ref,
+    padded_ref,
     placed_ref,
     sems,
 ):
@@ -114,14 +115,18 @@
 
     echo = jnp.transpose(echo_ref[...].astype(jnp.float32))
     blocks = ext // SUB
+    aligned = jnp.maximum(lax.axis_index("range") - bands, 0)
     for tile in range(lanes // LANES):
         cols = slice(tile * LANES, (tile + 1) * LANES)
         edge = jnp.zeros((SUB, LANES), jnp.float32)
         padded = jnp.concatenate([edge, echo[:, cols], edge], axis=0)
         height = padded.shape[0]
+        padded_ref[tile] = padded
         total = [None] * blocks
         for s in range(SUB):
-            moved = pltpu.roll(padded, height - s, 0) if s else padded
+            moved = padded
+            if s:
+                moved = padded_ref[tile, pl.ds(aligned + s, height - SUB), :]
             first_tap = (BAND - 1 - SUB + s) % SUB
             taps = {
                 k: jnp.broadcast_to(tap_ref[k : k + 1, cols], (SUB, LANES))
@@ -188,6 +193,7 @@
             pltpu.VMEM((pings, channels), jnp.float32),
             pltpu.VMEM((pings, channels), jnp.float32),
             pltpu.VMEM((BAND, lanes), jnp.float32),
+            pltpu.VMEM((lanes // LANES, samples + 2 * SUB, LANES), jnp.float32),
             pltpu.VMEM((lanes // LANES, height, LANES), jnp.float32),
             pltpu.SemaphoreType.DMA((5,)),
         ],
@@ -282,7 +288,7 @@
     column = column.astype(jnp.float32).astype(jnp.bfloat16)
     lane = lax.broadcasted_iota(jnp.int32, (SUB, LANES), 1)
     channel = (lane % channels).astype(jnp.float32)
-    held, come = None, share_slots(bands, near)
+    held, come, waiting = None, share_slots(bands, near), []
     for group in range(near):
         share = share_ref[come[group], :, : stack * lanes].astype(jnp.float32)
         for copy in range(1, copies):
@@ -326,10 +332,15 @@
         spread = jnp.concatenate(
             [jnp.where(block == float(k), share, none) for k in range(half)], axis=0
         )
+        waiting.append((spread, jnp.concatenate(hot, axis=0)))
+        if len(waiting) < 2 and group < near - 1:
+            continue
         part = jnp.dot(
-            spread, jnp.concatenate(hot, axis=0), preferred_element_type=jnp.float32
+            jnp.concatenate([left for left, _ in waiting], axis=1),
+            jnp.concatenate([right for _, right in waiting], axis=0),
+            preferred_element_type=jnp.float32,
         )
-        held = part if held is None else held + part
+        held, waiting = part if held is None else held + part, []
     held = held.astype(jnp.bfloat16)
     for k in range(half):
         block = held[k * rows : (k + 1) * rows]

time: 25.8 us -> 25.8 us (level)
  no operation moved by 1% of the time
where the time goes in v24:
time: 25.8 us; the launch traced here: 25.6 us
  blocking collectives  20.5 us (79%)
  Pallas kernels  4.51 us (17%)
  between operations  0.64 us (2%)
    all_to_all x1, blocking collectives, shards(): lax.all_to_all(image, ('far', 'near'), 0, 0, axis_index_groups=[listed(fa...  10.3 us
    all_to_all x1, blocking collectives, shards(): lax.all_to_all(share, ('range', 'near'), 0, 0, axis_index_groups=order, t...  10.1 us
    pallas_call x1, Pallas kernels, own_share(): pl.pallas_call(functools.partial(fir_kernel, bands, front, stack), out_sh...  1.9 us
    pallas_call x1, Pallas kernels, image_share(): pl.pallas_call(functools.partial(image_kernel, bands, scaling, near, ping...  1.88 us
    pallas_call x1, Pallas kernels, turned(): pl.pallas_call(functools.partial(turn_kernel, far, stack), out_shape=(out...  0.74 us

profile of v24, /device:TPU:0, one launch (start us, length us, event | category | flops | bytes accessed | tf_op | source)
XLA Modules:
  0.0 25.6 jit_solution(15209167245213701563)
XLA Ops:
  0.6 1.9 %fir.1 = bf16[16,8,640]{2,1,0:T(8,128)(2,1)S(1)} custom-call(s32[8]{0:T(128)} %offset_hbm.1, s32[8]{0:T(128)} %track_hbm.1, bf16[256,128]{1,0:T(8,128)(2,1)} %bitcast.1, f32[8,32]{1,0:T(8,128)} %sway_hbm.1, f32[8,32]{1,0:T(8,128)} %gain_hbm.1), custom_call_target="tpu_custom_call" | custom-call | tf_op jit(solution)/shard_map/fir/pallas_call | solution.py:184
  2.5 10.1 %all_to_all.10.share_ref = bf16[16,8,640]{2,1,0:T(8,128)(2,1)S(1)} all-to-all(bf16[16,8,640]{2,1,0:T(8,128)(2,1)S(1)} %fir.1), channel_id=1, replica_groups={{23,0,1,2,3,4,5,6,7,16,17,18,19,20,21,22},{31,8,9,10,11,12,13,14,15,24,..., dimensions={0} | all-to-all | bytes 327680 | tf_op jit(solution)/shard_map/all_to_all | solution.py:443
  12.7 1.9 %image.1 = bf16[16,8,512]{2,1,0:T(8,128)(2,1)S(1)} custom-call(bf16[16,8,640]{2,1,0:T(8,128)(2,1)S(1)} %all_to_all.10.share_ref), custom_call_target="tpu_custom_call" | custom-call | tf_op jit(solution)/shard_map/image/pallas_call | solution.py:383
  14.6 10.3 %all_to_all.11.in_ref = bf16[16,8,512]{2,1,0:T(8,128)(2,1)S(1)} all-to-all(bf16[16,8,512]{2,1,0:T(8,128)(2,1)S(1)} %image.1), channel_id=1, replica_groups={{15,0,1,2,3,4,5,6,7,8,9,10,11,12,13,14},{31,16,17,18,19,20,21,22,23,24,..., dimensions={0} | all-to-all | bytes 262144 | tf_op jit(solution)/shard_map/all_to_all | solution.py:460
  24.9 0.7 %turn.1 = (f32[128,128]{1,0:T(8,128)}, f32[128,128]{1,0:T(8,128)}) custom-call(bf16[16,8,512]{2,1,0:T(8,128)(2,1)S(1)} %all_to_all.11.in_ref), custom_call_target="tpu_custom_call" | custom-call | tf_op jit(solution)/shard_map/turn/pallas_call | solution.py:425

commit v25 on v24

--- a/solution.py
+++ b/solution.py
@@ -96,7 +96,9 @@
         placed_ref[tile, :front, :] = jnp.zeros((front, LANES), jnp.float32)
         placed_ref[tile, front + ext :, :] = jnp.zeros((tail, LANES), jnp.float32)
     tap_index = lax.broadcasted_iota(jnp.int32, (BAND, LANES), 0)
-    window = 0.5 - 0.5 * jnp.cos(2.0 * math.pi * (tap_index.astype(jnp.float32) + 0.5) / BAND)
+    across = (tap_index.astype(jnp.float32) + 0.5) * (1.0 / BAND)
+    window = sine_of_pi(jnp.minimum(across, 1.0 - across))
+    window = window * window
     window = jnp.where(tap_index % 2 == 0, window, -window)
 
     for fetch in fetches:
@@ -365,7 +367,7 @@
                     continue
                 term = part[(k - first) * rows : (k - first + 1) * rows, left : left + LANES]
                 image[block] = term if image[block] is None else image[block] + term
-    go = slots(groups)
+    go = list(range(groups))[::-1]
     for block in range(blocks):
         group, within = block // share_blocks, block % share_blocks
         value = image[block].astype(jnp.bfloat16)
@@ -398,7 +400,7 @@
 def turn_kernel(far, stack, in_ref, real_ref, imag_ref):
     groups, sub, width = in_ref.shape
     near = groups // far
-    come = slots(groups)
+    come = list(range(groups))[::-1]
     whole = []
     for source in range(near):
         total = in_ref[come[source]].astype(jnp.float32)
@@ -458,7 +460,7 @@
         )
     image = image_share(share, bands, scaling, far, near, stack, pings, channels)
     image = lax.all_to_all(
-        image, ("far", "near"), 0, 0, axis_index_groups=[listed(far * near)], tiled=True
+        image, ("far", "near"), 0, 0, axis_index_groups=[list(range(far * near))[::-1]], tiled=True
     )
     return turned(image, X // (far * near), samples, far, stack)
 

time: 25.8 us -> 26.2 us (1.016)
  blocking collectives: 20.5 us -> 20.8 us
    all_to_all x1, blocking collectives: 10.3 us -> 10.7 us  [shards(): lax.all_to_all(image, ('far', 'near'), 0, 0, axis_index_groups=[list(rang...]
where the time goes in v25:
time: 26.2 us; the launch traced here: 26 us
  blocking collectives  20.8 us (79%)
  Pallas kernels  4.51 us (17%)
  between operations  0.64 us (2%)
    all_to_all x1, blocking collectives, shards(): lax.all_to_all(image, ('far', 'near'), 0, 0, axis_index_groups=[list(rang...  10.7 us
    all_to_all x1, blocking collectives, shards(): lax.all_to_all(share, ('range', 'near'), 0, 0, axis_index_groups=order, t...  10.2 us
    pallas_call x1, Pallas kernels, own_share(): pl.pallas_call(functools.partial(fir_kernel, bands, front, stack), out_sh...  1.9 us
    pallas_call x1, Pallas kernels, image_share(): pl.pallas_call(functools.partial(image_kernel, bands, scaling, near, ping...  1.88 us
    pallas_call x1, Pallas kernels, turned(): pl.pallas_call(functools.partial(turn_kernel, far, stack), out_shape=(out...  0.74 us

profile of v25, /device:TPU:0, one launch (start us, length us, event | category | flops | bytes accessed | tf_op | source)
XLA Modules:
  0.0 26.0 jit_solution(8852806001122296502)
XLA Ops:
  0.6 1.9 %fir.1 = bf16[16,8,640]{2,1,0:T(8,128)(2,1)S(1)} custom-call(s32[8]{0:T(128)} %offset_hbm.1, s32[8]{0:T(128)} %track_hbm.1, bf16[256,128]{1,0:T(8,128)(2,1)} %bitcast.1, f32[8,32]{1,0:T(8,128)} %sway_hbm.1, f32[8,32]{1,0:T(8,128)} %gain_hbm.1), custom_call_target="tpu_custom_call" | custom-call | tf_op jit(solution)/shard_map/fir/pallas_call | solution.py:186
  2.5 10.2 %all_to_all.10.share_ref = bf16[16,8,640]{2,1,0:T(8,128)(2,1)S(1)} all-to-all(bf16[16,8,640]{2,1,0:T(8,128)(2,1)S(1)} %fir.1), channel_id=1, replica_groups={{23,0,1,2,3,4,5,6,7,16,17,18,19,20,21,22},{31,8,9,10,11,12,13,14,15,24,..., dimensions={0} | all-to-all | bytes 327680 | tf_op jit(solution)/shard_map/all_to_all | solution.py:445
  12.7 1.9 %image.1 = bf16[16,8,512]{2,1,0:T(8,128)(2,1)S(1)} custom-call(bf16[16,8,640]{2,1,0:T(8,128)(2,1)S(1)} %all_to_all.10.share_ref), custom_call_target="tpu_custom_call" | custom-call | tf_op jit(solution)/shard_map/image/pallas_call | solution.py:385
  14.6 10.7 %all_to_all.11.in_ref = bf16[16,8,512]{2,1,0:T(8,128)(2,1)S(1)} all-to-all(bf16[16,8,512]{2,1,0:T(8,128)(2,1)S(1)} %image.1), channel_id=1, replica_groups={{15,14,13,12,11,10,9,8,7,6,5,4,3,2,1,0},{31,30,29,28,27,26,25,24,23,22,..., dimensions={0} | all-to-all | bytes 262144 | tf_op jit(solution)/shard_map/all_to_all | solution.py:462
  25.2 0.7 %turn.1 = (f32[128,128]{1,0:T(8,128)}, f32[128,128]{1,0:T(8,128)}) custom-call(bf16[16,8,512]{2,1,0:T(8,128)(2,1)S(1)} %all_to_all.11.in_ref), custom_call_target="tpu_custom_call" | custom-call | tf_op jit(solution)/shard_map/turn/pallas_call | solution.py:427

commit v26 on v22

--- a/solution.py
+++ b/solution.py
@@ -26,9 +26,14 @@
     return [size - 1, *range(size - 1)]
 
 
-def slots(size):
-    order = listed(size)
-    return [order.index(device) for device in range(size)]
+def image_listed(size):
+    first = [size - 1, *range(min(2, size - 1))]
+    rest = [*range(size // 2, size - 1), *range(size // 2)]
+    return first + [device for device in rest if device not in first]
+
+
+def slots(size, order=listed):
+    return [order(size).index(device) for device in range(size)]
 
 
 def share_slots(bands, near):
@@ -354,7 +359,7 @@
                     continue
                 term = part[(k - first) * rows : (k - first + 1) * rows, left : left + LANES]
                 image[block] = term if image[block] is None else image[block] + term
-    go = slots(groups)
+    go = slots(groups, image_listed)
     for block in range(blocks):
         group, within = block // share_blocks, block % share_blocks
         value = image[block].astype(jnp.bfloat16)
@@ -387,7 +392,7 @@
 def turn_kernel(far, stack, in_ref, real_ref, imag_ref):
     groups, sub, width = in_ref.shape
     near = groups // far
-    come = slots(groups)
+    come = slots(groups, image_listed)
     whole = []
     for source in range(near):
         total = in_ref[come[source]].astype(jnp.float32)
@@ -447,7 +452,7 @@
         )
     image = image_share(share, bands, scaling, far, near, stack, pings, channels)
     image = lax.all_to_all(
-        image, ("far", "near"), 0, 0, axis_index_groups=[listed(far * near)], tiled=True
+        image, ("far", "near"), 0, 0, axis_index_groups=[image_listed(far * near)], tiled=True
     )
     return turned(image, X // (far * near), samples, far, stack)
 

time: 25.8 us -> 26.3 us (1.019)
  blocking collectives: 20.4 us -> 20.9 us
    all_to_all x1, blocking collectives: 10.3 us -> 10.8 us  [shards(): lax.all_to_all(image, ('far', 'near'), 0, 0, axis_index_groups=[image_lis...]
where the time goes in v26:
time: 26.3 us; the launch traced here: 26.1 us
  blocking collectives  20.9 us (79%)
  Pallas kernels  4.51 us (17%)
  between operations  0.64 us (2%)
    all_to_all x1, blocking collectives, shards(): lax.all_to_all(image, ('far', 'near'), 0, 0, axis_index_groups=[image_lis...  10.8 us
    all_to_all x1, blocking collectives, shards(): lax.all_to_all(share, ('range', 'near'), 0, 0, axis_index_groups=order, t...  10.2 us
    pallas_call x1, Pallas kernels, own_share(): pl.pallas_call(functools.partial(fir_kernel, bands, front, stack), out_sh...  1.89 us
    pallas_call x1, Pallas kernels, image_share(): pl.pallas_call(functools.partial(image_kernel, bands, scaling, near, ping...  1.88 us
    pallas_call x1, Pallas kernels, turned(): pl.pallas_call(functools.partial(turn_kernel, far, stack), out_shape=(out...  0.74 us

profile of v26, /device:TPU:0, one launch (start us, length us, event | category | flops | bytes accessed | tf_op | source)
XLA Modules:
  0.0 26.1 jit_solution(4791550638688497004)
XLA Ops:
  0.6 1.9 %fir.1 = bf16[16,8,640]{2,1,0:T(8,128)(2,1)S(1)} custom-call(s32[8]{0:T(128)} %offset_hbm.1, s32[8]{0:T(128)} %track_hbm.1, bf16[256,128]{1,0:T(8,128)(2,1)} %bitcast.1, f32[8,32]{1,0:T(8,128)} %sway_hbm.1, f32[8,32]{1,0:T(8,128)} %gain_hbm.1), custom_call_target="tpu_custom_call" | custom-call | tf_op jit(solution)/shard_map/fir/pallas_call | solution.py:184
  2.5 10.2 %all_to_all.10.share_ref = bf16[16,8,640]{2,1,0:T(8,128)(2,1)S(1)} all-to-all(bf16[16,8,640]{2,1,0:T(8,128)(2,1)S(1)} %fir.1), channel_id=1, replica_groups={{23,0,1,2,3,4,5,6,7,16,17,18,19,20,21,22},{31,8,9,10,11,12,13,14,15,24,..., dimensions={0} | all-to-all | bytes 327680 | tf_op jit(solution)/shard_map/all_to_all | solution.py:437
  12.7 1.9 %image.1 = bf16[16,8,512]{2,1,0:T(8,128)(2,1)S(1)} custom-call(bf16[16,8,640]{2,1,0:T(8,128)(2,1)S(1)} %all_to_all.10.share_ref), custom_call_target="tpu_custom_call" | custom-call | tf_op jit(solution)/shard_map/image/pallas_call | solution.py:377
  14.6 10.8 %all_to_all.11.in_ref = bf16[16,8,512]{2,1,0:T(8,128)(2,1)S(1)} all-to-all(bf16[16,8,512]{2,1,0:T(8,128)(2,1)S(1)} %image.1), channel_id=1, replica_groups={{15,0,1,8,9,10,11,12,13,14,2,3,4,5,6,7},{31,16,17,24,25,26,27,28,29,30,..., dimensions={0} | all-to-all | bytes 262144 | tf_op jit(solution)/shard_map/all_to_all | solution.py:454
  25.3 0.7 %turn.1 = (f32[128,128]{1,0:T(8,128)}, f32[128,128]{1,0:T(8,128)}) custom-call(bf16[16,8,512]{2,1,0:T(8,128)(2,1)S(1)} %all_to_all.11.in_ref), custom_call_target="tpu_custom_call" | custom-call | tf_op jit(solution)/shard_map/turn/pallas_call | solution.py:419

commit v27 on v22

--- a/solution.py
+++ b/solution.py
@@ -112,7 +112,14 @@
         scaled = jnp.where(whole, signed, amplitude[:, cols] / jnp.where(whole, 1.0, shift))
         tap_ref[:, cols] = scaled * window
 
-    echo = jnp.transpose(echo_ref[...].astype(jnp.float32))
+    row = lax.broadcasted_iota(jnp.int32, (samples, samples), 0)
+    same = row == lax.broadcasted_iota(jnp.int32, (samples, samples), 1)
+    echo = lax.dot_general(
+        jnp.where(same, 1.0, 0.0).astype(jnp.bfloat16),
+        echo_ref[...],
+        (((1,), (1,)), ((), ())),
+        preferred_element_type=jnp.float32,
+    )
     blocks = ext // SUB
     for tile in range(lanes // LANES):
         cols = slice(tile * LANES, (tile + 1) * LANES)

time: 25.8 us -> 25.9 us (level)
  no operation moved by 1% of the time
where the time goes in v27:
time: 25.9 us; the launch traced here: 25.7 us
  blocking collectives  20.5 us (79%)
  Pallas kernels  4.58 us (18%)
  between operations  0.64 us (2%)
    all_to_all x1, blocking collectives, shards(): lax.all_to_all(image, ('far', 'near'), 0, 0, axis_index_groups=[listed(fa...  10.3 us
    all_to_all x1, blocking collectives, shards(): lax.all_to_all(share, ('range', 'near'), 0, 0, axis_index_groups=order, t...  10.2 us
    pallas_call x1, Pallas kernels, own_share(): pl.pallas_call(functools.partial(fir_kernel, bands, front, stack), out_sh...  1.96 us
    pallas_call x1, Pallas kernels, image_share(): pl.pallas_call(functools.partial(image_kernel, bands, scaling, near, ping...  1.88 us
    pallas_call x1, Pallas kernels, turned(): pl.pallas_call(functools.partial(turn_kernel, far, stack), out_shape=(out...  0.74 us

profile of v27, /device:TPU:0, one launch (start us, length us, event | category | flops | bytes accessed | tf_op | source)
XLA Modules:
  0.0 25.7 jit_solution(4370315288266126165)
XLA Ops:
  0.6 2.0 %fir.1 = bf16[16,8,640]{2,1,0:T(8,128)(2,1)S(1)} custom-call(s32[8]{0:T(128)} %offset_hbm.1, s32[8]{0:T(128)} %track_hbm.1, bf16[256,128]{1,0:T(8,128)(2,1)} %bitcast.1, f32[8,32]{1,0:T(8,128)} %sway_hbm.1, f32[8,32]{1,0:T(8,128)} %gain_hbm.1), custom_call_target="tpu_custom_call" | custom-call | tf_op jit(solution)/shard_map/fir/pallas_call | solution.py:186
  2.6 10.2 %all_to_all.10.share_ref = bf16[16,8,640]{2,1,0:T(8,128)(2,1)S(1)} all-to-all(bf16[16,8,640]{2,1,0:T(8,128)(2,1)S(1)} %fir.1), channel_id=1, replica_groups={{23,0,1,2,3,4,5,6,7,16,17,18,19,20,21,22},{31,8,9,10,11,12,13,14,15,24,..., dimensions={0} | all-to-all | bytes 327680 | tf_op jit(solution)/shard_map/all_to_all | solution.py:439
  12.8 1.9 %image.1 = bf16[16,8,512]{2,1,0:T(8,128)(2,1)S(1)} custom-call(bf16[16,8,640]{2,1,0:T(8,128)(2,1)S(1)} %all_to_all.10.share_ref), custom_call_target="tpu_custom_call" | custom-call | tf_op jit(solution)/shard_map/image/pallas_call | solution.py:379
  14.6 10.3 %all_to_all.11.in_ref = bf16[16,8,512]{2,1,0:T(8,128)(2,1)S(1)} all-to-all(bf16[16,8,512]{2,1,0:T(8,128)(2,1)S(1)} %image.1), channel_id=1, replica_groups={{15,0,1,2,3,4,5,6,7,8,9,10,11,12,13,14},{31,16,17,18,19,20,21,22,23,24,..., dimensions={0} | all-to-all | bytes 262144 | tf_op jit(solution)/shard_map/all_to_all | solution.py:456
  24.9 0.7 %turn.1 = (f32[128,128]{1,0:T(8,128)}, f32[128,128]{1,0:T(8,128)}) custom-call(bf16[16,8,512]{2,1,0:T(8,128)(2,1)S(1)} %all_to_all.11.in_ref), custom_call_target="tpu_custom_call" | custom-call | tf_op jit(solution)/shard_map/turn/pallas_call | solution.py:421

commit v28 on v22

--- a/solution.py
+++ b/solution.py
@@ -112,7 +112,7 @@
         scaled = jnp.where(whole, signed, amplitude[:, cols] / jnp.where(whole, 1.0, shift))
         tap_ref[:, cols] = scaled * window
 
-    echo = jnp.transpose(echo_ref[...].astype(jnp.float32))
+    echo = jnp.transpose(echo_ref[...]).astype(jnp.float32)
     blocks = ext // SUB
     for tile in range(lanes // LANES):
         cols = slice(tile * LANES, (tile + 1) * LANES)

time: 25.8 us -> 25.9 us (level)
  no operation moved by 1% of the time
where the time goes in v28:
time: 25.9 us; the launch traced here: 25.6 us
  blocking collectives  20.5 us (79%)
  Pallas kernels  4.53 us (17%)
  between operations  0.64 us (2%)
    all_to_all x1, blocking collectives, shards(): lax.all_to_all(image, ('far', 'near'), 0, 0, axis_index_groups=[listed(fa...  10.3 us
    all_to_all x1, blocking collectives, shards(): lax.all_to_all(share, ('range', 'near'), 0, 0, axis_index_groups=order, t...  10.2 us
    pallas_call x1, Pallas kernels, own_share(): pl.pallas_call(functools.partial(fir_kernel, bands, front, stack), out_sh...  1.92 us
    pallas_call x1, Pallas kernels, image_share(): pl.pallas_call(functools.partial(image_kernel, bands, scaling, near, ping...  1.88 us
    pallas_call x1, Pallas kernels, turned(): pl.pallas_call(functools.partial(turn_kernel, far, stack), out_shape=(out...  0.74 us

profile of v28, /device:TPU:0, one launch (start us, length us, event | category | flops | bytes accessed | tf_op | source)
XLA Modules:
  0.0 25.6 jit_solution(1653857143658092194)
XLA Ops:
  0.6 1.9 %fir.1 = bf16[16,8,640]{2,1,0:T(8,128)(2,1)S(1)} custom-call(s32[8]{0:T(128)} %offset_hbm.1, s32[8]{0:T(128)} %track_hbm.1, bf16[256,128]{1,0:T(8,128)(2,1)} %bitcast.1, f32[8,32]{1,0:T(8,128)} %sway_hbm.1, f32[8,32]{1,0:T(8,128)} %gain_hbm.1), custom_call_target="tpu_custom_call" | custom-call | tf_op jit(solution)/shard_map/fir/pallas_call | solution.py:179
  2.6 10.2 %all_to_all.10.share_ref = bf16[16,8,640]{2,1,0:T(8,128)(2,1)S(1)} all-to-all(bf16[16,8,640]{2,1,0:T(8,128)(2,1)S(1)} %fir.1), channel_id=1, replica_groups={{23,0,1,2,3,4,5,6,7,16,17,18,19,20,21,22},{31,8,9,10,11,12,13,14,15,24,..., dimensions={0} | all-to-all | bytes 327680 | tf_op jit(solution)/shard_map/all_to_all | solution.py:432
  12.7 1.9 %image.1 = bf16[16,8,512]{2,1,0:T(8,128)(2,1)S(1)} custom-call(bf16[16,8,640]{2,1,0:T(8,128)(2,1)S(1)} %all_to_all.10.share_ref), custom_call_target="tpu_custom_call" | custom-call | tf_op jit(solution)/shard_map/image/pallas_call | solution.py:372
  14.6 10.3 %all_to_all.11.in_ref = bf16[16,8,512]{2,1,0:T(8,128)(2,1)S(1)} all-to-all(bf16[16,8,512]{2,1,0:T(8,128)(2,1)S(1)} %image.1), channel_id=1, replica_groups={{15,0,1,2,3,4,5,6,7,8,9,10,11,12,13,14},{31,16,17,18,19,20,21,22,23,24,..., dimensions={0} | all-to-all | bytes 262144 | tf_op jit(solution)/shard_map/all_to_all | solution.py:449
  24.9 0.7 %turn.1 = (f32[128,128]{1,0:T(8,128)}, f32[128,128]{1,0:T(8,128)}) custom-call(bf16[16,8,512]{2,1,0:T(8,128)(2,1)S(1)} %all_to_all.11.in_ref), custom_call_target="tpu_custom_call" | custom-call | tf_op jit(solution)/shard_map/turn/pallas_call | solution.py:414

commit v29 on v22

--- a/solution.py
+++ b/solution.py
@@ -65,8 +65,8 @@
     sway_ref,
     gain_ref,
     tap_ref,
-    placed_ref,
     sems,
+    *placed_refs,
 ):
     pairs = (
         (echo_hbm, echo_ref),
@@ -90,10 +90,10 @@
         base = -samples
 
     ext = round_up(samples + BAND - 1, SUB)
-    tail = placed_ref.shape[1] - front - ext
-    for tile in range(lanes // LANES):
-        placed_ref[tile, :front, :] = jnp.zeros((front, LANES), jnp.float32)
-        placed_ref[tile, front + ext :, :] = jnp.zeros((tail, LANES), jnp.float32)
+    tail = placed_refs[0].shape[0] - front - ext
+    for placed_ref in placed_refs:
+        placed_ref[:front, :] = jnp.zeros((front, LANES), jnp.float32)
+        placed_ref[front + ext :, :] = jnp.zeros((tail, LANES), jnp.float32)
     tap_index = lax.broadcasted_iota(jnp.int32, (BAND, LANES), 0)
     window = 0.5 - 0.5 * jnp.cos(2.0 * math.pi * (tap_index.astype(jnp.float32) + 0.5) / BAND)
     window = jnp.where(tap_index % 2 == 0, window, -window)
@@ -138,7 +138,7 @@
                     total[j] = term if total[j] is None else total[j] + term
         for j in range(blocks):
             value = jnp.zeros((SUB, LANES), jnp.float32) if total[j] is None else total[j]
-            placed_ref[tile, front + j * SUB : front + (j + 1) * SUB, :] = value
+            placed_refs[tile][front + j * SUB : front + (j + 1) * SUB, :] = value
 
     lane = lax.broadcasted_iota(jnp.int32, (rows, LANES), 1)
     for tile in range(lanes // LANES):
@@ -148,7 +148,7 @@
             if high <= 0 or low >= LANES:
                 continue
             start = base + offset_ref[ping] + (front + BAND - 1)
-            moved = placed_ref[tile, pl.ds(start, rows), :]
+            moved = placed_refs[tile][pl.ds(start, rows), :]
             value = moved if value is None else jnp.where(lane >= low, moved, value)
         value = value.astype(jnp.bfloat16).reshape(chunks, stack, SUB, LANES)
         for chunk, slot in enumerate(share_slots(bands, chunks // min(bands, 3))):
@@ -188,9 +188,9 @@
             pltpu.VMEM((pings, channels), jnp.float32),
             pltpu.VMEM((pings, channels), jnp.float32),
             pltpu.VMEM((BAND, lanes), jnp.float32),
-            pltpu.VMEM((lanes // LANES, height, LANES), jnp.float32),
             pltpu.SemaphoreType.DMA((5,)),
-        ],
+        ]
+        + [pltpu.VMEM((height, LANES), jnp.float32)] * (lanes // LANES),
         compiler_params=pltpu.CompilerParams(vmem_limit_bytes=8 * MIB),
         name="fir",
     )(

time: 25.8 us -> 25.8 us (level)
  no operation moved by 1% of the time
where the time goes in v29:
time: 25.8 us; the launch traced here: 25.6 us
  blocking collectives  20.5 us (79%)
  Pallas kernels  4.51 us (17%)
  between operations  0.64 us (2%)
    all_to_all x1, blocking collectives, shards(): lax.all_to_all(image, ('far', 'near'), 0, 0, axis_index_groups=[listed(fa...  10.3 us
    all_to_all x1, blocking collectives, shards(): lax.all_to_all(share, ('range', 'near'), 0, 0, axis_index_groups=order, t...  10.2 us
    pallas_call x1, Pallas kernels, own_share(): pl.pallas_call(functools.partial(fir_kernel, bands, front, stack), out_sh...  1.89 us
    pallas_call x1, Pallas kernels, image_share(): pl.pallas_call(functools.partial(image_kernel, bands, scaling, near, ping...  1.88 us
    pallas_call x1, Pallas kernels, turned(): pl.pallas_call(functools.partial(turn_kernel, far, stack), out_shape=(out...  0.74 us

profile of v29, /device:TPU:0, one launch (start us, length us, event | category | flops | bytes accessed | tf_op | source)
XLA Modules:
  0.0 25.6 jit_solution(13899961014308807505)
XLA Ops:
  0.6 1.9 %fir.1 = bf16[16,8,640]{2,1,0:T(8,128)(2,1)S(1)} custom-call(s32[8]{0:T(128)} %offset_hbm.1, s32[8]{0:T(128)} %track_hbm.1, bf16[256,128]{1,0:T(8,128)(2,1)} %bitcast.1, f32[8,32]{1,0:T(8,128)} %sway_hbm.1, f32[8,32]{1,0:T(8,128)} %gain_hbm.1), custom_call_target="tpu_custom_call" | custom-call | tf_op jit(solution)/shard_map/fir/pallas_call | solution.py:179
  2.5 10.2 %all_to_all.10.share_ref = bf16[16,8,640]{2,1,0:T(8,128)(2,1)S(1)} all-to-all(bf16[16,8,640]{2,1,0:T(8,128)(2,1)S(1)} %fir.1), channel_id=1, replica_groups={{23,0,1,2,3,4,5,6,7,16,17,18,19,20,21,22},{31,8,9,10,11,12,13,14,15,24,..., dimensions={0} | all-to-all | bytes 327680 | tf_op jit(solution)/shard_map/all_to_all | solution.py:432
  12.7 1.9 %image.1 = bf16[16,8,512]{2,1,0:T(8,128)(2,1)S(1)} custom-call(bf16[16,8,640]{2,1,0:T(8,128)(2,1)S(1)} %all_to_all.10.share_ref), custom_call_target="tpu_custom_call" | custom-call | tf_op jit(solution)/shard_map/image/pallas_call | solution.py:372
  14.6 10.3 %all_to_all.11.in_ref = bf16[16,8,512]{2,1,0:T(8,128)(2,1)S(1)} all-to-all(bf16[16,8,512]{2,1,0:T(8,128)(2,1)S(1)} %image.1), channel_id=1, replica_groups={{15,0,1,2,3,4,5,6,7,8,9,10,11,12,13,14},{31,16,17,18,19,20,21,22,23,24,..., dimensions={0} | all-to-all | bytes 262144 | tf_op jit(solution)/shard_map/all_to_all | solution.py:449
  24.9 0.7 %turn.1 = (f32[128,128]{1,0:T(8,128)}, f32[128,128]{1,0:T(8,128)}) custom-call(bf16[16,8,512]{2,1,0:T(8,128)(2,1)S(1)} %all_to_all.11.in_ref), custom_call_target="tpu_custom_call" | custom-call | tf_op jit(solution)/shard_map/turn/pallas_call | solution.py:414

commit v30 on v22

--- a/solution.py
+++ b/solution.py
@@ -276,10 +276,9 @@
     half = window_ref.shape[0] // rows // 2
     fill_table(bands, scaling, line_ref, table_ref)
 
-    one, none = jnp.ones((), jnp.bfloat16), jnp.zeros((), jnp.bfloat16)
     column = place_order(lax.broadcasted_iota(jnp.int32, (channels, depth), 1))
     column = (column - lax.broadcasted_iota(jnp.int32, (channels, depth), 0)) & (depth - 1)
-    column = column.astype(jnp.float32).astype(jnp.bfloat16)
+    column = column.astype(jnp.float32)
     lane = lax.broadcasted_iota(jnp.int32, (SUB, LANES), 1)
     channel = (lane % channels).astype(jnp.float32)
     held, come = None, share_slots(bands, near)
@@ -290,7 +289,7 @@
             share = share + more.astype(jnp.float32)
         share = jnp.concatenate(
             [share[:, i * lanes : (i + 1) * lanes] for i in range(stack)], axis=0
-        ).astype(jnp.bfloat16)
+        )
         hot, block = [], [None] * (lanes // LANES)
         for first in range(0, pings, SUB):
             at = stack * lanes + first // SUB * LANES
@@ -305,15 +304,14 @@
             for ping in range(first, min(first + SUB, pings)):
                 own = ping - first
                 meets = jnp.broadcast_to(inside[own : own + 1], (channels, LANES))
-                meets = meets.astype(jnp.bfloat16)
                 hot.append(
                     jnp.concatenate(
                         [
-                            jnp.where(column[:, i : i + LANES] == meets, one, none)
+                            jnp.where(column[:, i : i + LANES] == meets, 1.0, 0.0)
                             for i in range(0, depth, LANES)
                         ],
                         axis=1,
-                    )
+                    ).astype(jnp.bfloat16)
                 )
                 tile, low = ping * channels // LANES, ping * channels % LANES
                 one_block = jnp.broadcast_to(whole[own : own + 1], (rows, LANES))
@@ -322,9 +320,13 @@
                 else:
                     at_lane = lax.broadcasted_iota(jnp.int32, (rows, LANES), 1)
                     block[tile] = jnp.where(at_lane >= low, one_block, block[tile])
-        block = jnp.concatenate(block, axis=1).astype(jnp.bfloat16)
+        block = jnp.concatenate(block, axis=1)
         spread = jnp.concatenate(
-            [jnp.where(block == float(k), share, none) for k in range(half)], axis=0
+            [
+                jnp.where(block == float(k), share, 0.0).astype(jnp.bfloat16)
+                for k in range(half)
+            ],
+            axis=0,
         )
         part = jnp.dot(
             spread, jnp.concatenate(hot, axis=0), preferred_element_type=jnp.float32

time: 25.8 us -> 25.8 us (level)
  no operation moved by 1% of the time
where the time goes in v30:
time: 25.8 us; the launch traced here: 25.6 us
  blocking collectives  20.5 us (79%)
  Pallas kernels  4.5 us (17%)
  between operations  0.64 us (2%)
    all_to_all x1, blocking collectives, shards(): lax.all_to_all(image, ('far', 'near'), 0, 0, axis_index_groups=[listed(fa...  10.3 us
    all_to_all x1, blocking collectives, shards(): lax.all_to_all(share, ('range', 'near'), 0, 0, axis_index_groups=order, t...  10.1 us
    pallas_call x1, Pallas kernels, own_share(): pl.pallas_call(functools.partial(fir_kernel, bands, front, stack), out_sh...  1.89 us
    pallas_call x1, Pallas kernels, image_share(): pl.pallas_call(functools.partial(image_kernel, bands, scaling, near, ping...  1.87 us
    pallas_call x1, Pallas kernels, turned(): pl.pallas_call(functools.partial(turn_kernel, far, stack), out_shape=(out...  0.74 us

profile of v30, /device:TPU:0, one launch (start us, length us, event | category | flops | bytes accessed | tf_op | source)
XLA Modules:
  0.0 25.6 jit_solution(8649635522565064600)
XLA Ops:
  0.6 1.9 %fir.1 = bf16[16,8,640]{2,1,0:T(8,128)(2,1)S(1)} custom-call(s32[8]{0:T(128)} %offset_hbm.1, s32[8]{0:T(128)} %track_hbm.1, bf16[256,128]{1,0:T(8,128)(2,1)} %bitcast.1, f32[8,32]{1,0:T(8,128)} %sway_hbm.1, f32[8,32]{1,0:T(8,128)} %gain_hbm.1), custom_call_target="tpu_custom_call" | custom-call | tf_op jit(solution)/shard_map/fir/pallas_call | solution.py:179
  2.5 10.1 %all_to_all.10.share_ref = bf16[16,8,640]{2,1,0:T(8,128)(2,1)S(1)} all-to-all(bf16[16,8,640]{2,1,0:T(8,128)(2,1)S(1)} %fir.1), channel_id=1, replica_groups={{23,0,1,2,3,4,5,6,7,16,17,18,19,20,21,22},{31,8,9,10,11,12,13,14,15,24,..., dimensions={0} | all-to-all | bytes 327680 | tf_op jit(solution)/shard_map/all_to_all | solution.py:434
  12.7 1.9 %image.1 = bf16[16,8,512]{2,1,0:T(8,128)(2,1)S(1)} custom-call(bf16[16,8,640]{2,1,0:T(8,128)(2,1)S(1)} %all_to_all.10.share_ref), custom_call_target="tpu_custom_call" | custom-call | tf_op jit(solution)/shard_map/image/pallas_call | solution.py:374
  14.6 10.3 %all_to_all.11.in_ref = bf16[16,8,512]{2,1,0:T(8,128)(2,1)S(1)} all-to-all(bf16[16,8,512]{2,1,0:T(8,128)(2,1)S(1)} %image.1), channel_id=1, replica_groups={{15,0,1,2,3,4,5,6,7,8,9,10,11,12,13,14},{31,16,17,18,19,20,21,22,23,24,..., dimensions={0} | all-to-all | bytes 262144 | tf_op jit(solution)/shard_map/all_to_all | solution.py:451
  24.9 0.7 %turn.1 = (f32[128,128]{1,0:T(8,128)}, f32[128,128]{1,0:T(8,128)}) custom-call(bf16[16,8,512]{2,1,0:T(8,128)(2,1)S(1)} %all_to_all.11.in_ref), custom_call_target="tpu_custom_call" | custom-call | tf_op jit(solution)/shard_map/turn/pallas_call | solution.py:416

commit v31 on v22

--- a/solution.py
+++ b/solution.py
@@ -23,7 +23,8 @@
 
 
 def listed(size):
-    return [size - 1, *range(size - 1)]
+    last = range(max(size - 2, 0), size)
+    return [*last, *range(size - len(last))]
 
 
 def slots(size):

time: 25.8 us -> 26.5 us (1.027)
  blocking collectives: 20.4 us -> 21.2 us
    all_to_all x1, blocking collectives: 10.2 us -> 10.7 us  [shards(): lax.all_to_all(share, ('range', 'near'), 0, 0, axis_index_groups=order, t...]
where the time goes in v31:
time: 26.5 us; the launch traced here: 26.3 us
  blocking collectives  21.2 us (80%)
  Pallas kernels  4.51 us (17%)
  between operations  0.64 us (2%)
    all_to_all x1, blocking collectives, shards(): lax.all_to_all(share, ('range', 'near'), 0, 0, axis_index_groups=order, t...  10.7 us
    all_to_all x1, blocking collectives, shards(): lax.all_to_all(image, ('far', 'near'), 0, 0, axis_index_groups=[listed(fa...  10.4 us
    pallas_call x1, Pallas kernels, own_share(): pl.pallas_call(functools.partial(fir_kernel, bands, front, stack), out_sh...  1.89 us
    pallas_call x1, Pallas kernels, image_share(): pl.pallas_call(functools.partial(image_kernel, bands, scaling, near, ping...  1.88 us
    pallas_call x1, Pallas kernels, turned(): pl.pallas_call(functools.partial(turn_kernel, far, stack), out_shape=(out...  0.74 us

profile of v31, /device:TPU:0, one launch (start us, length us, event | category | flops | bytes accessed | tf_op | source)
XLA Modules:
  0.0 26.3 jit_solution(11281177545192055799)
XLA Ops:
  0.6 1.9 %fir.1 = bf16[16,8,640]{2,1,0:T(8,128)(2,1)S(1)} custom-call(s32[8]{0:T(128)} %offset_hbm.1, s32[8]{0:T(128)} %track_hbm.1, bf16[256,128]{1,0:T(8,128)(2,1)} %bitcast.1, f32[8,32]{1,0:T(8,128)} %sway_hbm.1, f32[8,32]{1,0:T(8,128)} %gain_hbm.1), custom_call_target="tpu_custom_call" | custom-call | tf_op jit(solution)/shard_map/fir/pallas_call | solution.py:180
  2.5 10.7 %all_to_all.10.share_ref = bf16[16,8,640]{2,1,0:T(8,128)(2,1)S(1)} all-to-all(bf16[16,8,640]{2,1,0:T(8,128)(2,1)S(1)} %fir.1), channel_id=1, replica_groups={{22,23,0,1,2,3,4,5,6,7,16,17,18,19,20,21},{30,31,8,9,10,11,12,13,14,15,..., dimensions={0} | all-to-all | bytes 327680 | tf_op jit(solution)/shard_map/all_to_all | solution.py:433
  13.2 1.9 %image.1 = bf16[16,8,512]{2,1,0:T(8,128)(2,1)S(1)} custom-call(bf16[16,8,640]{2,1,0:T(8,128)(2,1)S(1)} %all_to_all.10.share_ref), custom_call_target="tpu_custom_call" | custom-call | tf_op jit(solution)/shard_map/image/pallas_call | solution.py:373
  15.1 10.4 %all_to_all.11.in_ref = bf16[16,8,512]{2,1,0:T(8,128)(2,1)S(1)} all-to-all(bf16[16,8,512]{2,1,0:T(8,128)(2,1)S(1)} %image.1), channel_id=1, replica_groups={{14,15,0,1,2,3,4,5,6,7,8,9,10,11,12,13},{30,31,16,17,18,19,20,21,22,23,..., dimensions={0} | all-to-all | bytes 262144 | tf_op jit(solution)/shard_map/all_to_all | solution.py:450
  25.6 0.7 %turn.1 = (f32[128,128]{1,0:T(8,128)}, f32[128,128]{1,0:T(8,128)}) custom-call(bf16[16,8,512]{2,1,0:T(8,128)(2,1)S(1)} %all_to_all.11.in_ref), custom_call_target="tpu_custom_call" | custom-call | tf_op jit(solution)/shard_map/turn/pallas_call | solution.py:415

commit v32 on v29

--- a/solution.py
+++ b/solution.py
@@ -282,7 +282,7 @@
     column = column.astype(jnp.float32).astype(jnp.bfloat16)
     lane = lax.broadcasted_iota(jnp.int32, (SUB, LANES), 1)
     channel = (lane % channels).astype(jnp.float32)
-    held, come = None, share_slots(bands, near)
+    held, come, waiting = None, share_slots(bands, near), []
     for group in range(near):
         share = share_ref[come[group], :, : stack * lanes].astype(jnp.float32)
         for copy in range(1, copies):
@@ -326,10 +326,15 @@
         spread = jnp.concatenate(
             [jnp.where(block == float(k), share, none) for k in range(half)], axis=0
         )
+        waiting.append((spread, jnp.concatenate(hot, axis=0)))
+        if len(waiting) < 2 and group < near - 1:
+            continue
         part = jnp.dot(
-            spread, jnp.concatenate(hot, axis=0), preferred_element_type=jnp.float32
+            jnp.concatenate([left for left, _ in waiting], axis=1),
+            jnp.concatenate([right for _, right in waiting], axis=0),
+            preferred_element_type=jnp.float32,
         )
-        held = part if held is None else held + part
+        held, waiting = part if held is None else held + part, []
     held = held.astype(jnp.bfloat16)
     for k in range(half):
         block = held[k * rows : (k + 1) * rows]

time: 25.8 us -> 25.8 us (level)
  no operation moved by 1% of the time
where the time goes in v32:
time: 25.8 us; the launch traced here: 25.6 us
  blocking collectives  20.5 us (79%)
  Pallas kernels  4.51 us (17%)
  between operations  0.64 us (2%)
    all_to_all x1, blocking collectives, shards(): lax.all_to_all(image, ('far', 'near'), 0, 0, axis_index_groups=[listed(fa...  10.3 us
    all_to_all x1, blocking collectives, shards(): lax.all_to_all(share, ('range', 'near'), 0, 0, axis_index_groups=order, t...  10.2 us
    pallas_call x1, Pallas kernels, own_share(): pl.pallas_call(functools.partial(fir_kernel, bands, front, stack), out_sh...  1.89 us
    pallas_call x1, Pallas kernels, image_share(): pl.pallas_call(functools.partial(image_kernel, bands, scaling, near, ping...  1.88 us
    pallas_call x1, Pallas kernels, turned(): pl.pallas_call(functools.partial(turn_kernel, far, stack), out_shape=(out...  0.74 us

profile of v32, /device:TPU:0, one launch (start us, length us, event | category | flops | bytes accessed | tf_op | source)
XLA Modules:
  0.0 25.6 jit_solution(7617136328621346331)
XLA Ops:
  0.6 1.9 %fir.1 = bf16[16,8,640]{2,1,0:T(8,128)(2,1)S(1)} custom-call(s32[8]{0:T(128)} %offset_hbm.1, s32[8]{0:T(128)} %track_hbm.1, bf16[256,128]{1,0:T(8,128)(2,1)} %bitcast.1, f32[8,32]{1,0:T(8,128)} %sway_hbm.1, f32[8,32]{1,0:T(8,128)} %gain_hbm.1), custom_call_target="tpu_custom_call" | custom-call | tf_op jit(solution)/shard_map/fir/pallas_call | solution.py:179
  2.5 10.2 %all_to_all.10.share_ref = bf16[16,8,640]{2,1,0:T(8,128)(2,1)S(1)} all-to-all(bf16[16,8,640]{2,1,0:T(8,128)(2,1)S(1)} %fir.1), channel_id=1, replica_groups={{23,0,1,2,3,4,5,6,7,16,17,18,19,20,21,22},{31,8,9,10,11,12,13,14,15,24,..., dimensions={0} | all-to-all | bytes 327680 | tf_op jit(solution)/shard_map/all_to_all | solution.py:437
  12.7 1.9 %image.1 = bf16[16,8,512]{2,1,0:T(8,128)(2,1)S(1)} custom-call(bf16[16,8,640]{2,1,0:T(8,128)(2,1)S(1)} %all_to_all.10.share_ref), custom_call_target="tpu_custom_call" | custom-call | tf_op jit(solution)/shard_map/image/pallas_call | solution.py:377
  14.6 10.3 %all_to_all.11.in_ref = bf16[16,8,512]{2,1,0:T(8,128)(2,1)S(1)} all-to-all(bf16[16,8,512]{2,1,0:T(8,128)(2,1)S(1)} %image.1), channel_id=1, replica_groups={{15,0,1,2,3,4,5,6,7,8,9,10,11,12,13,14},{31,16,17,18,19,20,21,22,23,24,..., dimensions={0} | all-to-all | bytes 262144 | tf_op jit(solution)/shard_map/all_to_all | solution.py:454
  24.9 0.7 %turn.1 = (f32[128,128]{1,0:T(8,128)}, f32[128,128]{1,0:T(8,128)}) custom-call(bf16[16,8,512]{2,1,0:T(8,128)(2,1)S(1)} %all_to_all.11.in_ref), custom_call_target="tpu_custom_call" | custom-call | tf_op jit(solution)/shard_map/turn/pallas_call | solution.py:419
